TPU v7x, 32 devices: a whole 2x2x4 slice. The times are simulated.
32 devices in a mesh: batch: 16 (over z, x, core), src: 2 (over y).
Axes of the slice: x: 2, y: 2, z: 4, core: 2. Of those that a mesh axis runs over, the one named last changes fastest.
Arguments:
- dec_input: bfloat16 [16384, 512], P(('batch', 'src')), may hold values from -6 to 6
- enc_output: bfloat16 [65536, 512], P(('batch', 'src')), may hold values from -6 to 6
- segment_ids: int32 [32, 512], P(('batch', 'src')), may hold values from 0 to 7, never falling along the last dimension, each value on 1 to 128 neighbouring positions
- padding: int32 [32, 512], P(('batch', 'src')), may hold values 0 or 1
- pair_ids: int32 [32, 8], P(('batch', 'src')), may hold values from 0 to 7
- src_lengths: int32 [16, 16], P('batch'), may hold values from 1 to 2304, 4096 in all within a row
- delete_labels: int32 [32, 512], P(('batch', 'src')), may hold values 0 or 1
- insert_counts: int32 [32, 512], P(('batch', 'src')), may hold values from 0 to 255
- masked_positions: int32 [32, 16], P(('batch', 'src')), may hold values from 0 to 511, as said below
- masked_targets: int32 [32, 16], P(('batch', 'src')), may hold values from 0 to 32767
- norm_gain: bfloat16 [4, 512], P(None, ('batch', 'src')), may hold values from 0.5 to 1.5
- norm_bias: bfloat16 [4, 512], P(None, ('batch', 'src')), may hold values from -1 to 1
- pair_table: bfloat16 [8, 512], P(None, ('batch', 'src')), may hold values from -3 to 3
- self_qkv: bfloat16 [512, 1536], P(('batch', 'src')), may hold values from -0.25 to 0.25
- self_out: bfloat16 [512, 512], P(('batch', 'src')), may hold values from -1 to 1
- cross_q: bfloat16 [512, 512], P(('batch', 'src')), may hold values from -0.25 to 0.25
- cross_kv: bfloat16 [512, 1024], P(('batch', 'src')), may hold values from -0.25 to 0.25
- cross_out: bfloat16 [512, 512], P(('batch', 'src')), may hold values from -1 to 1
- ffn_in: bfloat16 [512, 2048], P(('batch', 'src')), may hold values from -0.25 to 0.25
- ffn_out: bfloat16 [2048, 512], P(('batch', 'src')), may hold values from -0.125 to 0.125
- w_delete: bfloat16 [512, 2], P(('batch', 'src')), may hold values from -0.75 to 0.75
- w_insert: bfloat16 [1024, 256], P(('batch', 'src')), may hold values from -0.375 to 0.375
- w_vocab: bfloat16 [32768, 512], P(('batch', 'src')), may hold values from -0.5 to 0.5
Outputs:
- block_out: bfloat16 [16384, 512], P(('batch', 'src'))
- grad_input: bfloat16 [16384, 512], P(('batch', 'src'))
- grad_enc: bfloat16 [65536, 512], P(('batch', 'src'))
- grad_norm_gain: float32 [4, 512], P(None, ('batch', 'src'))
- grad_norm_bias: float32 [4, 512], P(None, ('batch', 'src'))
- grad_pair_table: float32 [8, 512], P(None, ('batch', 'src'))
- grad_self_qkv: float32 [512, 1536], P(('batch', 'src'))
- grad_self_out: float32 [512, 512], P(('batch', 'src'))
- grad_cross_q: float32 [512, 512], P(('batch', 'src'))
- grad_cross_kv: float32 [512, 1024], P(('batch', 'src'))
- grad_cross_out: float32 [512, 512], P(('batch', 'src'))
- grad_ffn_in: float32 [512, 2048], P(('batch', 'src'))
- grad_ffn_out: float32 [2048, 512], P(('batch', 'src'))
- grad_delete: float32 [512, 2], P(('batch', 'src'))
- grad_insert: float32 [1024, 256], P(('batch', 'src'))
- grad_vocab: float32 [32768, 512], P(('batch', 'src'))
- mean_loss: float32 [], replicated
- token_losses: float32 [32, 16], P(('batch', 'src'))
Inputs may be any that keep to these rules, and one draw needn't show every extreme that they name: `masked_positions`: within each row the 16 positions are distinct. `src_lengths`: each row sums to 4096. `segment_ids`: never falling along a row; every number is used in every row.
All inputs are finite; a program needn't handle non-finite values. No bound on the sum of `padding` or of `delete_labels` on one device may be relied on, other than what follows from the above.
Results may differ from a plain program's by a relative error of at most 0.02.
Values may be sent and summed in bfloat16 or wider, within the bound.
A program may use at most 320 MiB of HBM per device.

v0:
```python
from functools import partial

import jax
import jax.numpy as jnp
from jax import lax
from jax.sharding import PartitionSpec as P

HD = 64
PAIRS = 8
SEGS = 8


epsilon = 1e-05
score_scale = 0.125
masked_fill = -1e30


def joined(x, axis, combine):
    everything = jax.tree.map(
        lambda part, kind: lax.all_gather(part.astype(kind), axis), x, (jnp.bfloat16, jnp.bfloat16)
    )

    def take(k):
        return jax.tree.map(lambda part, own: part[k].astype(own.dtype), everything, x)

    return lax.fori_loop(
        1, lax.axis_size(axis), lambda k, so_far: combine(so_far, take(k)), take(0)
    )


def joined_2(x, axis, combine):
    everything = jax.tree.map(
        lambda part, kind: lax.all_gather(part.astype(kind), axis),
        x,
        (jnp.bfloat16, jnp.bfloat16, jnp.bfloat16),
    )

    def take(k):
        return jax.tree.map(lambda part, own: part[k].astype(own.dtype), everything, x)

    return lax.fori_loop(
        1, lax.axis_size(axis), lambda k, so_far: combine(so_far, take(k)), take(0)
    )


def layer_norm(activation, scale_row, shift_row):
    centred = activation - jnp.mean(activation, axis=-1, keepdims=True)
    spread = jnp.mean(centred * centred, axis=-1, keepdims=True)
    return centred * lax.rsqrt(spread + epsilon) * scale_row + shift_row


def norm_backward(activation, scale_row, shift_row, upstream):
    pull_norm = jax.vjp(layer_norm, activation, scale_row, shift_row)[1]
    return pull_norm(upstream)


def matmul(left, right):
    return jnp.dot(left, right, preferred_element_type=jnp.float32)


def matmul_tn(left, right):
    return lax.dot_general(
        left, right, (((0,), (0,)), ((), ())), preferred_element_type=jnp.float32
    )


def matmul_nt(left, right):
    return lax.dot_general(
        left, right, (((1,), (1,)), ((), ())), preferred_element_type=jnp.float32
    )


def entropy_rows(logits, labels):
    row_top = jnp.max(logits, axis=1, keepdims=True)
    log_total = row_top[:, 0] + jnp.log(jnp.sum(jnp.exp(logits - row_top), axis=1))
    hits = labels[:, None] == lax.broadcasted_iota(jnp.int32, logits.shape, 1)
    return log_total - jnp.sum(jnp.where(hits, logits, 0.0), axis=1)


def entropy_grad(logits, labels, weight_rows):
    row_top = jnp.max(logits, axis=1, keepdims=True)
    exps_row = jnp.exp(logits - row_top)
    probabilities = exps_row / jnp.sum(exps_row, axis=1, keepdims=True)
    hits = (labels[:, None] == lax.broadcasted_iota(jnp.int32, logits.shape, 1)).astype(jnp.float32)
    return (weight_rows[:, None] * (probabilities - hits)).astype(jnp.bfloat16)


def head_columns(head_pos):
    return slice(head_pos * HD, (head_pos + 1) * HD)


def masked_scores(queries, key_rows, allowed):
    scores = matmul_nt(queries, key_rows) * score_scale
    return jnp.where(allowed, scores, masked_fill)


def attention_probs(queries, key_rows, allowed, row_top, row_total):
    scores = masked_scores(queries, key_rows, allowed)
    return jnp.where(allowed, jnp.exp(scores - row_top), 0.0) / row_total


def attention_stats(queries, key_rows, allowed):
    maxima, totals = ([], [])
    block_max = []
    block_total = []
    for head_pos in range(queries.shape[1] // HD):
        columns = head_columns(head_pos)
        scores = masked_scores(queries[:, columns], key_rows[:, columns], allowed)
        row_top = jnp.max(scores, axis=1, keepdims=True)
        block_max.append(row_top)
        block_total.append(
            jnp.sum(jnp.where(allowed, jnp.exp(scores - row_top), 0.0), axis=1, keepdims=True)
        )
    maxima.append(jnp.concatenate(block_max, 1))
    totals.append(jnp.concatenate(block_total, 1))
    return (maxima[0], totals[0])


def attention_output(queries, key_rows, values, allowed, row_top, row_total):
    pieces = []
    for head_pos in range(queries.shape[1] // HD):
        columns = head_columns(head_pos)
        probabilities = attention_probs(
            queries[:, columns],
            key_rows[:, columns],
            allowed,
            row_top[:, head_pos : head_pos + 1],
            row_total[:, head_pos : head_pos + 1],
        )
        pieces.append(matmul(probabilities.astype(jnp.bfloat16), values[:, columns]))
    return jnp.concatenate(pieces, 1)


def attention_delta(queries, key_rows, values, allowed, row_top, row_total, grad_rows, block):
    head_parts = []
    for head_pos in range(queries.shape[1] // HD):
        columns = head_columns(head_pos)
        probs_full = attention_probs(
            queries[0:block, columns],
            key_rows[:, columns],
            allowed,
            row_top[0:block, head_pos : head_pos + 1],
            row_total[0:block, head_pos : head_pos + 1],
        )
        grad_prob = matmul_nt(grad_rows[0:block, columns], values[:, columns])
        head_parts.append(jnp.sum(probs_full * grad_prob, axis=1, keepdims=True))
    parts = [jnp.concatenate(head_parts, 1)]
    return jnp.concatenate(parts, 0)


def attention_backward(
    queries, key_rows, values, allowed, row_top, row_total, delta, grad_rows, block
):
    heads_count = queries.shape[1] // HD
    grad_k = [jnp.zeros((key_rows.shape[0], HD), jnp.float32) for head_pos in range(heads_count)]
    grad_v = [jnp.zeros((key_rows.shape[0], HD), jnp.float32) for head_pos in range(heads_count)]
    rows_grad = grad_rows[0:block]
    q_pieces = []
    for head_pos in range(heads_count):
        columns = head_columns(head_pos)
        probs_full = attention_probs(
            queries[:, columns],
            key_rows[:, columns],
            allowed,
            row_top[0:block, head_pos : head_pos + 1],
            row_total[0:block, head_pos : head_pos + 1],
        )
        grad_prob = matmul_nt(rows_grad[:, columns], values[:, columns])
        grad_score = (probs_full * (grad_prob - delta[0:block, head_pos : head_pos + 1])).astype(
            jnp.bfloat16
        )
        q_pieces.append(matmul(grad_score, key_rows[:, columns]) * score_scale)
        grad_k[head_pos] = (
            grad_k[head_pos] + matmul_tn(grad_score, queries[:, columns]) * score_scale
        )
        grad_v[head_pos] = grad_v[head_pos] + matmul_tn(
            probs_full.astype(jnp.bfloat16), rows_grad[:, columns]
        )
    query_blocks = [jnp.concatenate(q_pieces, 1)]
    return (
        jnp.concatenate(query_blocks, 0),
        jnp.concatenate(grad_k, 1),
        jnp.concatenate(grad_v, 1),
    )


def merge_stats(first_part, second_part):
    top_both = jnp.maximum(first_part[0], second_part[0])
    return (
        top_both,
        first_part[1] * jnp.exp(first_part[0] - top_both)
        + second_part[1] * jnp.exp(second_part[0] - top_both),
    )


def merge_vocab(first_part, second_part):
    top_both = jnp.maximum(first_part[0], second_part[0])
    return (
        top_both,
        first_part[1] * jnp.exp(first_part[0] - top_both)
        + second_part[1] * jnp.exp(second_part[0] - top_both),
        first_part[2] + second_part[2],
    )


def body(
    dec_input,
    enc_output,
    segment_ids,
    padding,
    pair_ids,
    src_lengths,
    delete_labels,
    insert_counts,
    masked_positions,
    masked_targets,
    norm_gain,
    norm_bias,
    pair_table,
    self_qkv,
    self_out,
    cross_q,
    cross_kv,
    cross_out,
    ffn_in,
    ffn_out,
    w_delete,
    w_insert,
    w_vocab,
):
    tok_count = dec_input.shape[0]
    model_width = dec_input.shape[1]
    src_count = enc_output.shape[0]
    masked_count = masked_positions.shape[1]
    src_pos = lax.axis_index("src")
    device_pos = lax.axis_index(("batch", "src"))
    everyone = lax.axis_size(("batch", "src"))
    grad_scale = (tok_count * everyone) ** (-0.5)
    segment = segment_ids[0]
    not_padding = 1 - padding[0]
    keep_float = not_padding.astype(jnp.float32)
    positions = masked_positions[0]
    (
        full_gain,
        full_bias,
        full_table,
        full_qkv,
        full_self_out,
        full_cross_q,
        full_cross_kv,
        full_cross_out,
        full_ffn_in,
        full_ffn_out,
        full_delete,
        full_insert,
    ) = (
        lax.all_gather(norm_gain, ("batch", "src"), axis=1, tiled=True),
        lax.all_gather(norm_bias, ("batch", "src"), axis=1, tiled=True),
        lax.all_gather(pair_table, ("batch", "src"), axis=1, tiled=True),
        lax.all_gather(self_qkv, ("batch", "src"), axis=0, tiled=True),
        lax.all_gather(self_out, ("batch", "src"), axis=0, tiled=True),
        lax.all_gather(cross_q, ("batch", "src"), axis=0, tiled=True),
        lax.all_gather(cross_kv, ("batch", "src"), axis=0, tiled=True),
        lax.all_gather(cross_out, ("batch", "src"), axis=0, tiled=True),
        lax.all_gather(ffn_in, ("batch", "src"), axis=0, tiled=True),
        lax.all_gather(ffn_out, ("batch", "src"), axis=0, tiled=True),
        lax.all_gather(w_delete, ("batch", "src"), axis=0, tiled=True),
        lax.all_gather(w_insert, ("batch", "src"), axis=0, tiled=True),
    )
    gains_float = full_gain.astype(jnp.float32)
    biases_float = full_bias.astype(jnp.float32)
    seg_onehot = segment[:, None] == lax.broadcasted_iota(jnp.int32, (tok_count, SEGS), 1)
    token_pair = jnp.sum(jnp.where(seg_onehot, pair_ids[0][None, :], 0), axis=1)
    pair_onehot = (
        token_pair[:, None] == lax.broadcasted_iota(jnp.int32, (tok_count, PAIRS), 1)
    ).astype(jnp.bfloat16)
    start_state = dec_input.astype(jnp.float32) + matmul(pair_onehot, full_table)
    normed_one = layer_norm(start_state, gains_float[0], biases_float[0]).astype(jnp.bfloat16)
    qkv_proj = matmul(normed_one, full_qkv).astype(jnp.bfloat16)
    self_query = qkv_proj[:, :model_width]
    self_keys = qkv_proj[:, model_width : 2 * model_width]
    self_values = qkv_proj[:, 2 * model_width :]
    row_iota = lax.broadcasted_iota(jnp.int32, (tok_count, tok_count), 0)
    col_iota = lax.broadcasted_iota(jnp.int32, (tok_count, tok_count), 1)
    self_allowed = (segment[:, None] == segment[None, :]) & (
        (not_padding[None, :] == 1) | (row_iota == col_iota)
    )
    self_top, self_total = attention_stats(self_query, self_keys, self_allowed)
    self_low = attention_output(
        self_query, self_keys, self_values, self_allowed, self_top, self_total
    ).astype(jnp.bfloat16)
    after_self = start_state + matmul(self_low, full_self_out)
    normed_two = layer_norm(after_self, gains_float[1], biases_float[1]).astype(jnp.bfloat16)
    cross_query = matmul(normed_two, full_cross_q).astype(jnp.bfloat16)
    kv_proj = matmul(enc_output, full_cross_kv).astype(jnp.bfloat16)
    cross_keys = kv_proj[:, :model_width]
    cross_values = kv_proj[:, model_width:]
    query_all, segment_all = (
        lax.all_gather(cross_query, "src", axis=0, tiled=True),
        lax.all_gather(src_pos * SEGS + segment, "src", axis=0, tiled=True),
    )
    seg_ends = jnp.cumsum(src_lengths[0])
    src_index = src_pos * src_count + lax.broadcasted_iota(jnp.int32, (src_count, 1), 0)
    src_segment = jnp.sum((src_index >= seg_ends[None, :]).astype(jnp.int32), axis=1)
    cross_allowed = segment_all[:, None] == src_segment[None, :]
    block_rows = min(query_all.shape[0], 1024)
    part_top, part_total = attention_stats(query_all, cross_keys, cross_allowed)
    cross_top, cross_total = joined((part_top, part_total), "src", merge_stats)
    cross_low = lax.psum_scatter(
        attention_output(
            query_all, cross_keys, cross_values, cross_allowed, cross_top, cross_total
        ).astype(jnp.bfloat16),
        "src",
        scatter_dimension=0,
        tiled=True,
    )
    after_cross = after_self + matmul(cross_low, full_cross_out)
    normed_three = layer_norm(after_cross, gains_float[2], biases_float[2]).astype(jnp.bfloat16)
    pre_act = matmul(normed_three, full_ffn_in)
    gelu_tanh = partial(jax.nn.gelu, approximate=True)
    act_low = gelu_tanh(pre_act).astype(jnp.bfloat16)
    block_state = after_cross + matmul(act_low, full_ffn_out)
    head_in = layer_norm(block_state, gains_float[3], biases_float[3]).astype(jnp.bfloat16)
    delete_logits = matmul(head_in, full_delete)
    next_in = jnp.concatenate([head_in[1:], jnp.zeros((1, model_width), jnp.bfloat16)], axis=0)
    pair_in = jnp.concatenate([head_in, next_in], axis=1)
    insert_logits = matmul(pair_in, full_insert)
    next_segment = jnp.concatenate([segment[1:], -jnp.ones((1,), jnp.int32)])
    next_keep = jnp.concatenate([not_padding[1:], jnp.zeros((1,), jnp.int32)])
    insert_valid = ((segment == next_segment) & (not_padding == 1) & (next_keep == 1)).astype(
        jnp.float32
    )
    picked = jnp.take(head_in, positions, axis=0)
    picked_keep = jnp.take(not_padding, positions)
    target_or_none = jnp.where(picked_keep == 1, masked_targets[0], -1)
    rows_all, targets_all = (
        lax.all_gather(picked, ("batch", "src"), axis=0, tiled=True),
        lax.all_gather(target_or_none, ("batch", "src"), axis=0, tiled=True),
    )
    vocab_local = w_vocab.shape[0]
    vocab_logits = matmul_nt(rows_all, w_vocab)
    vocab_ids = device_pos * vocab_local + lax.broadcasted_iota(jnp.int32, (1, vocab_local), 1)
    vocab_hits = targets_all[:, None] == vocab_ids
    local_top = jnp.max(vocab_logits, axis=1)
    local_total = jnp.sum(jnp.exp(vocab_logits - local_top[:, None]), axis=1)
    local_chosen = jnp.sum(jnp.where(vocab_hits, vocab_logits, 0.0), axis=1)
    vocab_top, vocab_total, vocab_chosen = joined_2(
        (local_top, local_total, local_chosen), ("batch", "src"), merge_vocab
    )
    token_weight = (targets_all >= 0).astype(jnp.float32)
    token_losses = token_weight * (vocab_top + jnp.log(vocab_total) - vocab_chosen)
    own_token = lax.dynamic_slice_in_dim(token_losses, device_pos * masked_count, masked_count)
    local_loss = (
        jnp.sum(keep_float * entropy_rows(delete_logits, delete_labels[0]))
        + jnp.sum(insert_valid * entropy_rows(insert_logits, insert_counts[0]))
        + jnp.sum(own_token)
    )
    mean_loss = lax.psum(local_loss, ("batch", "src")) / (tok_count * everyone)
    (
        full_gain,
        full_bias,
        full_table,
        full_qkv,
        full_self_out,
        full_cross_q,
        full_cross_kv,
        full_cross_out,
        full_ffn_in,
        full_ffn_out,
        full_delete,
        full_insert,
    ) = (
        lax.all_gather(norm_gain, ("batch", "src"), axis=1, tiled=True),
        lax.all_gather(norm_bias, ("batch", "src"), axis=1, tiled=True),
        lax.all_gather(pair_table, ("batch", "src"), axis=1, tiled=True),
        lax.all_gather(self_qkv, ("batch", "src"), axis=0, tiled=True),
        lax.all_gather(self_out, ("batch", "src"), axis=0, tiled=True),
        lax.all_gather(cross_q, ("batch", "src"), axis=0, tiled=True),
        lax.all_gather(cross_kv, ("batch", "src"), axis=0, tiled=True),
        lax.all_gather(cross_out, ("batch", "src"), axis=0, tiled=True),
        lax.all_gather(ffn_in, ("batch", "src"), axis=0, tiled=True),
        lax.all_gather(ffn_out, ("batch", "src"), axis=0, tiled=True),
        lax.all_gather(w_delete, ("batch", "src"), axis=0, tiled=True),
        lax.all_gather(w_insert, ("batch", "src"), axis=0, tiled=True),
    )
    gains_float = full_gain.astype(jnp.float32)
    biases_float = full_bias.astype(jnp.float32)
    vocab_probs = jnp.exp(vocab_logits - vocab_top[:, None]) / vocab_total[:, None]
    grad_vocab_logits = (
        token_weight[:, None] * (vocab_probs - vocab_hits.astype(jnp.float32))
    ).astype(jnp.bfloat16)
    grad_vocab = matmul_tn(grad_vocab_logits, rows_all) * grad_scale
    grad_picked = lax.psum_scatter(
        matmul(
            lax.slice_in_dim(
                grad_vocab_logits, 0, masked_count * lax.axis_size(("batch", "src")), axis=0
            ),
            w_vocab,
        ),
        ("batch", "src"),
        scatter_dimension=0,
        tiled=True,
    )
    grad_delete_logits = entropy_grad(delete_logits, delete_labels[0], keep_float)
    grad_delete_w = matmul_tn(head_in, grad_delete_logits)
    grad_insert_logits = entropy_grad(insert_logits, insert_counts[0], insert_valid)
    grad_insert_w = matmul_tn(pair_in, grad_insert_logits)
    grad_pair = matmul_nt(grad_insert_logits, full_insert)
    grad_head = (
        matmul_nt(grad_delete_logits, full_delete)
        + grad_pair[:, :model_width]
        + jnp.concatenate(
            [jnp.zeros((1, model_width), jnp.float32), grad_pair[:-1, model_width:]], axis=0
        )
    )
    grad_head = grad_head.at[positions].add(grad_picked)
    grad_block, grad_gain_four, grad_bias_four = norm_backward(
        block_state, gains_float[3], biases_float[3], grad_head
    )
    grad_ffn_branch = grad_block.astype(jnp.bfloat16)
    grad_ffn_out_w = matmul_tn(act_low, grad_ffn_branch)
    grad_act = matmul_nt(grad_ffn_branch, full_ffn_out)
    pull_act = jax.vjp(gelu_tanh, pre_act)[1]
    grad_pre = pull_act(grad_act)[0].astype(jnp.bfloat16)
    grad_ffn_in_w = matmul_tn(normed_three, grad_pre)
    grad_norm_three, grad_gain_three, grad_bias_three = norm_backward(
        after_cross, gains_float[2], biases_float[2], matmul_nt(grad_pre, full_ffn_in)
    )
    grad_cross_state = grad_block + grad_norm_three
    grad_cross_branch = grad_cross_state.astype(jnp.bfloat16)
    grad_cross_out_w = matmul_tn(cross_low, grad_cross_branch)
    grad_cross_attn = matmul_nt(grad_cross_branch, full_cross_out).astype(jnp.bfloat16)
    grad_attn_all = lax.all_gather(grad_cross_attn, "src", axis=0, tiled=True)
    delta_part = attention_delta(
        query_all,
        cross_keys,
        cross_values,
        cross_allowed,
        cross_top,
        cross_total,
        grad_attn_all,
        block_rows,
    )
    delta_full = lax.psum(delta_part.astype(jnp.bfloat16), "src").astype(jnp.float32)
    grad_query_all, grad_cross_keys, grad_cross_values = attention_backward(
        query_all,
        cross_keys,
        cross_values,
        cross_allowed,
        cross_top,
        cross_total,
        delta_full,
        grad_attn_all,
        block_rows,
    )
    grad_query = lax.psum_scatter(
        grad_query_all.astype(jnp.bfloat16), "src", scatter_dimension=0, tiled=True
    )
    grad_cross_q_w = matmul_tn(normed_two, grad_query)
    grad_kv = jnp.concatenate([grad_cross_keys, grad_cross_values], axis=1).astype(jnp.bfloat16)
    grad_cross_kv_w = matmul_tn(enc_output, grad_kv)
    grad_enc = matmul_nt(grad_kv, full_cross_kv).astype(jnp.bfloat16)
    grad_norm_two, grad_gain_two, grad_bias_two = norm_backward(
        after_self, gains_float[1], biases_float[1], matmul_nt(grad_query, full_cross_q)
    )
    grad_self_state = grad_cross_state + grad_norm_two
    grad_self_branch = grad_self_state.astype(jnp.bfloat16)
    grad_self_out_w = matmul_tn(self_low, grad_self_branch)
    grad_self_attn = matmul_nt(grad_self_branch, full_self_out).astype(jnp.bfloat16)
    self_delta = attention_delta(
        self_query,
        self_keys,
        self_values,
        self_allowed,
        self_top,
        self_total,
        grad_self_attn,
        tok_count,
    )
    grad_self_q, grad_self_k, grad_self_v = attention_backward(
        self_query,
        self_keys,
        self_values,
        self_allowed,
        self_top,
        self_total,
        self_delta,
        grad_self_attn,
        tok_count,
    )
    grad_qkv = jnp.concatenate([grad_self_q, grad_self_k, grad_self_v], axis=1).astype(jnp.bfloat16)
    grad_qkv_w = matmul_tn(normed_one, grad_qkv)
    grad_norm_one, grad_gain_one, grad_bias_one = norm_backward(
        start_state, gains_float[0], biases_float[0], matmul_nt(grad_qkv, full_qkv)
    )
    grad_start = grad_self_state + grad_norm_one
    grad_input = grad_start.astype(jnp.bfloat16)
    grad_table = lax.dot_general(
        pair_onehot.astype(jnp.float32),
        grad_start,
        (((0,), (0,)), ((), ())),
        precision=lax.Precision.HIGHEST,
        preferred_element_type=jnp.float32,
    )
    summed = (
        lax.psum_scatter(
            jnp.stack([grad_gain_one, grad_gain_two, grad_gain_three, grad_gain_four]),
            ("batch", "src"),
            scatter_dimension=1,
            tiled=True,
        ),
        lax.psum_scatter(
            jnp.stack([grad_bias_one, grad_bias_two, grad_bias_three, grad_bias_four]),
            ("batch", "src"),
            scatter_dimension=1,
            tiled=True,
        ),
        lax.psum_scatter(grad_table, ("batch", "src"), scatter_dimension=1, tiled=True),
        lax.psum_scatter(grad_qkv_w, ("batch", "src"), scatter_dimension=0, tiled=True),
        lax.psum_scatter(grad_self_out_w, ("batch", "src"), scatter_dimension=0, tiled=True),
        lax.psum_scatter(grad_cross_q_w, ("batch", "src"), scatter_dimension=0, tiled=True),
        lax.psum_scatter(grad_cross_kv_w, ("batch", "src"), scatter_dimension=0, tiled=True),
        lax.psum_scatter(grad_cross_out_w, ("batch", "src"), scatter_dimension=0, tiled=True),
        lax.psum_scatter(grad_ffn_in_w, ("batch", "src"), scatter_dimension=0, tiled=True),
        lax.psum_scatter(grad_ffn_out_w, ("batch", "src"), scatter_dimension=0, tiled=True),
        lax.psum_scatter(grad_delete_w, ("batch", "src"), scatter_dimension=0, tiled=True),
        lax.psum_scatter(grad_insert_w, ("batch", "src"), scatter_dimension=0, tiled=True),
    )
    return (
        block_state.astype(jnp.bfloat16),
        grad_input,
        grad_enc,
        summed[0] * grad_scale,
        summed[1] * grad_scale,
        summed[2] * grad_scale,
        summed[3] * grad_scale,
        summed[4] * grad_scale,
        summed[5] * grad_scale,
        summed[6] * grad_scale,
        summed[7] * grad_scale,
        summed[8] * grad_scale,
        summed[9] * grad_scale,
        summed[10] * grad_scale,
        summed[11] * grad_scale,
        grad_vocab,
        mean_loss,
        own_token[None, :],
    )


def solution(mesh):
    return jax.shard_map(
        body,
        mesh=mesh,
        in_specs=(
            P(("batch", "src"), None),
            P(("batch", "src"), None),
            P(("batch", "src"), None),
            P(("batch", "src"), None),
            P(("batch", "src"), None),
            P("batch", None),
            P(("batch", "src"), None),
            P(("batch", "src"), None),
            P(("batch", "src"), None),
            P(("batch", "src"), None),
            P(None, ("batch", "src")),
            P(None, ("batch", "src")),
            P(None, ("batch", "src")),
            P(("batch", "src"), None),
            P(("batch", "src"), None),
            P(("batch", "src"), None),
            P(("batch", "src"), None),
            P(("batch", "src"), None),
            P(("batch", "src"), None),
            P(("batch", "src"), None),
            P(("batch", "src"), None),
            P(("batch", "src"), None),
            P(("batch", "src"), None),
        ),
        out_specs=(
            P(("batch", "src"), None),
            P(("batch", "src"), None),
            P(("batch", "src"), None),
            P(None, ("batch", "src")),
            P(None, ("batch", "src")),
            P(None, ("batch", "src")),
            P(("batch", "src"), None),
            P(("batch", "src"), None),
            P(("batch", "src"), None),
            P(("batch", "src"), None),
            P(("batch", "src"), None),
            P(("batch", "src"), None),
            P(("batch", "src"), None),
            P(("batch", "src"), None),
            P(("batch", "src"), None),
            P(("batch", "src"), None),
            P(),
            P(("batch", "src"), None),
        ),
        check_vma=False,
    )
```

profile of v0, /device:TPU:0, one launch (start us, length us, event | category | flops | bytes accessed | tf_op | source)
XLA Modules:
  0.0 2950.8 jit_solution(7134924680358696800)
XLA Ops:
  9.4 70.0 %all-gather.4 = bf16[32,16,4]{1,2,0:T(4,128)(2,1)S(1)} all-gather(bf16[1,16,4]{1,2,0:T(4,128)(2,1)} %bitcast.372), channel_id=1, replica_groups=mesh['batch'=16,'src'=2] {'batch','src'}, dimensions={0}, use_global_device_ids=true | all-gather | bytes 4224 | tf_op jit(solution)/shard_map/all_gather | solution.py:257
  79.5 63.7 %all-gather.5 = bf16[32,16,4]{1,2,0:T(4,128)(2,1)S(1)} all-gather(bf16[1,16,4]{1,2,0:T(4,128)(2,1)} %bitcast.373), channel_id=1, replica_groups=mesh['batch'=16,'src'=2] {'batch','src'}, dimensions={0}, use_global_device_ids=true | all-gather | bytes 4224 | tf_op jit(solution)/shard_map/all_gather | solution.py:258
  144.9 66.1 %all-gather.3 = bf16[32,16,8]{1,2,0:T(8,128)(2,1)S(1)} all-gather(bf16[1,16,8]{1,2,0:T(8,128)(2,1)} %bitcast.369), channel_id=1, replica_groups=mesh['batch'=16,'src'=2] {'batch','src'}, dimensions={0}, use_global_device_ids=true | all-gather | bytes 8448 | tf_op jit(solution)/shard_map/all_gather | solution.py:259
  211.1 71.2 %all_gather.85 = bf16[512,512]{1,0:T(8,128)(2,1)} all-gather(bf16[16,512]{1,0:T(8,128)(2,1)} %param.39), channel_id=1, replica_groups=mesh['batch'=16,'src'=2] {'batch','src'}, dimensions={0}, use_global_device_ids=true | all-gather | bytes 540672 | tf_op jit(solution)/shard_map/all_gather | solution.py:261
  282.4 73.4 %all_gather.87 = bf16[512,512]{1,0:T(8,128)(2,1)} all-gather(bf16[16,512]{1,0:T(8,128)(2,1)} %param.40), channel_id=1, replica_groups=mesh['batch'=16,'src'=2] {'batch','src'}, dimensions={0}, use_global_device_ids=true | all-gather | bytes 540672 | tf_op jit(solution)/shard_map/all_gather | solution.py:262
  389.1 6.5 all-gather.20.cloned.1.call-done
  431.0 22.5 fusion.23
  453.7 26.1 fusion.8
  489.0 25.7 fusion.15
  514.8 7.8 fusion.112
  526.0 15.8 fusion.12
  541.9 10.6 fusion.124
  567.9 39.7 %all-reduce.2 = s32[512]{0:T(512)S(1)} all-reduce(s32[512]{0:T(512)S(1)} %fusion.419), channel_id=1, replica_groups=mesh['batch'=16,'src'=2] {'batch','src'}, use_global_device_ids=true, to_apply=%add.2 | all-reduce | flops 512 | bytes 4096
  607.6 73.9 %all_gather.92 = bf16[512,512]{1,0:T(8,128)(2,1)} all-gather(bf16[16,512]{1,0:T(8,128)(2,1)S(1)} %copy-done.108), channel_id=1, replica_groups=mesh['batch'=16,'src'=2] {'batch','src'}, dimensions={0}, use_global_device_ids=true | all-gather | bytes 540672 | tf_op jit(solution)/shard_map/all_gather | solution.py:264
  688.9 17.5 all-gather.26.cloned.1.call-done
  717.1 69.3 %all_gather.98 = bf16[512,512]{1,0:T(8,128)(2,1)S(1)} all-gather(bf16[16,512]{1,0:T(8,128)(2,1)S(1)} %broadcast_select_fusion), channel_id=1, replica_groups=mesh['batch'=16,'src'=2] {'batch','src'}, dimensions={0}, use_global_device_ids=true | all-gather | bytes 540672 | tf_op jit(solution)/shard_map/all_gather | solution.py:337
  791.2 63.7 %all-gather.9 = bf16[32,1,512]{2,1,0:T(2,128)(2,1)S(1)} all-gather(bf16[1,1,512]{2,1,0:T(2,128)(2,1)S(1)} %reshape.698), channel_id=3, replica_groups=mesh['batch'=16,'src'=2] {'batch','src'}, dimensions={0}, use_global_device_ids=true | all-gather | bytes 33792 | tf_op jit(solution)/shard_map/all_gather | solution.py:33
  854.9 65.9 %all-gather.8 = bf16[32,1,512]{2,1,0:T(2,128)(2,1)S(1)} all-gather(bf16[1,1,512]{2,1,0:T(2,128)(2,1)S(1)} %reshape.696), channel_id=2, replica_groups=mesh['batch'=16,'src'=2] {'batch','src'}, dimensions={0}, use_global_device_ids=true | all-gather | bytes 33792 | tf_op jit(solution)/shard_map/all_gather | solution.py:33
  920.9 63.7 %all-gather.10 = bf16[32,1,512]{2,1,0:T(2,128)(2,1)S(1)} all-gather(bf16[1,1,512]{2,1,0:T(2,128)(2,1)S(1)} %reshape.700), channel_id=4, replica_groups=mesh['batch'=16,'src'=2] {'batch','src'}, dimensions={0}, use_global_device_ids=true | all-gather | bytes 33792 | tf_op jit(solution)/shard_map/all_gather | solution.py:33
  994.5 65.2 %all-gather.7 = bf16[32,16,2]{1,2,0:T(2,128)(2,1)S(1)} all-gather(bf16[1,16,2]{1,2,0:T(2,128)(2,1)S(1)} %bitcast.376), channel_id=1, replica_groups=mesh['batch'=16,'src'=2] {'batch','src'}, dimensions={0}, use_global_device_ids=true | all-gather | bytes 2112 | tf_op jit(solution)/shard_map/all_gather | solution.py:267
  1059.8 66.9 %all_gather.96 = bf16[1024,256]{1,0:T(8,128)(2,1)S(1)} all-gather(bf16[32,256]{1,0:T(8,128)(2,1)S(1)} %copy-done.109), channel_id=1, replica_groups=mesh['batch'=16,'src'=2] {'batch','src'}, dimensions={0}, use_global_device_ids=true | all-gather | bytes 540672 | tf_op jit(solution)/shard_map/all_gather | solution.py:268
  1163.2 18.6 all-gather.28.cloned.1.call-done
  1181.8 8.2 multiply_reduce_fusion
  1190.0 8.1 multiply_reduce_fusion.1
  1232.0 7.4 psum.14
  1239.5 8.5 multiply_convert_fusion.7
  1252.3 8.5 multiply_convert_fusion.6
  1260.8 8.5 multiply_convert_fusion.5
  1269.3 8.5 multiply_convert_fusion.4
  1277.8 8.5 multiply_convert_fusion.3
  1286.3 8.5 multiply_convert_fusion.2
  1294.8 8.5 multiply_convert_fusion
  1303.3 8.5 multiply_convert_fusion.1
  1426.7 5.9 convolution_bitcast_fusion
  1445.7 6.4 fusion.330
  1462.2 40.6 %psum.15 = f32[]{:T(128)} all-reduce(f32[]{:T(128)S(6)} %add.335), channel_id=1, replica_groups=mesh['batch'=16,'src'=2] {'batch','src'}, use_global_device_ids=true, to_apply=%region_106.107 | all-reduce | flops 1 | bytes 8 | tf_op jit(solution)/shard_map/psum | solution.py:358
  1509.1 116.6 %reduce-scatter.44.cloned.1.call-done = f32[32,256]{1,0:T(8,128)} async-done(((f32[1024,256]{1,0:T(8,128)}), f32[32,256]{1,0:T(8,128)}) %reduce-scatter.44.cloned.1.call-update) | async-done | bytes 32784 | tf_op jit(solution)/shard_map/reduce_scatter | solution.py:527
  1627.0 6.3 convolution_convert_fusion.1
  1633.3 125.4 %reduce-scatter.38.cloned.1.call-done = f32[16,512]{1,0:T(8,128)} async-done(((f32[512,512]{1,0:T(8,128)}), f32[16,512]{1,0:T(8,128)}) %reduce-scatter.38.cloned.1.call-update) | async-done | bytes 32784 | tf_op jit(solution)/shard_map/reduce_scatter | solution.py:523
  1761.1 129.4 %reduce-scatter.48.cloned.1.call-done = f32[16,4]{1,0:T(8,128)} async-done(((f32[512,4]{1,0:T(8,128)}), f32[16,4]{1,0:T(8,128)}) %reduce-scatter.48.cloned.1.call-update) | async-done | bytes 272
  1891.2 130.8 %reduce-scatter.46.cloned.1.call-done = f32[16,4]{1,0:T(8,128)} async-done(((f32[512,4]{1,0:T(8,128)}), f32[16,4]{1,0:T(8,128)}) %reduce-scatter.46.cloned.1.call-update) | async-done | bytes 272
  2023.9 129.5 %reduce-scatter.50.cloned.1.call-done = f32[16,8]{1,0:T(8,128)} async-done(((f32[512,8]{1,0:T(8,128)}), f32[16,8]{1,0:T(8,128)}) %reduce-scatter.50.cloned.1.call-update) | async-done | bytes 528
  2154.8 133.5 %reduce-scatter.52.cloned.1.call-done = f32[16,1024]{1,0:T(8,128)} async-done(((f32[512,1024]{1,0:T(8,128)}), f32[16,1024]{1,0:T(8,128)}) %reduce-scatter.52.cloned.1.call-update) | async-done | bytes 65552
  2290.2 131.5 %reduce-scatter.36.cloned.1.call-done = f32[16,512]{1,0:T(8,128)} async-done(((f32[512,512]{1,0:T(8,128)}), f32[16,512]{1,0:T(8,128)}) %reduce-scatter.36.cloned.1.call-update) | async-done | bytes 32784 | tf_op jit(solution)/shard_map/reduce_scatter | solution.py:521
  2423.1 131.6 %reduce-scatter.34.cloned.1.call-done = f32[16,512]{1,0:T(8,128)} async-done(((f32[512,512]{1,0:T(8,128)}), f32[16,512]{1,0:T(8,128)}) %reduce-scatter.34.cloned.1.call-update) | async-done | bytes 32784 | tf_op jit(solution)/shard_map/reduce_scatter | solution.py:520
  2556.1 101.6 %reduce-scatter.32.cloned.1.call-done = f32[16,1536]{1,0:T(8,128)} async-done(((f32[512,1536]{1,0:T(8,128)}), f32[16,1536]{1,0:T(8,128)}) %reduce-scatter.32.cloned.1.call-update) | async-done | bytes 98320 | tf_op jit(solution)/shard_map/reduce_scatter | solution.py:519
  2659.2 141.2 %reduce-scatter.42.cloned.1.call-done = f32[64,512]{1,0:T(8,128)} async-done(((f32[2048,512]{1,0:T(8,128)}), f32[64,512]{1,0:T(8,128)}) %reduce-scatter.42.cloned.1.call-update) | async-done | bytes 131088 | tf_op jit(solution)/shard_map/reduce_scatter | solution.py:525
  2802.0 139.1 %reduce-scatter.40.cloned.1.call-done = f32[16,2048]{1,0:T(8,128)} async-done(((f32[512,2048]{1,0:T(8,128)}), f32[16,2048]{1,0:T(8,128)}) %reduce-scatter.40.cloned.1.call-update) | async-done | bytes 131088 | tf_op jit(solution)/shard_map/reduce_scatter | solution.py:524
  (860 shorter events, 366.3 us)
Async XLA Ops:
  7.2 376.3 %copy-start = (bf16[2048,512]{1,0:T(8,128)(2,1)S(1)}, bf16[2048,512]{1,0:T(8,128)(2,1)}, u32[]{:S(2)}) copy-start(bf16[2048,512]{1,0:T(8,128)(2,1)} %param.26) | copy-start | bytes 6291460
  7.2 353.8 %all-gather.18.cloned.1.call-start = ((), (), s32[]{:S(2)}) async-start(), calls=%async_computation.15 | async-start | bytes 1622016 | tf_op jit(solution)/shard_map/all_gather | solution.py:260
  7.9 375.5 %all-gather.22.cloned.1.call-start = ((), (), s32[]{:S(2)}) async-start(), calls=%async_computation.17 | async-start | bytes 1081344 | tf_op jit(solution)/shard_map/all_gather | solution.py:263
  8.7 386.9 %all-gather.20.cloned.1.call-start = ((), (), s32[]{:S(2)}) async-start(), calls=%async_computation.16 | async-start | bytes 1572864 | tf_op jit(solution)/shard_map/all_gather | solution.py:299
  9.4 364.5 %copy-start.110 = (pred[512]{0:T(512)(128)(4,1)}, pred[512]{0:T(512)(128)(4,1)S(1)}, u32[]{:S(2)}) copy-start(pred[512]{0:T(512)(128)(4,1)S(1)} %compare_reduce_fusion) | copy-start | bytes 1540
  144.1 219.5 %copy-start.114 = (f32[1,512]{1,0:T(1,128)}, f32[1,512]{1,0:T(1,128)S(1)}, u32[]{:S(2)}) copy-start(f32[1,512]{1,0:T(1,128)S(1)} %get-tuple-element.441) | copy-start | bytes 6148
  144.1 231.9 %copy-start.116 = (f32[1,512]{1,0:T(1,128)}, f32[1,512]{1,0:T(1,128)S(1)}, u32[]{:S(2)}) copy-start(f32[1,512]{1,0:T(1,128)S(1)} %get-tuple-element.440) | copy-start | bytes 6148
  144.9 218.7 %copy-start.90 = (f32[1,512]{1,0:T(1,128)}, f32[1,512]{1,0:T(1,128)S(1)}, u32[]{:S(2)}) copy-start(f32[1,512]{1,0:T(1,128)S(1)} %get-tuple-element.437) | copy-start | bytes 6148
  144.9 231.1 %copy-start.99 = (f32[1,512]{1,0:T(1,128)}, f32[1,512]{1,0:T(1,128)S(1)}, u32[]{:S(2)}) copy-start(f32[1,512]{1,0:T(1,128)S(1)} %get-tuple-element.436) | copy-start | bytes 6148
  360.1 14.5 copy-start.6
  378.2 303.3 %reduce-scatter.26.cloned.1.call-start = ((), (), s32[]{:S(2)}) async-start(), calls=%async_computation.18 | async-start | bytes 1572864 | tf_op jit(solution)/shard_map/reduce_scatter | solution.py:309
  408.9 44.8 %copy-start.5 = (f32[1024,2048]{1,0:T(8,128)}, f32[1024,2048]{1,0:T(8,128)S(1)}, u32[]{:S(2)}) copy-start(f32[1024,2048]{1,0:T(8,128)S(1)} %fusion.306) | copy-start | bytes 25165828
  514.8 47.7 %copy-start.1 = (f32[1024,2048]{1,0:T(8,128)}, f32[1024,2048]{1,0:T(8,128)S(1)}, u32[]{:S(2)}) copy-start(f32[1024,2048]{1,0:T(8,128)S(1)} %get-tuple-element.426) | copy-start | bytes 25165828
  541.9 15.7 copy-start.4
  541.9 15.7 slice-start.6
  562.5 45.1 %copy-start.108 = (bf16[16,512]{1,0:T(8,128)(2,1)S(1)}, bf16[16,512]{1,0:T(8,128)(2,1)}, u32[]{:S(2)}) copy-start(bf16[16,512]{1,0:T(8,128)(2,1)} %param.42) | copy-start | bytes 49156
  564.9 118.9 %copy-start.82 = (f32[1,512]{1,0:T(1,128)S(1)}, f32[1,512]{1,0:T(1,128)}, u32[]{:S(2)}) copy-start(f32[1,512]{1,0:T(1,128)} %get-tuple-element.435) | copy-start | bytes 6148
  564.9 118.9 %copy-start.86 = (f32[1,512]{1,0:T(1,128)S(1)}, f32[1,512]{1,0:T(1,128)}, u32[]{:S(2)}) copy-start(f32[1,512]{1,0:T(1,128)} %get-tuple-element.439) | copy-start | bytes 6148
  565.9 117.9 %all-gather.24.cloned.1.call-start = ((), (), s32[]{:S(2)}) async-start(), calls=%async_computation.19 | async-start | bytes 2162688 | tf_op jit(solution)/shard_map/all_gather | solution.py:265
  566.5 140.0 %all-gather.26.cloned.1.call-start = ((), (), s32[]{:S(2)}) async-start(), calls=%async_computation.20 | async-start | bytes 2162688 | tf_op jit(solution)/shard_map/all_gather | solution.py:266
  567.0 566.8 %reduce-scatter.28.cloned.1.call-start = ((), (), s32[]{:S(2)}) async-start(), calls=%async_computation.21 | async-start | bytes 1081344 | tf_op jit(solution)/shard_map/reduce_scatter | solution.py:393
  683.6 476.6 %copy-start.21 = (f32[512,512]{0,1:T(8,128)}, f32[512,512]{0,1:T(8,128)S(1)}, u32[]{:S(2)}) copy-start(f32[512,512]{0,1:T(8,128)S(1)} %get-tuple-element.475) | copy-start | bytes 3145732
  683.6 476.6 %copy-start.80 = (f32[512]{0:T(512)}, f32[512]{0:T(512)S(1)}, u32[]{:S(2)}) copy-start(f32[512]{0:T(512)S(1)} %broadcast_multiply_fusion.12) | copy-start | bytes 6148
  683.8 476.4 %copy-start.84 = (f32[512]{0:T(512)}, f32[512]{0:T(512)S(1)}, u32[]{:S(2)}) copy-start(f32[512]{0:T(512)S(1)} %fusion.417) | copy-start | bytes 6148
  688.9 23.4 copy-start.96
  688.9 23.4 copy-start.119
  920.9 73.6 %copy-start.159 = (bf16[16,2]{0,1:T(2,128)(2,1)S(1)}, bf16[16,2]{0,1:T(2,128)(2,1)}, u32[]{:S(2)}) copy-start(bf16[16,2]{0,1:T(2,128)(2,1)} %param.45) | copy-start | bytes 196
  920.9 138.9 %copy-start.109 = (bf16[32,256]{1,0:T(8,128)(2,1)S(1)}, bf16[32,256]{1,0:T(8,128)(2,1)}, u32[]{:S(2)}) copy-start(bf16[32,256]{1,0:T(8,128)(2,1)} %param.46) | copy-start | bytes 49156
  988.1 141.4 %copy-start.107 = (s32[1,512]{1,0:T(1,128)S(1)}, s32[1,512]{1,0:T(1,128)}, u32[]{:S(2)}) copy-start(s32[1,512]{1,0:T(1,128)} %param.31) | copy-start | bytes 6148
  994.3 136.8 %copy-start.154 = (s32[1,512]{1,0:T(1,128)S(1)}, s32[1,512]{1,0:T(1,128)}, u32[]{:S(2)}) copy-start(s32[1,512]{1,0:T(1,128)} %param.32) | copy-start | bytes 6148
  994.3 187.5 %all-gather.28.cloned.1.call-start = ((), (), s32[]{:S(2)}) async-start(), calls=%async_computation.22 | async-start | bytes 1572864 | tf_op jit(solution)/shard_map/all_gather | solution.py:433
  1145.2 15.0 copy-start.112
  1162.9 218.7 %reduce-scatter.30.cloned.1.call-start = ((), (), s32[]{:S(2)}) async-start(), calls=%async_computation.23 | async-start | bytes 1572864 | tf_op jit(solution)/shard_map/reduce_scatter | solution.py:456
  1335.2 171.5 %reduce-scatter.54.cloned.1.call-start = ((), (), s32[]{:S(2)}) async-start(), calls=%async_computation.35 | async-start | bytes 270336
  1336.3 289.4 %reduce-scatter.44.cloned.1.call-start = ((), (), s32[]{:S(2)}) async-start(), calls=%async_computation.30 | async-start | bytes 1081344 | tf_op jit(solution)/shard_map/reduce_scatter | solution.py:527
  1339.3 419.4 %reduce-scatter.38.cloned.1.call-start = ((), (), s32[]{:S(2)}) async-start(), calls=%async_computation.27 | async-start | bytes 1081344 | tf_op jit(solution)/shard_map/reduce_scatter | solution.py:523
  1343.3 547.2 %reduce-scatter.48.cloned.1.call-start = ((), (), s32[]{:S(2)}) async-start(), calls=%async_computation.32 | async-start | bytes 270336
  1423.0 599.0 %reduce-scatter.46.cloned.1.call-start = ((), (), s32[]{:S(2)}) async-start(), calls=%async_computation.31 | async-start | bytes 270336
  1424.0 729.5 %reduce-scatter.50.cloned.1.call-start = ((), (), s32[]{:S(2)}) async-start(), calls=%async_computation.33 | async-start | bytes 270336
  1426.7 861.6 %reduce-scatter.52.cloned.1.call-start = ((), (), s32[]{:S(2)}) async-start(), calls=%async_computation.34 | async-start | bytes 2162688
  1435.8 985.9 %reduce-scatter.36.cloned.1.call-start = ((), (), s32[]{:S(2)}) async-start(), calls=%async_computation.26 | async-start | bytes 1081344 | tf_op jit(solution)/shard_map/reduce_scatter | solution.py:521
  1438.7 1116.0 %reduce-scatter.34.cloned.1.call-start = ((), (), s32[]{:S(2)}) async-start(), calls=%async_computation.25 | async-start | bytes 1081344 | tf_op jit(solution)/shard_map/reduce_scatter | solution.py:520
  1441.4 1216.2 %reduce-scatter.32.cloned.1.call-start = ((), (), s32[]{:S(2)}) async-start(), calls=%async_computation.24 | async-start | bytes 3244032 | tf_op jit(solution)/shard_map/reduce_scatter | solution.py:519
  1445.7 1354.7 %reduce-scatter.42.cloned.1.call-start = ((), (), s32[]{:S(2)}) async-start(), calls=%async_computation.29 | async-start | bytes 4325376 | tf_op jit(solution)/shard_map/reduce_scatter | solution.py:525
  1452.1 1488.9 %reduce-scatter.40.cloned.1.call-start = ((), (), s32[]{:S(2)}) async-start(), calls=%async_computation.28 | async-start | bytes 4325376 | tf_op jit(solution)/shard_map/reduce_scatter | solution.py:524
  1458.2 45.2 %copy-start.43 = (bf16[512,512]{1,0:T(8,128)(2,1)S(1)}, bf16[512,512]{1,0:T(8,128)(2,1)}, u32[]{:S(2)}) copy-start(bf16[512,512]{1,0:T(8,128)(2,1)} %copy-done.42) | copy-start | bytes 1572868
  1458.3 49.8 %copy-start.69 = (bf16[512,512]{0,1:T(8,128)(2,1)S(1)}, bf16[512,512]{0,1:T(8,128)(2,1)}, u32[]{:S(2)}) copy-start(bf16[512,512]{0,1:T(8,128)(2,1)} %get-tuple-element.399) | copy-start | bytes 1572868
  1627.0 133.1 %copy-start.70 = (bf16[512,512]{0,1:T(8,128)(2,1)S(1)}, bf16[512,512]{0,1:T(8,128)(2,1)}, u32[]{:S(2)}) copy-start(bf16[512,512]{0,1:T(8,128)(2,1)} %get-tuple-element.391) | copy-start | bytes 1572868
  (166 other events, 625.8 us)
Sparse Core Ops, SparseCore 0:
  10.9 57.8 all-gather.17
  71.7 52.6 all-gather.21
  378.4 17.1 all-gather.19
  566.0 20.8 reduce-scatter.25
  590.3 57.3 all-gather.23
  651.1 55.2 all-gather.25
  994.4 133.4 reduce-scatter.27
  1163.0 18.7 all-gather.27
  1335.3 21.4 reduce-scatter.29
  1359.0 133.5 reduce-scatter.53
  1494.8 130.7 reduce-scatter.43
  1627.8 130.8 reduce-scatter.37
  1760.9 129.4 reduce-scatter.47
  1892.6 129.3 reduce-scatter.45
  2024.1 129.3 reduce-scatter.49
  2155.7 132.5 reduce-scatter.51
  2290.4 131.2 reduce-scatter.35
  2423.9 130.7 reduce-scatter.33
  2560.1 97.5 reduce-scatter.31
  2659.8 140.5 reduce-scatter.41
  2802.7 138.3 reduce-scatter.39
where the time goes:
time: 2960 us; the launch traced here: 2950 us
  waiting for transfers between devices  1460 us (49%)
  blocking collectives  914 us (31%)
  matrix products  313 us (11%)
  other arithmetic  189 us (6%)
  local copies, waits for them, and re-layouts  54.7 us (2%)
    unnamed x26, waiting for transfers between devices  526 us
    all_gather x3, blocking collectives, joined_2(): lax.all_gather(part.astype(kind), axis)  193 us
    dot_general x42, matrix products, matmul_nt(): lax.dot_general(left, right, (((1,), (1,)), ((), ())), preferred_element_...  141 us
    reduce_scatter x1, waiting for transfers between devices, body(): lax.psum_scatter(grad_ffn_out_w, ('batch', 'src'), scatter_dimension=0, t...  141 us
    reduce_scatter x1, waiting for transfers between devices, body(): lax.psum_scatter(grad_ffn_in_w, ('batch', 'src'), scatter_dimension=0, ti...  139 us
    reduce_scatter x1, waiting for transfers between devices, body(): lax.psum_scatter(grad_self_out_w, ('batch', 'src'), scatter_dimension=0,...  132 us
    reduce_scatter x1, waiting for transfers between devices, body(): lax.psum_scatter(grad_cross_q_w, ('batch', 'src'), scatter_dimension=0, t...  132 us
    reduce_scatter x1, waiting for transfers between devices, body(): lax.psum_scatter(grad_cross_out_w, ('batch', 'src'), scatter_dimension=0,...  125 us
  transfers between devices with their start and end apart: 21, of which 14 were waited for; matrix products, arithmetic and copies ran while one was open for 6% of the time, Pallas kernels for 0%

commit v1 on v0

--- a/solution.py
+++ b/solution.py
@@ -3,6 +3,8 @@
 import jax
 import jax.numpy as jnp
 from jax import lax
+from jax.experimental import pallas as pl
+from jax.experimental.pallas import tpu as pltpu
 from jax.sharding import PartitionSpec as P
 
 HD = 64
@@ -13,34 +15,485 @@
 epsilon = 1e-05
 score_scale = 0.125
 masked_fill = -1e30
-
-
-def joined(x, axis, combine):
-    everything = jax.tree.map(
-        lambda part, kind: lax.all_gather(part.astype(kind), axis), x, (jnp.bfloat16, jnp.bfloat16)
-    )
-
-    def take(k):
-        return jax.tree.map(lambda part, own: part[k].astype(own.dtype), everything, x)
-
-    return lax.fori_loop(
-        1, lax.axis_size(axis), lambda k, so_far: combine(so_far, take(k)), take(0)
-    )
-
-
-def joined_2(x, axis, combine):
-    everything = jax.tree.map(
-        lambda part, kind: lax.all_gather(part.astype(kind), axis),
-        x,
-        (jnp.bfloat16, jnp.bfloat16, jnp.bfloat16),
-    )
-
-    def take(k):
-        return jax.tree.map(lambda part, own: part[k].astype(own.dtype), everything, x)
-
-    return lax.fori_loop(
-        1, lax.axis_size(axis), lambda k, so_far: combine(so_far, take(k)), take(0)
-    )
+BLOCK = 512
+PIECES = 18
+
+
+MESH = pl.DeviceIdType.MESH
+ANY = pl.BlockSpec(memory_space=pl.ANY)
+BOTH = ("batch", "src")
+LOW = jnp.bfloat16
+WIDE = jnp.float32
+
+
+def greet(peers):
+    barrier = pltpu.get_barrier_semaphore()
+    for peer in peers:
+        pl.semaphore_signal(barrier, inc=1, device_id=peer, device_id_type=MESH)
+    pl.semaphore_wait(barrier, len(peers))
+
+
+def remote(src, dst, send, recv, peer):
+    return pltpu.make_async_remote_copy(
+        src_ref=src,
+        dst_ref=dst,
+        send_sem=send,
+        recv_sem=recv,
+        device_id=peer,
+        device_id_type=MESH,
+    )
+
+
+class Place:
+    def __init__(self, depth):
+        b = lax.axis_index("batch")
+        self.depth = depth
+        self.y = lax.axis_index("src")
+        self.c = lax.rem(b, 2)
+        self.x = lax.rem(b // 2, 2)
+        self.z = b // 4
+
+    def at(self, z=None, x=None, c=None, y=None):
+        z = self.z if z is None else z
+        x = self.x if x is None else x
+        c = self.c if c is None else c
+        y = self.y if y is None else y
+        return ((z * 2 + x) * 2 + c, y)
+
+    def along(self, k):
+        return self.at(z=lax.rem(self.z + k, self.depth))
+
+    def peers(self):
+        return [self.along(k) for k in range(1, self.depth)] + [
+            self.at(x=1 - self.x),
+            self.at(y=1 - self.y),
+            self.at(c=1 - self.c),
+        ]
+
+
+def gather_kernel(depth, bounds, x_ref, g_ref, own_sem, send, recv):
+    me = Place(depth)
+    z, x, c, y = me.z, me.x, me.c, me.y
+    greet(me.peers())
+    own = pltpu.make_async_copy(x_ref, g_ref.at[z, x, c, y], own_sem)
+    own.start()
+    count = len(bounds) - 1
+    started = [[None] * 4 for _ in range(count)]
+
+    def launch(k, stage):
+        low, high = bounds[k], bounds[k + 1]
+        middle = (low + high) // 2
+        if stage == 0:
+            rows = pl.ds(low, high - low)
+            copies = [
+                remote(
+                    x_ref.at[rows],
+                    g_ref.at[z, x, c, y, rows],
+                    send.at[k, j],
+                    recv.at[k, j],
+                    me.along(j + 1),
+                )
+                for j in range(depth - 1)
+            ]
+        elif stage == 3:
+            block = g_ref.at[:, :, c, :, pl.ds(low, high - low)]
+            slot = depth + 3
+            copies = [remote(block, block, send.at[k, slot], recv.at[k, slot], me.at(c=1 - c))]
+        else:
+            one, two = pl.ds(low, middle - low), pl.ds(middle, high - middle)
+            if stage == 1:
+                blocks = (g_ref.at[:, x, c, y, one], g_ref.at[:, x, c, y, two])
+                peers = (me.at(x=1 - x), me.at(y=1 - y))
+            else:
+                blocks = (g_ref.at[:, :, c, y, one], g_ref.at[:, x, c, :, two])
+                peers = (me.at(y=1 - y), me.at(x=1 - x))
+            slot = depth - 1 + 2 * (stage - 1)
+            copies = [
+                remote(block, block, send.at[k, slot + i], recv.at[k, slot + i], peer)
+                for i, (block, peer) in enumerate(zip(blocks, peers))
+            ]
+        for copy in copies:
+            copy.start()
+        started[k][stage] = copies
+
+    for step in range(count + 4):
+        for stage in range(4, -1, -1):
+            k = step - stage
+            if not 0 <= k < count:
+                continue
+            if stage == 1 and k == 0:
+                own.wait()
+            if stage > 0:
+                for copy in started[k][stage - 1]:
+                    copy.wait_recv()
+            if stage < 4:
+                launch(k, stage)
+    for stages in started:
+        for copies in stages:
+            for copy in copies:
+                copy.wait_send()
+
+
+def gather_packed(packed, depth, bounds):
+    count = len(bounds) - 1
+    rows, cols = packed.shape
+    out = pl.pallas_call(
+        partial(gather_kernel, depth, bounds),
+        name="gather_packed",
+        out_shape=jax.ShapeDtypeStruct((depth, 2, 2, 2, rows, cols), packed.dtype),
+        in_specs=[ANY],
+        out_specs=ANY,
+        scratch_shapes=[
+            pltpu.SemaphoreType.DMA(()),
+            pltpu.SemaphoreType.DMA((count, depth + 4)),
+            pltpu.SemaphoreType.DMA((count, depth + 4)),
+        ],
+        compiler_params=pltpu.CompilerParams(collective_id=0, has_side_effects=True),
+    )(packed)
+    return out.reshape(depth * 8, rows, cols)
+
+
+def reduce_kernel(depth, bounds, s_ref, o_ref, mine, got_c, got_1, got_2, got_z, load, send, recv):
+    me = Place(depth)
+    z, x, c, y = me.z, me.x, me.c, me.y
+    greet(me.peers())
+    count = len(bounds) - 1
+    pieces = [pl.ds(lo, hi - lo) for lo, hi in zip(bounds[:-1], bounds[1:])]
+    loads = []
+    for k, rows in enumerate(pieces):
+        copy = pltpu.make_async_copy(s_ref.at[:, :, c, :, rows], mine.at[:, :, :, rows], load.at[k])
+        copy.start()
+        loads.append(copy)
+    started = [[None] * 4 for _ in pieces]
+
+    def halves(k):
+        low, high = bounds[k], bounds[k + 1]
+        middle = (low + high) // 2
+        return pl.ds(low, middle - low), pl.ds(middle, high - middle)
+
+    def launch(k, stage):
+        rows = pieces[k]
+        one, two = halves(k)
+        if stage == 0:
+            blocks = [s_ref.at[:, :, 1 - c, :, rows]]
+            places = [got_c.at[:, :, :, rows]]
+            peers = [me.at(c=1 - c)]
+        elif stage == 1:
+            blocks = [mine.at[:, :, 1 - y, one], mine.at[:, 1 - x, :, two]]
+            places = [got_1.at[:, :, one], got_1.at[:, :, two]]
+            peers = [me.at(y=1 - y), me.at(x=1 - x)]
+        elif stage == 2:
+            blocks = [mine.at[:, 1 - x, y, one], mine.at[:, x, 1 - y, two]]
+            places = [got_2.at[:, one], got_2.at[:, two]]
+            peers = [me.at(x=1 - x), me.at(y=1 - y)]
+        else:
+            hops = range(1, depth)
+            blocks = [mine.at[lax.rem(z + j, depth), x, y, rows] for j in hops]
+            places = [got_z.at[j - 1, rows] for j in hops]
+            peers = [me.along(j) for j in hops]
+        slot = (0, 1, 3, 5)[stage]
+        copies = [
+            remote(block, where, send.at[k, slot + i], recv.at[k, slot + i], peer)
+            for i, (block, where, peer) in enumerate(zip(blocks, places, peers))
+        ]
+        for copy in copies:
+            copy.start()
+        started[k][stage] = copies
+
+    def add(where, other):
+        mine[where] = (mine[where].astype(WIDE) + other.astype(WIDE)).astype(LOW)
+
+    def absorb(k, stage):
+        rows = pieces[k]
+        one, two = halves(k)
+        for copy in started[k][stage]:
+            copy.wait_recv()
+        if stage == 0:
+            loads[k].wait()
+
+            @pl.loop(0, depth)
+            def _(zz):
+                for xx in range(2):
+                    for yy in range(2):
+                        add((zz, xx, yy, rows), got_c[zz, xx, yy, rows])
+
+        elif stage == 1:
+
+            @pl.loop(0, depth)
+            def _(zz):
+                for q in range(2):
+                    add((zz, q, y, one), got_1[zz, q, one])
+                    add((zz, x, q, two), got_1[zz, q, two])
+
+        elif stage == 2:
+
+            @pl.loop(0, depth)
+            def _(zz):
+                add((zz, x, y, rows), got_2[zz, rows])
+
+        else:
+            total = mine[z, x, y, rows].astype(WIDE)
+            for j in range(1, depth):
+                total = total + got_z[j - 1, rows].astype(WIDE)
+            o_ref[rows] = total
+
+    for step in range(count + 4):
+        for stage in range(4, -1, -1):
+            k = step - stage
+            if not 0 <= k < count:
+                continue
+            if stage > 0:
+                absorb(k, stage - 1)
+            if stage < 4:
+                launch(k, stage)
+    for stages in started:
+        for copies in stages:
+            for copy in copies:
+                copy.wait_send()
+
+
+def reduce_packed(parts, depth, bounds):
+    count = len(bounds) - 1
+    rows, cols = parts.shape[1:]
+    return pl.pallas_call(
+        partial(reduce_kernel, depth, bounds),
+        name="reduce_packed",
+        out_shape=jax.ShapeDtypeStruct((rows, cols), WIDE),
+        in_specs=[ANY],
+        out_specs=pl.BlockSpec(memory_space=pltpu.VMEM),
+        scratch_shapes=[
+            pltpu.VMEM((depth, 2, 2, rows, cols), LOW),
+            pltpu.VMEM((depth, 2, 2, rows, cols), LOW),
+            pltpu.VMEM((depth, 2, rows, cols), LOW),
+            pltpu.VMEM((depth, rows, cols), LOW),
+            pltpu.VMEM((depth - 1, rows, cols), LOW),
+            pltpu.SemaphoreType.DMA((count,)),
+            pltpu.SemaphoreType.DMA((count, depth + 4)),
+            pltpu.SemaphoreType.DMA((count, depth + 4)),
+        ],
+        compiler_params=pltpu.CompilerParams(
+            collective_id=1, has_side_effects=True, vmem_limit_bytes=48 << 20
+        ),
+    )(parts.reshape((depth, 2, 2, 2, rows, cols)))
+
+
+def swap_kernel(count, *refs):
+    ins, outs, (send, recv) = refs[:count], refs[count : 2 * count], refs[2 * count :]
+    peer = (lax.axis_index("batch"), 1 - lax.axis_index("src"))
+    greet([peer])
+    copies = [
+        remote(ins[k], outs[k], send.at[k], recv.at[k], peer) for k in range(count)
+    ]
+    for copy in copies:
+        copy.start()
+    for copy in copies:
+        copy.wait()
+
+
+def swap(arrays, cid):
+    count = len(arrays)
+    return pl.pallas_call(
+        partial(swap_kernel, count),
+        name=f"swap_{cid}",
+        out_shape=[jax.ShapeDtypeStruct(a.shape, a.dtype) for a in arrays],
+        in_specs=[ANY] * count,
+        out_specs=[ANY] * count,
+        scratch_shapes=[
+            pltpu.SemaphoreType.DMA((count,)),
+            pltpu.SemaphoreType.DMA((count,)),
+        ],
+        compiler_params=pltpu.CompilerParams(collective_id=cid, has_side_effects=True),
+    )(*arrays)
+
+
+def spread_kernel(count, devices, split, *refs):
+    ins, outs, (own_sem, send, recv) = refs[:count], refs[count : 2 * count], refs[2 * count :]
+    pos = lax.axis_index(BOTH)
+    barrier = pltpu.get_barrier_semaphore()
+
+    def peer_of(k):
+        other = lax.rem(pos + k, devices)
+        return other, (other // 2, lax.rem(other, 2))
+
+    def meet(k, carry):
+        pl.semaphore_signal(barrier, inc=1, device_id=peer_of(k)[1], device_id_type=MESH)
+        return carry
+
+    lax.fori_loop(1, devices, meet, 0)
+    pl.semaphore_wait(barrier, devices - 1)
+    locals_ = []
+    for a in range(count):
+        src = ins[a].at[pos] if split else ins[a]
+        locals_.append(pltpu.make_async_copy(src, outs[a].at[pos], own_sem.at[a]))
+        locals_[-1].start()
+
+    def copy_to(a, k):
+        other, peer = peer_of(k)
+        src = ins[a].at[other] if split else ins[a]
+        return remote(src, outs[a].at[pos], send.at[a, k], recv.at[a, k], peer)
+
+    def begin(k, carry):
+        for a in range(count):
+            copy_to(a, k).start()
+        return carry
+
+    def finish(k, carry):
+        for a in range(count):
+            copy_to(a, k).wait()
+        return carry
+
+    lax.fori_loop(1, devices, begin, 0)
+    for copy in locals_:
+        copy.wait()
+    lax.fori_loop(1, devices, finish, 0)
+
+
+def spread(arrays, devices, cid, split):
+    count = len(arrays)
+    lead = () if split else (devices,)
+    return pl.pallas_call(
+        partial(spread_kernel, count, devices, split),
+        name=f"spread_{cid}",
+        out_shape=[jax.ShapeDtypeStruct(lead + a.shape, a.dtype) for a in arrays],
+        in_specs=[ANY] * count,
+        out_specs=[ANY] * count,
+        scratch_shapes=[
+            pltpu.SemaphoreType.DMA((count,)),
+            pltpu.SemaphoreType.DMA((count, devices)),
+            pltpu.SemaphoreType.DMA((count, devices)),
+        ],
+        compiler_params=pltpu.CompilerParams(collective_id=cid, has_side_effects=True),
+    )(*arrays)
+
+
+def piece_bounds(rows, count):
+    step = rows // 32
+    return tuple(32 * (-(-step * k // count)) for k in range(count)) + (rows,)
+
+
+def blocks_of(a, rows):
+    return a.reshape(rows, -1, BLOCK).swapaxes(0, 1).reshape(-1, BLOCK)
+
+
+def pack_weights(
+    gain, bias, table, qkv, self_out, cross_q, cross_kv, cross_out, ffn_in, ffn_out, delete, insert
+):
+    rows = qkv.shape[0]
+    small = jnp.concatenate([gain, bias, table, delete.T], axis=0).T
+    small = jnp.pad(small, ((0, 0), (0, BLOCK - small.shape[1])))
+    pair = jnp.concatenate([insert[:rows], insert[rows:]], axis=1)
+    return jnp.concatenate(
+        [
+            blocks_of(qkv, rows),
+            self_out,
+            cross_q,
+            blocks_of(cross_kv, rows),
+            cross_out,
+            blocks_of(ffn_in, rows),
+            ffn_out,
+            pair,
+            small,
+        ],
+        axis=0,
+    )
+
+
+def unpack_weights(whole):
+    devices = whole.shape[0]
+    rows = whole.shape[1] // PIECES
+
+    def blocks(first, count):
+        part = whole[:, first * rows : (first + count) * rows]
+        part = part.reshape(devices, count, rows, BLOCK).swapaxes(1, 2)
+        return part.reshape(devices * rows, count * BLOCK)
+
+    ffn_out = whole[:, 12 * rows : 16 * rows].reshape(devices * rows * 4, BLOCK)
+    insert = whole[:, 16 * rows : 17 * rows].reshape(devices, rows, 2, BLOCK // 2)
+    insert = insert.swapaxes(1, 2).reshape(devices * rows * 2, BLOCK // 2)
+    small = whole[:, 17 * rows :].reshape(devices * rows, BLOCK)
+    return (
+        small[:, 0:4].T,
+        small[:, 4:8].T,
+        small[:, 8:16].T,
+        blocks(0, 3),
+        blocks(3, 1),
+        blocks(4, 1),
+        blocks(5, 2),
+        blocks(7, 1),
+        blocks(8, 4),
+        ffn_out,
+        small[:, 16:18],
+        insert,
+    )
+
+
+def pack_grads(
+    devices, gain, bias, table, qkv, self_out, cross_q, cross_kv, cross_out, ffn_in, ffn_out, delete, insert
+):
+    rows = BLOCK // devices
+
+    def blocks(a):
+        a = a.astype(LOW).reshape(devices, rows, -1, BLOCK).swapaxes(1, 2)
+        return a.reshape(devices, -1, BLOCK)
+
+    small = jnp.concatenate([gain, bias, table, delete.T], axis=0).T.astype(LOW)
+    small = jnp.pad(small, ((0, 0), (0, BLOCK - small.shape[1])))
+    pair = insert.astype(LOW).reshape(devices, 2, rows, BLOCK // 2).swapaxes(1, 2)
+    return jnp.concatenate(
+        [
+            blocks(qkv),
+            blocks(self_out),
+            blocks(cross_q),
+            blocks(cross_kv),
+            blocks(cross_out),
+            blocks(ffn_in),
+            ffn_out.astype(LOW).reshape(devices, rows * 4, BLOCK),
+            pair.reshape(devices, rows, BLOCK),
+            small.reshape(devices, rows, BLOCK),
+        ],
+        axis=1,
+    )
+
+
+def unpack_grads(own):
+    rows = own.shape[0] // PIECES
+
+    def blocks(first, count):
+        part = own[first * rows : (first + count) * rows].reshape(count, rows, BLOCK)
+        return part.swapaxes(0, 1).reshape(rows, count * BLOCK)
+
+    pair = own[16 * rows : 17 * rows]
+    small = own[17 * rows :]
+    return (
+        small[:, 0:4].T,
+        small[:, 4:8].T,
+        small[:, 8:16].T,
+        blocks(0, 3),
+        blocks(3, 1),
+        blocks(4, 1),
+        blocks(5, 2),
+        blocks(7, 1),
+        blocks(8, 4),
+        own[12 * rows : 16 * rows],
+        small[:, 16:18],
+        jnp.concatenate([pair[:, : BLOCK // 2], pair[:, BLOCK // 2 :]], axis=0),
+    )
+
+
+def gather_weights(packed, devices):
+    rows = packed.shape[0]
+    if rows % (16 * PIECES):
+        return lax.all_gather(packed, BOTH)
+    return gather_packed(packed, devices // 8, piece_bounds(rows, 5))
+
+
+def reduce_grads(parts):
+    devices, rows = parts.shape[:2]
+    if rows % (16 * PIECES):
+        return lax.psum_scatter(
+            parts.astype(WIDE).reshape(devices * rows, -1), BOTH, scatter_dimension=0, tiled=True
+        )
+    return reduce_packed(parts, devices // 8, piece_bounds(rows, 5))
 
 
 def layer_norm(activation, scale_row, shift_row):
@@ -190,16 +643,6 @@
         top_both,
         first_part[1] * jnp.exp(first_part[0] - top_both)
         + second_part[1] * jnp.exp(second_part[0] - top_both),
-    )
-
-
-def merge_vocab(first_part, second_part):
-    top_both = jnp.maximum(first_part[0], second_part[0])
-    return (
-        top_both,
-        first_part[1] * jnp.exp(first_part[0] - top_both)
-        + second_part[1] * jnp.exp(second_part[0] - top_both),
-        first_part[2] + second_part[2],
     )
 
 
@@ -253,19 +696,24 @@
         full_ffn_out,
         full_delete,
         full_insert,
-    ) = (
-        lax.all_gather(norm_gain, ("batch", "src"), axis=1, tiled=True),
-        lax.all_gather(norm_bias, ("batch", "src"), axis=1, tiled=True),
-        lax.all_gather(pair_table, ("batch", "src"), axis=1, tiled=True),
-        lax.all_gather(self_qkv, ("batch", "src"), axis=0, tiled=True),
-        lax.all_gather(self_out, ("batch", "src"), axis=0, tiled=True),
-        lax.all_gather(cross_q, ("batch", "src"), axis=0, tiled=True),
-        lax.all_gather(cross_kv, ("batch", "src"), axis=0, tiled=True),
-        lax.all_gather(cross_out, ("batch", "src"), axis=0, tiled=True),
-        lax.all_gather(ffn_in, ("batch", "src"), axis=0, tiled=True),
-        lax.all_gather(ffn_out, ("batch", "src"), axis=0, tiled=True),
-        lax.all_gather(w_delete, ("batch", "src"), axis=0, tiled=True),
-        lax.all_gather(w_insert, ("batch", "src"), axis=0, tiled=True),
+    ) = unpack_weights(
+        gather_weights(
+            pack_weights(
+                norm_gain,
+                norm_bias,
+                pair_table,
+                self_qkv,
+                self_out,
+                cross_q,
+                cross_kv,
+                cross_out,
+                ffn_in,
+                ffn_out,
+                w_delete,
+                w_insert,
+            ),
+            everyone,
+        )
     )
     gains_float = full_gain.astype(jnp.float32)
     biases_float = full_bias.astype(jnp.float32)
@@ -295,25 +743,34 @@
     kv_proj = matmul(enc_output, full_cross_kv).astype(jnp.bfloat16)
     cross_keys = kv_proj[:, :model_width]
     cross_values = kv_proj[:, model_width:]
-    query_all, segment_all = (
-        lax.all_gather(cross_query, "src", axis=0, tiled=True),
-        lax.all_gather(src_pos * SEGS + segment, "src", axis=0, tiled=True),
-    )
+    own_segment = src_pos * SEGS + segment
+    other_query, other_segment = swap(
+        [cross_query, jnp.broadcast_to(own_segment[None, :], (8, tok_count))], 2
+    )
+    in_order = lambda own, other: jnp.where(
+        src_pos == 0, jnp.concatenate([own, other]), jnp.concatenate([other, own])
+    )
+    query_all = in_order(cross_query, other_query)
+    segment_all = in_order(own_segment, other_segment[0])
     seg_ends = jnp.cumsum(src_lengths[0])
     src_index = src_pos * src_count + lax.broadcasted_iota(jnp.int32, (src_count, 1), 0)
     src_segment = jnp.sum((src_index >= seg_ends[None, :]).astype(jnp.int32), axis=1)
     cross_allowed = segment_all[:, None] == src_segment[None, :]
     block_rows = min(query_all.shape[0], 1024)
     part_top, part_total = attention_stats(query_all, cross_keys, cross_allowed)
-    cross_top, cross_total = joined((part_top, part_total), "src", merge_stats)
-    cross_low = lax.psum_scatter(
-        attention_output(
-            query_all, cross_keys, cross_values, cross_allowed, cross_top, cross_total
-        ).astype(jnp.bfloat16),
-        "src",
-        scatter_dimension=0,
-        tiled=True,
-    )
+    other_stats = swap(
+        [jnp.concatenate([part_top, part_total], axis=1).T], 3
+    )[0].T
+    heads = part_top.shape[1]
+    cross_top, cross_total = merge_stats(
+        (part_top, part_total), (other_stats[:, :heads], other_stats[:, heads:])
+    )
+    part_out = attention_output(
+        query_all, cross_keys, cross_values, cross_allowed, cross_top, cross_total
+    )
+    own_part = lax.dynamic_slice_in_dim(part_out, src_pos * tok_count, tok_count)
+    sent_part = lax.dynamic_slice_in_dim(part_out, (1 - src_pos) * tok_count, tok_count)
+    cross_low = (own_part + swap([sent_part.astype(LOW)], 4)[0].astype(WIDE)).astype(LOW)
     after_cross = after_self + matmul(cross_low, full_cross_out)
     normed_three = layer_norm(after_cross, gains_float[2], biases_float[2]).astype(jnp.bfloat16)
     pre_act = matmul(normed_three, full_ffn_in)
@@ -333,10 +790,12 @@
     picked = jnp.take(head_in, positions, axis=0)
     picked_keep = jnp.take(not_padding, positions)
     target_or_none = jnp.where(picked_keep == 1, masked_targets[0], -1)
-    rows_all, targets_all = (
-        lax.all_gather(picked, ("batch", "src"), axis=0, tiled=True),
-        lax.all_gather(target_or_none, ("batch", "src"), axis=0, tiled=True),
-    )
+    target_tile = jnp.broadcast_to(
+        jnp.pad(target_or_none, (0, 128 - masked_count))[None, :], (8, 128)
+    )
+    rows_all, targets_all = spread([picked, target_tile], everyone, 5, False)
+    rows_all = rows_all.reshape(-1, model_width)
+    targets_all = targets_all[:, 0, :masked_count].reshape(-1)
     vocab_local = w_vocab.shape[0]
     vocab_logits = matmul_nt(rows_all, w_vocab)
     vocab_ids = device_pos * vocab_local + lax.broadcasted_iota(jnp.int32, (1, vocab_local), 1)
@@ -344,11 +803,13 @@
     local_top = jnp.max(vocab_logits, axis=1)
     local_total = jnp.sum(jnp.exp(vocab_logits - local_top[:, None]), axis=1)
     local_chosen = jnp.sum(jnp.where(vocab_hits, vocab_logits, 0.0), axis=1)
-    vocab_top, vocab_total, vocab_chosen = joined_2(
-        (local_top, local_total, local_chosen), ("batch", "src"), merge_vocab
-    )
+    local_stats = jnp.stack([local_top + jnp.log(local_total), local_chosen]).reshape(-1, 128)
+    stats_all = spread([local_stats], everyone, 6, False)[0]
+    stats_all = stats_all.reshape(everyone, 2, -1)
+    vocab_top = jax.nn.logsumexp(stats_all[:, 0], axis=0)
+    vocab_chosen = jnp.sum(stats_all[:, 1], axis=0)
     token_weight = (targets_all >= 0).astype(jnp.float32)
-    token_losses = token_weight * (vocab_top + jnp.log(vocab_total) - vocab_chosen)
+    token_losses = token_weight * (vocab_top - vocab_chosen)
     own_token = lax.dynamic_slice_in_dim(token_losses, device_pos * masked_count, masked_count)
     local_loss = (
         jnp.sum(keep_float * entropy_rows(delete_logits, delete_labels[0]))
@@ -356,51 +817,14 @@
         + jnp.sum(own_token)
     )
     mean_loss = lax.psum(local_loss, ("batch", "src")) / (tok_count * everyone)
-    (
-        full_gain,
-        full_bias,
-        full_table,
-        full_qkv,
-        full_self_out,
-        full_cross_q,
-        full_cross_kv,
-        full_cross_out,
-        full_ffn_in,
-        full_ffn_out,
-        full_delete,
-        full_insert,
-    ) = (
-        lax.all_gather(norm_gain, ("batch", "src"), axis=1, tiled=True),
-        lax.all_gather(norm_bias, ("batch", "src"), axis=1, tiled=True),
-        lax.all_gather(pair_table, ("batch", "src"), axis=1, tiled=True),
-        lax.all_gather(self_qkv, ("batch", "src"), axis=0, tiled=True),
-        lax.all_gather(self_out, ("batch", "src"), axis=0, tiled=True),
-        lax.all_gather(cross_q, ("batch", "src"), axis=0, tiled=True),
-        lax.all_gather(cross_kv, ("batch", "src"), axis=0, tiled=True),
-        lax.all_gather(cross_out, ("batch", "src"), axis=0, tiled=True),
-        lax.all_gather(ffn_in, ("batch", "src"), axis=0, tiled=True),
-        lax.all_gather(ffn_out, ("batch", "src"), axis=0, tiled=True),
-        lax.all_gather(w_delete, ("batch", "src"), axis=0, tiled=True),
-        lax.all_gather(w_insert, ("batch", "src"), axis=0, tiled=True),
-    )
-    gains_float = full_gain.astype(jnp.float32)
-    biases_float = full_bias.astype(jnp.float32)
-    vocab_probs = jnp.exp(vocab_logits - vocab_top[:, None]) / vocab_total[:, None]
+    vocab_probs = jnp.exp(vocab_logits - vocab_top[:, None])
     grad_vocab_logits = (
         token_weight[:, None] * (vocab_probs - vocab_hits.astype(jnp.float32))
     ).astype(jnp.bfloat16)
     grad_vocab = matmul_tn(grad_vocab_logits, rows_all) * grad_scale
-    grad_picked = lax.psum_scatter(
-        matmul(
-            lax.slice_in_dim(
-                grad_vocab_logits, 0, masked_count * lax.axis_size(("batch", "src")), axis=0
-            ),
-            w_vocab,
-        ),
-        ("batch", "src"),
-        scatter_dimension=0,
-        tiled=True,
-    )
+    grad_rows = matmul(grad_vocab_logits, w_vocab).astype(LOW)
+    grad_rows = spread([grad_rows.reshape(everyone, masked_count, model_width)], everyone, 7, True)
+    grad_picked = jnp.sum(grad_rows[0].astype(WIDE), axis=0)
     grad_delete_logits = entropy_grad(delete_logits, delete_labels[0], keep_float)
     grad_delete_w = matmul_tn(head_in, grad_delete_logits)
     grad_insert_logits = entropy_grad(insert_logits, insert_counts[0], insert_valid)
@@ -430,7 +854,7 @@
     grad_cross_branch = grad_cross_state.astype(jnp.bfloat16)
     grad_cross_out_w = matmul_tn(cross_low, grad_cross_branch)
     grad_cross_attn = matmul_nt(grad_cross_branch, full_cross_out).astype(jnp.bfloat16)
-    grad_attn_all = lax.all_gather(grad_cross_attn, "src", axis=0, tiled=True)
+    grad_attn_all = in_order(grad_cross_attn, swap([grad_cross_attn], 8)[0])
     delta_part = attention_delta(
         query_all,
         cross_keys,
@@ -441,7 +865,7 @@
         grad_attn_all,
         block_rows,
     )
-    delta_full = lax.psum(delta_part.astype(jnp.bfloat16), "src").astype(jnp.float32)
+    delta_full = delta_part + swap([delta_part.T], 9)[0].T
     grad_query_all, grad_cross_keys, grad_cross_values = attention_backward(
         query_all,
         cross_keys,
@@ -453,9 +877,9 @@
         grad_attn_all,
         block_rows,
     )
-    grad_query = lax.psum_scatter(
-        grad_query_all.astype(jnp.bfloat16), "src", scatter_dimension=0, tiled=True
-    )
+    own_part = lax.dynamic_slice_in_dim(grad_query_all, src_pos * tok_count, tok_count)
+    sent_part = lax.dynamic_slice_in_dim(grad_query_all, (1 - src_pos) * tok_count, tok_count)
+    grad_query = (own_part + swap([sent_part.astype(LOW)], 10)[0].astype(WIDE)).astype(LOW)
     grad_cross_q_w = matmul_tn(normed_two, grad_query)
     grad_kv = jnp.concatenate([grad_cross_keys, grad_cross_values], axis=1).astype(jnp.bfloat16)
     grad_cross_kv_w = matmul_tn(enc_output, grad_kv)
@@ -502,29 +926,24 @@
         precision=lax.Precision.HIGHEST,
         preferred_element_type=jnp.float32,
     )
-    summed = (
-        lax.psum_scatter(
-            jnp.stack([grad_gain_one, grad_gain_two, grad_gain_three, grad_gain_four]),
-            ("batch", "src"),
-            scatter_dimension=1,
-            tiled=True,
-        ),
-        lax.psum_scatter(
-            jnp.stack([grad_bias_one, grad_bias_two, grad_bias_three, grad_bias_four]),
-            ("batch", "src"),
-            scatter_dimension=1,
-            tiled=True,
-        ),
-        lax.psum_scatter(grad_table, ("batch", "src"), scatter_dimension=1, tiled=True),
-        lax.psum_scatter(grad_qkv_w, ("batch", "src"), scatter_dimension=0, tiled=True),
-        lax.psum_scatter(grad_self_out_w, ("batch", "src"), scatter_dimension=0, tiled=True),
-        lax.psum_scatter(grad_cross_q_w, ("batch", "src"), scatter_dimension=0, tiled=True),
-        lax.psum_scatter(grad_cross_kv_w, ("batch", "src"), scatter_dimension=0, tiled=True),
-        lax.psum_scatter(grad_cross_out_w, ("batch", "src"), scatter_dimension=0, tiled=True),
-        lax.psum_scatter(grad_ffn_in_w, ("batch", "src"), scatter_dimension=0, tiled=True),
-        lax.psum_scatter(grad_ffn_out_w, ("batch", "src"), scatter_dimension=0, tiled=True),
-        lax.psum_scatter(grad_delete_w, ("batch", "src"), scatter_dimension=0, tiled=True),
-        lax.psum_scatter(grad_insert_w, ("batch", "src"), scatter_dimension=0, tiled=True),
+    summed = unpack_grads(
+        reduce_grads(
+            pack_grads(
+                everyone,
+                jnp.stack([grad_gain_one, grad_gain_two, grad_gain_three, grad_gain_four]),
+                jnp.stack([grad_bias_one, grad_bias_two, grad_bias_three, grad_bias_four]),
+                grad_table,
+                grad_qkv_w,
+                grad_self_out_w,
+                grad_cross_q_w,
+                grad_cross_kv_w,
+                grad_cross_out_w,
+                grad_ffn_in_w,
+                grad_ffn_out_w,
+                grad_delete_w,
+                grad_insert_w,
+            )
+        )
     )
     return (
         block_state.astype(jnp.bfloat16),

time: 2960 us -> 913 us (0.31)
  waiting for transfers between devices: 1460 us -> 0 us
  blocking collectives: 914 us -> 40.3 us
  Pallas kernels: 0 us -> 232 us
  local copies, waits for them, and re-layouts: 54.7 us -> 147 us
  matrix products: 313 us -> 274 us
    reduce_scatter x10 -> x0, waiting for transfers between devices: 887 us -> none  [the longest x1 141 us: body(): lax.psum_scatter(grad_ffn_out_w, ('batch', 'src'), scatter_dimension=0, t...]
    all_gather x15 -> x0, blocking collectives: 827 us -> none  [the longest x3 193 us: joined_2(): lax.all_gather(part.astype(kind), axis)]
    unnamed x26 -> x0, waiting for transfers between devices: 526 us -> none
    pallas_call x0 -> x11, Pallas kernels: none -> 232 us  [the longest x6 64.6 us: swap(): pl.pallas_call(partial(swap_kernel, count), name=f'swap_{cid}', out_shape...]
    all_gather x6 -> x0, waiting for transfers between devices: 42.7 us -> none  [the longest x1 18.6 us: body(): grad_attn_all = lax.all_gather(grad_cross_attn, 'src', axis=0, tiled=True)]
    unnamed x1 -> x0, blocking collectives: 39.7 us -> none
    dot_general x41 -> x42, matrix products: 71.4 us -> 49.3 us  [matmul_tn(): lax.dot_general(left, right, (((0,), (0,)), ((), ())), preferred_element_...]
  transfers between devices with their start and end apart: 21 -> 0, of which waited for: 14 -> 0; matrix products, arithmetic and copies ran while one was open for 6% -> 0% of each run, Pallas kernels for 0% -> 0%
where the time goes in v1:
time: 913 us; the launch traced here: 902 us
  matrix products  274 us (30%)
  Pallas kernels  232 us (25%)
  other arithmetic  201 us (22%)
  local copies, waits for them, and re-layouts  147 us (16%)
  blocking collectives  40.3 us (4%)
    dot_general x42, matrix products, matmul_nt(): lax.dot_general(left, right, (((1,), (1,)), ((), ())), preferred_element_...  145 us
    dot_general x43, matrix products, matmul(): return jnp.dot(left, right, preferred_element_type=jnp.float32)  78 us
    convert_element_type x11, other arithmetic, attention_backward(): (probs_full * (grad_prob - delta[0:block, head_pos:head_pos + 1])).astype...  72.8 us
    pallas_call x6, Pallas kernels, swap(): pl.pallas_call(partial(swap_kernel, count), name=f'swap_{cid}', out_shape...  64.6 us
    pallas_call x1, Pallas kernels, gather_packed(): pl.pallas_call(partial(gather_kernel, depth, bounds), name='gather_packed...  62.8 us
    pallas_call x1, Pallas kernels, reduce_packed(): pl.pallas_call(partial(reduce_kernel, depth, bounds), name='reduce_packed...  61.7 us
    unnamed x467, local copies, waits for them, and re-layouts  56.6 us
    dot_general x42, matrix products, matmul_tn(): lax.dot_general(left, right, (((0,), (0,)), ((), ())), preferred_element_...  49.3 us

profile of v1, /device:TPU:0, one launch (start us, length us, event | category | flops | bytes accessed | tf_op | source)
XLA Modules:
  0.0 901.6 jit_solution(14957313558239900407)
XLA Ops:
  23.7 62.8 %gather_packed.1 = bf16[4,2,2,2,288,512]{5,4,3,2,1,0:T(8,128)(2,1)} custom-call(bf16[288,512]{1,0:T(8,128)(2,1)} %copy-done.97), custom_call_target="tpu_custom_call" | custom-call | tf_op jit(solution)/shard_map/gather_packed/pallas_call | solution.py:140
  125.4 15.0 %swap_2.1 = (bf16[512,512]{1,0:T(8,128)(2,1)}, s32[8,512]{1,0:T(8,128)}) custom-call(bf16[512,512]{1,0:T(8,128)(2,1)} %convolution_convert_fusion.20.refs_0_, s32[8,512]{1,0:T(8,128)} %broadcast_in_dim.362.refs_1_), custom_call_target="tpu_custom_call" | custom-call | tf_op jit(solution)/shard_map/swap_2/pallas_call | solution.py:295
  145.5 4.5 fusion.231
  152.5 16.8 %fusion.246 = f32[1024,2048]{1,0:T(8,128)} fusion(bf16[2048,1024]{0,1:T(8,128)(2,1)S(1)} %convert_bitcast_fusion, bf16[1024,512]{1,0:T(8,128)(2,1)S(1)} %maximum_select_fusion), kind=kOutput, calls=%fused_computation.453 | convolution fusion | flops 268435456 | bytes 8912896 | tf_op jit(solution)/shard_map/dot_general | solution.py:521
  169.3 4.5 fusion.251
  173.8 4.6 fusion.256
  178.4 4.5 fusion.261
  182.9 20.4 %fusion.23 = (f32[1024]{0:T(1024)S(1)}, f32[1024]{0:T(1024)S(1)}, f32[1024]{0:T(1024)S(1)}, f32[1024]{0:T(1024)S(1)}, f32[1024]{0:T(1024)S(1)}, /*index=5*/f32[1...) fusion(s32[2048]{0:T(1024)S(1)} %convert_reduce_fusion.1, s32[1024]{0:T(1024)S(1)} %add_select_fusion, ...), kind=kOutput, calls=%fused_computation.68 | convolution fusion | flops 320856064 | bytes 67678208 | tf_op jit(solution)/shard_map/dot_general | solution.py:521
  203.4 27.3 %fusion.7 = (f32[1024]{0:T(1024)S(1)}, f32[1024]{0:T(1024)S(1)}, f32[1024]{0:T(1024)S(1)}, f32[1024]{0:T(1024)S(1)}, f32[1024]{0:T(1024)S(1)}, /*index=5*/f32[1024]{0:T(1024)S(1)}, f32[1024]{0:T(1024)S(1)}, f32[1024]{0:T(1024)S(1)}) fusion(f32[1024,2048]{1,0:T(8,128)} %get-tuple-element.272, f32[1024]{0:T(1024)S(1)} %get-tuple-element.146, ...), kind=kLoop, calls=%fused_computation.34 | loop fusion | flops 85975040 | bytes 67186688 | tf_op jit(solution)/shard_map/reduce_sum | solution.py:565
  232.1 4.6 swap_3.1
  237.6 17.8 %fusion.13 = (f32[1024,2048]{1,0:T(8,128)S(1)}, f32[1024,2048]{1,0:T(8,128)}, f32[1024,2048]{1,0:T(8,128)}) fusion(f32[1024,2048]{1,0:T(8,128)} %copy-done.2, f32[1024]{0:T(1024)S(1)} %bitcast.440, f32[1024]{0:T(1024)S(1)} %bitcast.435, s32[2048]{0:T(1024)S(1)} %convert_reduce_fusion.1, s32[1024]{0:T(1024)S(1)} %add_select_fusion, f32[1024]{0:T(1024)S(1)} %bitcast.441, ...), kind=kLoop, calls=%fused_computation.40 | loop fusion | flops 33554432 | bytes 50368512 | tf_op jit(solution)/shard_map/div | solution.py:552
  255.4 31.0 %fusion.15 = (f32[1024,2048]{1,0:T(8,128)}, f32[1024,2048]{1,0:T(8,128)}, f32[1024,2048]{1,0:T(8,128)}, f32[1024,2048]{1,0:T(8,128)}, f32[1024,2048]{1,0:T(8,128)}) fusion(f32[1024,2048]{1,0:T(8,128)} %get-tuple-element.272, f32[1024]{0:T(1024)S(1)} %bitcast.428, f32[1024]{0:T(1024)S(1)} %bitcast.423, s32[2048]{0:T(1024)S(1)} %convert_reduce_fusion.1, ...), kind=kLoop, calls=%fused_computation.42 | loop fusion | flops 54525952 | bytes 83939328 | tf_op jit(solution)/shard_map/div | solution.py:552
  286.5 4.8 fusion.60
  313.8 4.5 concatenate.134
  320.5 12.7 %swap_4.1 = bf16[512,512]{1,0:T(8,128)(2,1)} custom-call(bf16[512,512]{1,0:T(8,128)(2,1)} %dynamic-slice_convert_fusion.1.refs_0_), custom_call_target="tpu_custom_call" | custom-call | tf_op jit(solution)/shard_map/swap_4/pallas_call | solution.py:295
  360.6 15.6 %spread_5.1 = (bf16[32,16,512]{2,1,0:T(8,128)(2,1)}, s32[32,8,128]{2,1,0:T(8,128)}) custom-call(bf16[16,512]{1,0:T(8,128)(2,1)} %broadcast_select_fusion.refs_0_, s32[8,128]{1,0:T(8,128)} %broadcast_in_dim.384.refs_1_), custom_call_target="tpu_custom_call" | custom-call | tf_op jit(solution)/shard_map/spread_5/pallas_call | solution.py:354
  385.0 13.3 %spread_6.1 = f32[32,8,128]{2,1,0:T(8,128)} custom-call(f32[8,128]{1,0:T(8,128)} %reshape.538.refs_0_), custom_call_target="tpu_custom_call" | custom-call | tf_op jit(solution)/shard_map/spread_6/pallas_call | solution.py:354
  401.3 40.3 %psum.7 = f32[]{:T(128)} all-reduce(f32[]{:T(128)S(6)} %add.297), channel_id=1, replica_groups=mesh['batch'=16,'src'=2] {'batch','src'}, use_global_device_ids=true, to_apply=%region_92.93 | all-reduce | flops 1 | bytes 8 | tf_op jit(solution)/shard_map/psum | solution.py:819
  448.1 14.1 %spread_7.1 = bf16[32,16,512]{2,1,0:T(8,128)(2,1)} custom-call(bf16[32,16,512]{2,1,0:T(8,128)(2,1)} %bitcast.338), custom_call_target="tpu_custom_call" | custom-call | tf_op jit(solution)/shard_map/spread_7/pallas_call | solution.py:354
  476.0 5.6 fusion.30
  489.9 4.9 reshape.543
  514.5 15.1 %swap_8.1 = bf16[512,512]{1,0:T(8,128)(2,1)} custom-call(bf16[512,512]{1,0:T(8,128)(2,1)} %convolution_convert_fusion.19.refs_0_), custom_call_target="tpu_custom_call" | custom-call | tf_op jit(solution)/shard_map/swap_8/pallas_call | solution.py:295
  532.7 8.2 multiply_reduce_fusion
  540.9 5.6 multiply_reduce_fusion.1
  546.6 5.7 multiply_reduce_fusion.2
  552.3 5.6 multiply_reduce_fusion.3
  557.9 5.7 multiply_reduce_fusion.4
  563.7 5.7 multiply_reduce_fusion.5
  569.4 5.9 multiply_reduce_fusion.6
  575.4 5.5 multiply_reduce_fusion.7
  581.5 4.2 swap_9.1
  586.6 8.5 multiply_convert_fusion.7
  595.1 8.5 multiply_convert_fusion.6
  603.6 8.5 multiply_convert_fusion.5
  612.1 8.5 multiply_convert_fusion.4
  620.6 8.6 multiply_convert_fusion.3
  629.2 8.5 multiply_convert_fusion.2
  637.7 8.5 multiply_convert_fusion
  646.3 8.6 multiply_convert_fusion.1
  654.9 4.4 convolution_multiply_fusion.18
  662.4 3.6 convolution_multiply_fusion.19
  681.6 4.6 concatenate.144
  725.7 13.0 %swap_10.1 = bf16[512,512]{1,0:T(8,128)(2,1)} custom-call(bf16[512,512]{1,0:T(8,128)(2,1)} %dynamic-slice_convert_fusion.refs_0_), custom_call_target="tpu_custom_call" | custom-call | tf_op jit(solution)/shard_map/swap_10/pallas_call | solution.py:295
  762.9 3.8 convolution_convert_fusion.1
  774.3 4.8 multiply_reduce_fusion.17
  802.1 5.8 reshape.541
  827.8 3.7 copy-done.35
  831.5 61.7 %reduce_packed.1 = f32[288,512]{1,0:T(8,128)S(1)} custom-call(bf16[4,2,2,2,288,512]{5,4,3,2,1,0:T(8,128)(2,1)} %copy-done.35), custom_call_target="tpu_custom_call" | custom-call | tf_op jit(solution)/shard_map/reduce_packed/pallas_call | solution.py:258
  (748 shorter events, 323.2 us)
Async XLA Ops:
  0.7 142.4 %copy-start = (bf16[2048,512]{1,0:T(8,128)(2,1)S(1)}, bf16[2048,512]{1,0:T(8,128)(2,1)}, u32[]{:S(2)}) copy-start(bf16[2048,512]{1,0:T(8,128)(2,1)} %param.24) | copy-start | bytes 6291460
  1.5 118.8 %copy-start.127 = (pred[512]{0:T(512)(128)(4,1)}, pred[512]{0:T(512)(128)(4,1)S(1)}, u32[]{:S(2)}) copy-start(pred[512]{0:T(512)(128)(4,1)S(1)} %compare_reduce_fusion) | copy-start | bytes 1540
  2.2 84.4 %copy-start.171 = (s32[16]{0:T(128)}, s32[16]{0:T(128)S(1)}, u32[]{:S(2)}) copy-start(s32[16]{0:T(128)S(1)} %fusion.355) | copy-start | bytes 196
  3.0 104.8 %copy-start.114 = (s32[512]{0:T(512)}, s32[512]{0:T(512)S(1)}, u32[]{:S(2)}) copy-start(s32[512]{0:T(512)S(1)} %select_reduce_fusion.1) | copy-start | bytes 6148
  3.7 82.9 %copy-start.4 = (s32[1,512]{1,0:T(1,128)}, s32[1,512]{1,0:T(1,128)S(1)}, u32[]{:S(2)}) copy-start(s32[1,512]{1,0:T(1,128)S(1)} %broadcast_subtract_fusion) | copy-start | bytes 6148
  96.4 11.4 %copy-start.77 = (bf16[32,16,512]{2,1,0:T(8,128)(2,1)}, bf16[32,16,512]{2,1,0:T(8,128)(2,1)S(1)}, u32[]{:S(2)}) copy-start(bf16[32,16,512]{2,1,0:T(8,128)(2,1)S(1)} %get-tuple-element.189) | copy-start | bytes 1572868
  96.4 24.6 %copy-start.45 = (bf16[32,16,512]{2,1,0:T(8,128)(2,1)}, bf16[32,16,512]{2,1,0:T(8,128)(2,1)S(1)}, u32[]{:S(2)}) copy-start(bf16[32,16,512]{2,1,0:T(8,128)(2,1)S(1)} %get-tuple-element.188) | copy-start | bytes 1572868
  107.8 14.7 %copy-start.125 = (f32[512]{0:T(512)}, f32[512]{0:T(512)S(1)}, u32[]{:S(2)}) copy-start(f32[512]{0:T(512)S(1)} %get-tuple-element.308) | copy-start | bytes 6148
  108.2 12.7 %copy-start.7 = (f32[512,512]{0,1:T(8,128)}, f32[512,512]{0,1:T(8,128)S(1)}, u32[]{:S(2)}) copy-start(f32[512,512]{0,1:T(8,128)S(1)} %get-tuple-element.253) | copy-start | bytes 3145732
  109.7 10.6 %copy-start.42 = (bf16[512,1536]{1,0:T(8,128)(2,1)}, bf16[512,1536]{1,0:T(8,128)(2,1)S(1)}, u32[]{:S(2)}) copy-start(bf16[512,1536]{1,0:T(8,128)(2,1)S(1)} %convolution_convert_fusion.2) | copy-start | bytes 4718596
  110.2 10.1 %copy-start.61 = (f32[512,512]{0,1:T(8,128)}, f32[512,512]{0,1:T(8,128)S(1)}, u32[]{:S(2)}) copy-start(f32[512,512]{0,1:T(8,128)S(1)} %get-tuple-element.255) | copy-start | bytes 3145732
  110.2 10.1 %copy-start.145 = (f32[512]{0:T(512)}, f32[512]{0:T(512)S(1)}, u32[]{:S(2)}) copy-start(f32[512]{0:T(512)S(1)} %get-tuple-element.254) | copy-start | bytes 6148
  110.9 8.8 copy-start.63
  110.9 8.8 copy-start.147
  111.5 7.6 copy-start.65
  111.5 7.6 copy-start.149
  121.8 21.2 %copy-start.93 = (bf16[64,8,2,512]{3,1,2,0:T(8,128)(2,1)S(1)}, bf16[64,8,2,512]{3,1,2,0:T(8,128)(2,1)}, u32[]{:S(2)}) copy-start(bf16[64,8,2,512]{3,1,2,0:T(8,128)(2,1)} %copy.330) | copy-start | bytes 3145732
  143.0 39.8 %copy-start.9 = (bf16[1024,512]{1,0:T(8,128)(2,1)}, bf16[1024,512]{1,0:T(8,128)(2,1)S(1)}, u32[]{:S(2)}) copy-start(bf16[1024,512]{1,0:T(8,128)(2,1)S(1)} %maximum_select_fusion) | copy-start | bytes 3145732
  145.4 33.0 %copy-start.36 = (bf16[2048,1024]{0,1:T(8,128)(2,1)}, bf16[2048,1024]{0,1:T(8,128)(2,1)S(1)}, u32[]{:S(2)}) copy-start(bf16[2048,1024]{0,1:T(8,128)(2,1)S(1)} %convert_bitcast_fusion) | copy-start | bytes 12582916
  151.2 31.7 %copy-start.2 = (f32[1024,2048]{1,0:T(8,128)}, f32[1024,2048]{1,0:T(8,128)S(1)}, u32[]{:S(2)}) copy-start(f32[1024,2048]{1,0:T(8,128)S(1)} %fusion.236) | copy-start | bytes 25165828
  152.5 30.4 %copy-start.3 = (f32[1024,2048]{1,0:T(8,128)}, f32[1024,2048]{1,0:T(8,128)S(1)}, u32[]{:S(2)}) copy-start(f32[1024,2048]{1,0:T(8,128)S(1)} %fusion.241) | copy-start | bytes 25165828
  255.4 49.1 %copy-start.1 = (f32[1024,2048]{1,0:T(8,128)}, f32[1024,2048]{1,0:T(8,128)S(1)}, u32[]{:S(2)}) copy-start(f32[1024,2048]{1,0:T(8,128)S(1)} %get-tuple-element.238) | copy-start | bytes 25165828
  286.5 8.3 slice-start.30
  318.4 19.4 %copy-start.101 = (f32[512]{0:T(512)S(1)}, f32[512]{0:T(512)}, u32[]{:S(2)}) copy-start(f32[512]{0:T(512)} %get-tuple-element.309) | copy-start | bytes 6148
  318.4 19.4 %copy-start.122 = (f32[512]{0:T(512)S(1)}, f32[512]{0:T(512)}, u32[]{:S(2)}) copy-start(f32[512]{0:T(512)} %get-tuple-element.133) | copy-start | bytes 6148
  342.0 8.5 copy-start.173
  343.2 9.8 %copy-start.170 = (s32[1,512]{1,0:T(1,128)S(1)}, s32[1,512]{1,0:T(1,128)}, u32[]{:S(2)}) copy-start(s32[1,512]{1,0:T(1,128)} %param.30) | copy-start | bytes 6148
  343.2 10.0 %copy-start.5 = (s32[1,512]{1,0:T(1,128)S(1)}, s32[1,512]{1,0:T(1,128)}, u32[]{:S(2)}) copy-start(s32[1,512]{1,0:T(1,128)} %copy-done.4) | copy-start | bytes 6148
  343.2 10.0 %copy-start.99 = (s32[1,512]{1,0:T(1,128)S(1)}, s32[1,512]{1,0:T(1,128)}, u32[]{:S(2)}) copy-start(s32[1,512]{1,0:T(1,128)} %param.25) | copy-start | bytes 6148
  343.3 10.0 %copy-start.134 = (s32[1,511]{1,0:T(1,128)S(1)}, s32[1,511]{1,0:T(1,128)}, u32[]{:S(2)}) copy-start(s32[1,511]{1,0:T(1,128)} %slice.916) | copy-start | bytes 6136
  343.3 10.0 %copy-start.135 = (s32[1,511]{1,0:T(1,128)S(1)}, s32[1,511]{1,0:T(1,128)}, u32[]{:S(2)}) copy-start(s32[1,511]{1,0:T(1,128)} %slice.779) | copy-start | bytes 6136
  399.4 63.9 %copy-start.172 = (s32[16]{0:T(128)S(1)}, s32[16]{0:T(128)}, u32[]{:S(2)}) copy-start(s32[16]{0:T(128)} %copy-done.171) | copy-start | bytes 196
  529.6 11.2 %slice-start.20 = ((s8[8388608]{0:T(1024)(128)(4,1)}), s8[4194304]{0:T(1024)(128)(4,1)S(1)}, s32[]{:S(2)}) async-start(s8[8388608]{0:T(1024)(128)(4,1)} %bitcast.267), calls=%async_computation.20 | async-start | bytes 8388608
  532.6 8.2 slice-start.21
  723.5 16.9 %copy-start.16 = (f32[512,512]{0,1:T(8,128)S(1)}, f32[512,512]{0,1:T(8,128)}, u32[]{:S(2)}) copy-start(f32[512,512]{0,1:T(8,128)} %copy-done.15) | copy-start | bytes 3145732
  723.5 16.9 %copy-start.109 = (f32[512]{0:T(512)S(1)}, f32[512]{0:T(512)}, u32[]{:S(2)}) copy-start(f32[512]{0:T(512)} %copy-done.108) | copy-start | bytes 6148
  723.5 16.9 %copy-start.124 = (f32[512]{0:T(512)S(1)}, f32[512]{0:T(512)}, u32[]{:S(2)}) copy-start(f32[512]{0:T(512)} %copy-done.123) | copy-start | bytes 6148
  723.5 16.9 %copy-start.126 = (f32[512]{0:T(512)S(1)}, f32[512]{0:T(512)}, u32[]{:S(2)}) copy-start(f32[512]{0:T(512)} %copy-done.125) | copy-start | bytes 6148
  740.4 8.2 copy-start.121
  751.4 8.2 copy-start.111
  766.7 7.4 copy-start.138
  766.7 7.4 copy-start.140
  766.7 7.4 copy-start.142
  766.7 7.4 copy-start.144
  766.7 7.4 copy-start.154
  766.8 7.4 copy-start.160
  766.8 7.4 copy-start.166
  766.8 7.4 copy-start.168
  (170 other events, 620.7 us)

commit v2 on v0

v2 whole, which is shorter than its diff:
```python
from functools import partial

import jax
import jax.numpy as jnp
from jax import lax
from jax.experimental import pallas as pl
from jax.experimental.pallas import tpu as pltpu
from jax.sharding import PartitionSpec as P

HD = 64
PAIRS = 8
SEGS = 8
BLOCK = 512
EPSILON = 1e-05
SCALE = 0.125
FILL = -1e30
GELU = 0.7978845608
CUBIC = 0.044715

MESH = pl.DeviceIdType.MESH
ANY = pl.BlockSpec(memory_space=pl.ANY)
VMEM = pl.BlockSpec(memory_space=pltpu.VMEM)
SMEM = pl.BlockSpec(memory_space=pltpu.SMEM)
BOTH = ("batch", "src")
LOW = jnp.bfloat16
WIDE = jnp.float32
LIMIT = 60 << 20


def shape_of(shape, kind):
    return jax.ShapeDtypeStruct(shape, kind)


def dot(left, right):
    return jnp.dot(left, right, preferred_element_type=WIDE)


def dot_tn(left, right):
    return lax.dot_general(left, right, (((0,), (0,)), ((), ())), preferred_element_type=WIDE)


def dot_nt(left, right):
    return lax.dot_general(left, right, (((1,), (1,)), ((), ())), preferred_element_type=WIDE)


def normalised(v):
    centred = v - jnp.mean(v, axis=-1, keepdims=True)
    r = lax.rsqrt(jnp.mean(centred * centred, axis=-1, keepdims=True) + EPSILON)
    return centred * r, r


def norm_back(v, gain, upstream):
    hat, r = normalised(v)
    scaled = upstream * gain
    first = jnp.mean(scaled, axis=-1, keepdims=True)
    second = jnp.mean(scaled * hat, axis=-1, keepdims=True)
    grad_gain = jnp.sum(upstream * hat, axis=0, keepdims=True)
    grad_bias = jnp.sum(upstream, axis=0, keepdims=True)
    return r * (scaled - first - hat * second), grad_gain, grad_bias


def lanes(shape):
    return lax.broadcasted_iota(jnp.int32, shape, len(shape) - 1)


def rows_of(shape):
    return lax.broadcasted_iota(jnp.int32, shape, len(shape) - 2)


def both_heads(x):
    low = lanes(x.shape) < HD
    zero = jnp.zeros_like(x)
    return jnp.concatenate([jnp.where(low, x, zero), jnp.where(low, zero, x)], axis=0)


def join_heads(x):
    half = x.shape[0] // 2
    return jnp.where(lanes((half, x.shape[1])) < HD, x[:half], x[half:])


def twice(x):
    return jnp.concatenate([x, x], axis=0)


def transposed_rows(rows):
    count, width = rows.shape
    return jnp.concatenate([rows, jnp.zeros((128 - count, width), WIDE)], axis=0).T


def greet(peers):
    barrier = pltpu.get_barrier_semaphore()
    for peer in peers:
        pl.semaphore_signal(barrier, inc=1, device_id=peer, device_id_type=MESH)
    pl.semaphore_wait(barrier, len(peers))


def remote(src, dst, send, recv, peer):
    return pltpu.make_async_remote_copy(
        src_ref=src,
        dst_ref=dst,
        send_sem=send,
        recv_sem=recv,
        device_id=peer,
        device_id_type=MESH,
    )


class Place:
    def __init__(self, depth):
        b = lax.axis_index("batch")
        self.depth = depth
        self.y = lax.axis_index("src")
        self.c = lax.rem(b, 2)
        self.x = lax.rem(b // 2, 2)
        self.z = b // 4

    def at(self, z=None, x=None, c=None, y=None):
        z = self.z if z is None else z
        x = self.x if x is None else x
        c = self.c if c is None else c
        y = self.y if y is None else y
        return ((z * 2 + x) * 2 + c, y)

    def along(self, k):
        return self.at(z=lax.rem(self.z + k, self.depth))

    def others(self):
        return [self.along(k) for k in range(1, self.depth)]

    def across_x(self):
        return self.at(x=1 - self.x)

    def across_y(self):
        return self.at(y=1 - self.y)

    def across_both(self):
        return self.at(x=1 - self.x, y=1 - self.y)

    def across_core(self):
        return self.at(c=1 - self.c)


def gather_steps(me, chunks, send, recv):
    z, x, c, y = me.z, me.x, me.c, me.y
    depth = me.depth
    count = len(chunks)
    started = [[None] * 4 for _ in chunks]
    used = [0] * count

    def launch(k, stage):
        copies = []

        def push(block, peer):
            slot = used[k]
            used[k] += 1
            copy = remote(block, block, send.at[k, slot], recv.at[k, slot], peer)
            copy.start()
            copies.append(copy)

        one, two = chunks[k]
        every = slice(None)
        if stage == 0:
            for view in one + two:
                for j in range(1, depth):
                    push(view(z, x, c, y), me.along(j))
        elif stage == 1:
            for view in one:
                push(view(every, x, c, y), me.across_x())
            for view in two:
                push(view(every, x, c, y), me.across_y())
        elif stage == 2:
            for view in one:
                push(view(every, every, c, y), me.across_y())
            for view in two:
                push(view(every, x, c, every), me.across_x())
        else:
            for view in one + two:
                push(view(every, every, c, every), me.across_core())
        started[k][stage] = copies

    for step in range(count + 4):
        for stage in range(4, -1, -1):
            k = step - stage
            if not 0 <= k < count:
                continue
            if stage > 0:
                for copy in started[k][stage - 1]:
                    copy.wait_recv()
            if stage < 4:
                launch(k, stage)
        yield step - 4
    for stages in started:
        for copies in stages:
            for copy in copies:
                copy.wait_send()


def self_window(block, tok_count):
    low = jnp.clip(block * 128 - 128, 0, tok_count - 384)
    return pl.multiple_of(low, 128)


def self_mask(row_seg, row_keep, col_seg, block, low):
    at = pl.ds(low, 384)
    keys = row_seg[0:1, at]
    keep = row_keep[0:1, at]
    queries = col_seg[pl.ds(pl.multiple_of(block * 128, 128), 128), 0:1]
    shape = (128, 384)
    own = (rows_of(shape) + block * 128) == (lanes(shape) + low)
    return (queries == keys) & ((keep > 0.5) | own)


def self_forward(qkv, out, lse_ref, row_seg, row_keep, col_seg):
    tok_count, width = out.shape
    blocks = tok_count // 128
    lse_ref[...] = jnp.zeros_like(lse_ref)

    def one(t, carry):
        pair, block = t // blocks, lax.rem(t, blocks)
        at = pl.ds(pl.multiple_of(block * 128, 128), 128)
        low = self_window(block, tok_count)
        keys = pl.ds(low, 384)
        base = pl.multiple_of(pair * 128, 128)
        q = both_heads(qkv[at, pl.ds(base, 128)])
        k = qkv[keys, pl.ds(pl.multiple_of(base + width, 128), 128)]
        v = qkv[keys, pl.ds(pl.multiple_of(base + 2 * width, 128), 128)]
        allowed = self_mask(row_seg, row_keep, col_seg, block, low)
        scores = jnp.where(twice(allowed), dot_nt(q, k) * SCALE, FILL)
        top = jnp.max(scores, axis=1, keepdims=True)
        exps = jnp.exp(scores - top)
        total = jnp.sum(exps, axis=1, keepdims=True)
        probs = (exps * (1.0 / total)).astype(LOW)
        out[at, pl.ds(base, 128)] = join_heads(dot(probs, v)).astype(LOW)
        lse = top + jnp.log(total)
        lane = lanes((128, 128))
        lse_ref[at, :] = jnp.where(
            lane == 2 * pair, lse[:128], jnp.where(lane == 2 * pair + 1, lse[128:], lse_ref[at, :])
        )
        return carry

    lax.fori_loop(0, blocks * (width // 128), one, 0)


def first_kernel(depth, gathers, *refs):
    (seg, pad, pair, dec, enc, small, raw_qkv, raw_so, raw_cq, raw_kv, raw_co, raw_fi, raw_fo, raw_in) = refs[:14]
    refs = refs[14:]
    if gathers:
        (ga, gf, gi, gs) = refs[:4]
        refs = refs[4:]
    else:
        ga, gf, gi, gs = None, None, None, None
        (ga_in, gs_in) = refs[:2]
        refs = refs[2:]
    (start_out, one_out, qkv_out, low_out, lse_out, after_out, two_out, query_out, other_out, kv_out) = refs[:10]
    (w_qkv, w_so, w_cq, w_kv, w_s, row_seg, row_keep, col_seg, own_sem, load_sem, send, recv) = refs[10:]
    tok_count, width = dec.shape
    src_count = enc.shape[0]
    me = Place(depth)
    z, x, c, y = me.z, me.x, me.c, me.y

    if gathers:
        owns = []

        def own(src, dst):
            copy = pltpu.make_async_copy(src, dst, own_sem.at[len(owns)])
            copy.start()
            owns.append(copy)

        own(small, gs.at[z, x, c, y])
        first = 0
        for raw, count in ((raw_qkv, 3), (raw_so, 1), (raw_cq, 1), (raw_kv, 2), (raw_co, 1), (raw_fi, 4)):
            for k in range(count):
                own(raw.at[:, pl.ds(k * BLOCK, BLOCK)], ga.at[first + k, z, x, c, y])
            first += count
        own(raw_fo, gf.at[z, x, c, y])
        own(raw_in, gi.at[z, x, c, y])
        greet(me.others() + [me.across_x(), me.across_y(), me.across_core()])
        for copy in owns:
            copy.wait()

        def piece(lo, hi):
            return lambda *at: ga.at[(slice(lo, hi),) + at]

        def part(ref, lo, hi):
            return lambda *at: ref.at[at + (pl.ds(lo, hi - lo),)]

        half_f, half_i = raw_fo.shape[0] // 2, raw_in.shape[0] // 2
        chunks = [
            ([part(gs, 0, 16), piece(0, 2)], [piece(2, 4)]),
            ([piece(4, 6)], [piece(6, 8)]),
            ([piece(8, 10)], [piece(10, 12)]),
            (
                [part(gf, 0, half_f), part(gi, 0, half_i)],
                [part(gf, half_f, 2 * half_f), part(gi, half_i, 2 * half_i)],
            ),
        ]
        steps = gather_steps(me, chunks, send, recv)
    else:
        greet([me.across_y()])
        steps = iter(())

    def advance():
        return next(steps, None)

    def have(chunk):
        if gathers:
            while True:
                done = advance()
                if done is None or done >= chunk:
                    return

    loads = []

    def load(src, dst):
        copy = pltpu.make_async_copy(src, dst, load_sem.at[len(loads)])
        copy.start()
        loads.append(copy)
        return copy

    def fetch(lo, hi, dst):
        if gathers:
            return load(ga.at[lo:hi], dst)
        return load(ga_in.at[lo:hi], dst)

    segments = seg[...].astype(WIDE)
    row_seg[...] = segments
    row_keep[...] = 1.0 - pad[...].astype(WIDE)
    pair_row = jnp.zeros((1, tok_count), WIDE)
    for k in range(SEGS):
        pair_row = jnp.where(segments == k, pair[0, k].astype(WIDE), pair_row)
    columns = transposed_rows(jnp.concatenate([segments, pair_row, jnp.zeros((6, tok_count), WIDE)], axis=0))
    col_seg[...] = columns

    def flat(ref):
        value = ref[...]
        return value.reshape((-1, value.shape[-1]))

    have(0)
    copies = [load(gs if gathers else gs_in, w_s), fetch(0, 3, w_qkv), fetch(3, 4, w_so)]
    for copy in copies:
        copy.wait()
    table = flat(w_s).astype(WIDE).T
    onehot = (lanes((tok_count, 128)) == (columns[:, 1:2].astype(jnp.int32) + 8)).astype(LOW)
    start = dec[...].astype(WIDE) + dot(onehot, table.astype(LOW))
    start_out[...] = start
    one = (normalised(start)[0] * table[0:1] + table[4:5]).astype(LOW)
    one_out[...] = one
    for k in range(3):
        weight = w_qkv[k].reshape((-1, BLOCK))
        qkv_out[:, pl.ds(k * BLOCK, BLOCK)] = dot(one, weight).astype(LOW)
    advance()
    self_forward(qkv_out, low_out, lse_out, row_seg, row_keep, col_seg)
    have(1)
    copies = [fetch(4, 5, w_cq), fetch(5, 7, w_kv)]
    after = start_out[...] + dot(low_out[...], flat(w_so))
    after_out[...] = after
    two = (normalised(after)[0] * table[1:2] + table[5:6]).astype(LOW)
    two_out[...] = two
    for copy in copies:
        copy.wait()
    query_out[...] = dot(two, flat(w_cq)).astype(LOW)
    swap = remote(query_out, other_out, send.at[len(chunks) if gathers else 0, 0], recv.at[len(chunks) if gathers else 0, 0], me.across_y())
    swap.start()
    advance()
    w_key, w_val = w_kv[0].reshape((-1, BLOCK)), w_kv[1].reshape((-1, BLOCK))
    parts = 4
    for k in range(parts):
        span = src_count // parts
        at = pl.ds(k * span, span)
        kv_out[at, 0:width] = dot(enc[at, :], w_key).astype(LOW)
        kv_out[at, width : 2 * width] = dot(enc[at, :], w_val).astype(LOW)
        advance()
    for _ in steps:
        pass
    swap.wait()


def first_part(depth, gathers, seg, pad, pair, dec, enc, small, raw, whole):
    tok_count, width = dec.shape
    src_count = enc.shape[0]
    sharded = (depth, 2, 2, 2)
    rows = BLOCK // (depth * 8)
    lead = sharded + (rows,) if gathers else (BLOCK,)
    outs = []
    if gathers:
        outs = [
            (shape_of((12,) + sharded + (rows, BLOCK), LOW), ANY),
            (shape_of(sharded + raw[6].shape, LOW), ANY),
            (shape_of(sharded + raw[7].shape, LOW), ANY),
            (shape_of(sharded + small.shape, LOW), ANY),
        ]
    local = [
        (shape_of((tok_count, width), WIDE), VMEM),
        (shape_of((tok_count, width), LOW), VMEM),
        (shape_of((tok_count, 3 * width), LOW), VMEM),
        (shape_of((tok_count, width), LOW), VMEM),
        (shape_of((tok_count, 128), WIDE), VMEM),
        (shape_of((tok_count, width), WIDE), VMEM),
        (shape_of((tok_count, width), LOW), VMEM),
        (shape_of((tok_count, width), LOW), VMEM),
        (shape_of((tok_count, width), LOW), ANY),
        (shape_of((src_count, 2 * width), LOW), VMEM),
    ]
    outs += local
    extra = [] if gathers else [whole[0], whole[3]]
    res = pl.pallas_call(
        partial(first_kernel, depth, gathers),
        name="first_part",
        out_shape=[o for o, _ in outs],
        in_specs=[VMEM, VMEM, SMEM, VMEM, VMEM] + [ANY] * (9 + len(extra)),
        out_specs=[s for _, s in outs],
        scratch_shapes=[
            pltpu.VMEM((3,) + lead + (BLOCK,), LOW),
            pltpu.VMEM((1,) + lead + (BLOCK,), LOW),
            pltpu.VMEM((1,) + lead + (BLOCK,), LOW),
            pltpu.VMEM((2,) + lead + (BLOCK,), LOW),
            pltpu.VMEM((lead if gathers else (BLOCK,)) + (128,), LOW),
            pltpu.VMEM((1, tok_count), WIDE),
            pltpu.VMEM((1, tok_count), WIDE),
            pltpu.VMEM((tok_count, 128), WIDE),
            pltpu.SemaphoreType.DMA((16,)),
            pltpu.SemaphoreType.DMA((8,)),
            pltpu.SemaphoreType.DMA((5, 4 * (depth + 2))),
            pltpu.SemaphoreType.DMA((5, 4 * (depth + 2))),
        ],
        compiler_params=pltpu.CompilerParams(
            collective_id=0, has_side_effects=True, vmem_limit_bytes=LIMIT
        ),
    )(seg, pad, pair, dec, enc, small, *raw, *extra)
    if gathers:
        ga, gf, gi, gs = res[:4]
        whole = (
            ga.reshape((12, BLOCK, BLOCK)),
            gf.reshape((-1, BLOCK)),
            gi.reshape((-1, raw[7].shape[1])),
            gs.reshape((-1, 128)),
        )
        res = res[4:]
    return whole, res


def block_ranges(seg_s, ends_s, off, src_count, side, block, tile):
    at = pl.multiple_of(block * 128, 128)
    low_seg = seg_s[side, at]
    high_seg = seg_s[side, at + 127]
    low = jnp.clip(ends_s[low_seg] - off, 0, src_count)
    high = jnp.clip(ends_s[high_seg + 1] - off, 0, src_count)
    return low // tile, jnp.where(high > low, (high + tile - 1) // tile, low // tile)


def bounds_columns(ends_s, seg_col, off):
    low = jnp.zeros_like(seg_col)
    high = jnp.zeros_like(seg_col)
    for s in range(2 * SEGS):
        low = jnp.where(seg_col == s, ends_s[s] - off, low)
        high = jnp.where(seg_col == s, ends_s[s + 1] - off, high)
    return low, high


TILE = 256


def cross_forward_kernel(seg_s, ends_s, seg_cols, q_own, q_other, kv, o_own, o_other, lse_own, lse_other, top_ref, total_ref, acc_ref):
    tok_count, width = q_own.shape
    src_count = kv.shape[0]
    pairs = width // 128
    off = lax.axis_index("src") * src_count
    for side, (q, o, lse_ref) in enumerate(((q_own, o_own, lse_own), (q_other, o_other, lse_other))):

        @pl.loop(0, tok_count // 128)
        def _(block):
            at = pl.ds(pl.multiple_of(block * 128, 128), 128)
            first, last = block_ranges(seg_s, ends_s, off, src_count, side, block, TILE)
            low, high = bounds_columns(ends_s, seg_cols[at, side : side + 1], off)
            top_ref[...] = jnp.full_like(top_ref, FILL)
            total_ref[...] = jnp.zeros_like(total_ref)
            acc_ref[...] = jnp.zeros_like(acc_ref)

            def one(t, carry):
                base = pl.multiple_of(t * TILE, TILE)
                keys = pl.ds(base, TILE)
                index = lanes((128, TILE)) + base
                allowed = twice((index >= low) & (index < high))
                for p in range(pairs):
                    cols = pl.ds(p * 128, 128)
                    k = kv[keys, cols]
                    v = kv[keys, pl.ds(width + p * 128, 128)]
                    scores = dot_nt(both_heads(q[at, cols]), k) * SCALE
                    scores = jnp.where(allowed, scores, FILL)
                    old = top_ref[p]
                    top = jnp.maximum(old, jnp.max(scores, axis=1, keepdims=True))
                    exps = jnp.where(allowed, jnp.exp(scores - top[:, 0:1]), 0.0)
                    fade = jnp.exp(old - top)
                    top_ref[p] = top
                    total_ref[p] = total_ref[p] * fade + jnp.sum(exps, axis=1, keepdims=True)
                    acc_ref[p] = acc_ref[p] * fade + dot(exps.astype(LOW), v)
                return carry

            lax.fori_loop(first, last, one, 0)
            lane = lanes((128, 128))
            stats = jnp.zeros((128, 128), WIDE)
            for p in range(pairs):
                total = total_ref[p]
                safe = jnp.where(total > 0.0, total, 1.0)
                o[at, pl.ds(p * 128, 128)] = join_heads(acc_ref[p] / safe).astype(LOW)
                lse = jnp.where(total > 0.0, top_ref[p] + jnp.log(safe), FILL)
                stats = jnp.where(lane == 2 * p, lse[:128], jnp.where(lane == 2 * p + 1, lse[128:], stats))
            lse_ref[:, at] = stats.T[0:8]


def cross_forward(seg_s, ends_s, seg_cols, q_own, q_other, kv):
    tok_count, width = q_own.shape
    heads = width // HD
    out = shape_of((tok_count, width), LOW)
    lse = shape_of((heads, tok_count), WIDE)
    return pl.pallas_call(
        cross_forward_kernel,
        name="cross_forward",
        out_shape=[out, out, lse, lse],
        in_specs=[SMEM, SMEM, VMEM, VMEM, VMEM, VMEM],
        out_specs=[VMEM] * 4,
        scratch_shapes=[pltpu.VMEM((width // 128, 256, 128), WIDE)] * 3,
        compiler_params=pltpu.CompilerParams(vmem_limit_bytes=LIMIT),
    )(seg_s, ends_s, seg_cols, q_own, q_other, kv)


def cross_backward_kernel(
    seg_s, ends_s, seg_cols, q_own, q_other, g_own, g_other, st_own, st_other, kv, dq_own, dq_other, dkv, acc, col_ref, dq_acc
):
    tok_count, width = q_own.shape
    src_count = kv.shape[0]
    pairs = width // 128
    off = lax.axis_index("src") * src_count
    acc[...] = jnp.zeros_like(acc)
    sides = ((q_own, g_own, st_own, dq_own), (q_other, g_other, st_other, dq_other))
    for side, (q, g, st, dq) in enumerate(sides):

        @pl.loop(0, tok_count // 128)
        def _(block):
            at = pl.ds(pl.multiple_of(block * 128, 128), 128)
            first, last = block_ranges(seg_s, ends_s, off, src_count, side, block, TILE)
            low, high = bounds_columns(ends_s, seg_cols[at, side : side + 1], off)
            dq_acc[...] = jnp.zeros_like(dq_acc)
            col_ref[...] = jnp.concatenate([st[:, at], jnp.zeros((112, 128), WIDE)], axis=0).T

            def one(t, carry):
                base = pl.multiple_of(t * TILE, TILE)
                keys = pl.ds(base, TILE)
                index = lanes((128, TILE)) + base
                allowed = twice((index >= low) & (index < high))
                for p in range(pairs):
                    cols = pl.ds(p * 128, 128)
                    vals = pl.ds(width + p * 128, 128)
                    k = kv[keys, cols]
                    v = kv[keys, vals]
                    qs = both_heads(q[at, cols])
                    gs = both_heads(g[at, cols])
                    lse = jnp.concatenate([col_ref[:, 2 * p : 2 * p + 1], col_ref[:, 2 * p + 1 : 2 * p + 2]], axis=0)
                    delta = jnp.concatenate(
                        [col_ref[:, 8 + 2 * p : 9 + 2 * p], col_ref[:, 9 + 2 * p : 10 + 2 * p]], axis=0
                    )
                    scores = dot_nt(qs, k) * SCALE
                    probs = jnp.exp(jnp.where(allowed, scores - lse, FILL))
                    gscores = (probs * (dot_nt(gs, v) - delta)).astype(LOW)
                    dq_acc[:, cols] = dq_acc[:, cols] + join_heads(dot(gscores, k))
                    acc[keys, cols] = acc[keys, cols] + dot_tn(gscores, qs)
                    acc[keys, vals] = acc[keys, vals] + dot_tn(probs.astype(LOW), gs)
                return carry

            lax.fori_loop(first, last, one, 0)
            dq[at, :] = (dq_acc[...] * SCALE).astype(dq.dtype)

    @pl.loop(0, src_count // 256)
    def _(t):
        at = pl.ds(pl.multiple_of(t * 256, 256), 256)
        dkv[at, 0:width] = (acc[at, 0:width] * SCALE).astype(LOW)
        dkv[at, width : 2 * width] = acc[at, width : 2 * width].astype(LOW)


def cross_backward(seg_s, ends_s, seg_cols, q_own, q_other, g_own, g_other, st_own, st_other, kv):
    tok_count, width = q_own.shape
    src_count = kv.shape[0]
    return pl.pallas_call(
        cross_backward_kernel,
        name="cross_backward",
        out_shape=[
            shape_of((tok_count, width), WIDE),
            shape_of((tok_count, width), LOW),
            shape_of((src_count, 2 * width), LOW),
        ],
        in_specs=[SMEM, SMEM] + [VMEM] * 8,
        out_specs=[VMEM] * 3,
        scratch_shapes=[
            pltpu.VMEM((src_count, 2 * width), WIDE),
            pltpu.VMEM((128, 128), WIDE),
            pltpu.VMEM((128, width), WIDE),
        ],
        compiler_params=pltpu.CompilerParams(vmem_limit_bytes=LIMIT),
    )(seg_s, ends_s, seg_cols, q_own, q_other, g_own, g_other, st_own, st_other, kv)


def merge_all(parts):
    top = parts[0][0:1]
    for part in parts[1:]:
        top = jnp.maximum(top, part[0:1])
    total = sum(jnp.exp(part[0:1] - top) for part in parts)
    rest = sum(part for part in parts)
    return jnp.where(rows_of(rest.shape) == 0, top + jnp.log(total), rest)


def middle_kernel(depth, natural, *refs):
    (
        seg, pad, labels, counts, positions, targets, w_vocab, after_self, o_own, o_other, lse_own, lse_other,
        ga, gf, gi, gs,
    ) = refs[:16]
    refs = refs[16:]
    (
        block_out, state_out, g_own, g_other, st_own, st_other, gw_a, gw_f, gw_i, small_rows, small_cols,
        grad_vocab, token_out, loss_out,
    ) = refs[:14]
    (
        w_co, w_fi, w_fo, w_in, w_s, got_o, got_lse, cross_o, cross_low, ac, bs, n3, act, slope, gpre, head,
        lt, gt, pb, rb, got_rc, got_rq, got_rz, st_c, st_q, st_z, gh, load_sem, send, recv,
    ) = refs[14:]
    tok_count, width = after_self.shape
    hidden = act.shape[1]
    masked = positions.shape[0]
    vocab_local = w_vocab.shape[0]
    everyone = depth * 8
    me = Place(depth)
    z, x, c, y = me.z, me.x, me.c, me.y
    greet(me.others() + [me.across_x(), me.across_y(), me.across_both(), me.across_core()])
    used = [0]

    def push(src, dst, peer):
        k = used[0]
        used[0] += 1
        copy = remote(src, dst, send.at[k], recv.at[k], peer)
        copy.start()
        return copy

    pending = []

    def arrive(copies):
        for copy in copies:
            copy.wait_recv()
        pending.extend(copies)

    swap = [push(o_other, got_o, me.across_y()), push(lse_other, got_lse, me.across_y())]
    sources = ((ga.at[7:8], w_co), (ga.at[8:12], w_fi), (gf, w_fo), (gi, w_in), (gs, w_s))
    loads = []
    for k, (src, dst) in enumerate(sources):
        copy = pltpu.make_async_copy(src, dst, load_sem.at[k])
        copy.start()
        loads.append(copy)

    segments = seg[...].astype(WIDE)
    keep = 1.0 - pad[...].astype(WIDE)
    lane_row = lanes((1, tok_count))
    inside = lane_row < tok_count - 1

    def following(row):
        return pltpu.roll(jnp.concatenate([row, jnp.zeros((7, tok_count), WIDE)], axis=0), tok_count - 1, 1)[0:1]

    follows = inside & (following(segments) == segments) & (keep > 0.5) & (following(keep) > 0.5)
    valid = jnp.where(follows, 1.0, 0.0)
    rows = [keep, valid, labels[...].astype(WIDE), counts[...].astype(WIDE)]
    columns = transposed_rows(jnp.concatenate(rows + [jnp.zeros((4, tok_count), WIDE)], axis=0))
    col_keep, col_valid = columns[:, 0:1], columns[:, 1:2]
    col_label, col_count = columns[:, 2:3], columns[:, 3:4].astype(jnp.int32)

    for copy in loads:
        copy.wait()
    table = w_s[...].reshape((-1, 128)).astype(WIDE).T

    arrive(swap)
    top = jnp.maximum(lse_own[...], got_lse[...])
    lse = top + jnp.log(jnp.exp(lse_own[...] - top) + jnp.exp(got_lse[...] - top))
    shares = jnp.concatenate([jnp.exp(lse_own[...] - lse), jnp.exp(got_lse[...] - lse)], axis=0)
    shares = transposed_rows(shares)
    low_half = lanes((tok_count, 128)) < HD
    for p in range(width // 128):
        at = slice(p * 128, (p + 1) * 128)
        share_own = jnp.where(low_half, shares[:, 2 * p : 2 * p + 1], shares[:, 2 * p + 1 : 2 * p + 2])
        share_got = jnp.where(low_half, shares[:, 8 + 2 * p : 9 + 2 * p], shares[:, 9 + 2 * p : 10 + 2 * p])
        mixed = o_own[:, at].astype(WIDE) * share_own + got_o[:, at].astype(WIDE) * share_got
        cross_o[:, at] = mixed
        cross_low[:, at] = mixed.astype(LOW)
    weight_co = w_co[...].reshape((-1, BLOCK))
    after_cross = after_self[...] + dot(cross_low[...], weight_co)
    ac[...] = after_cross
    n3[...] = (normalised(after_cross)[0] * table[2:3] + table[6:7]).astype(LOW)
    bs[...] = after_cross
    blocks = hidden // BLOCK
    flat_fo = w_fo[...].reshape((-1, BLOCK))
    for j in range(blocks):
        at = slice(j * BLOCK, (j + 1) * BLOCK)
        pre = dot(n3[...], w_fi[j].reshape((-1, BLOCK)))
        square = pre * pre
        bent = jnp.tanh(GELU * pre * (1.0 + CUBIC * square))
        half = 0.5 * (1.0 + bent)
        act[:, at] = (pre * half).astype(LOW)
        slope[:, at] = half + 0.5 * pre * (1.0 - bent * bent) * (GELU * (1.0 + 3.0 * CUBIC * square))
        bs[...] = bs[...] + dot(act[:, at], flat_fo[at])
    state = bs[...]
    block_out[...] = state.astype(LOW)
    head_in = (normalised(state)[0] * table[3:4] + table[7:8]).astype(LOW)
    head[...] = head_in

    chosen_rows = positions[...] == lanes((masked, tok_count))
    picker = chosen_rows.astype(LOW)
    picked = dot(picker, head_in).astype(LOW)
    kept = jnp.sum(jnp.where(chosen_rows, keep, 0.0), axis=1, keepdims=True)
    code = jnp.where(kept > 0.5, targets[...] + 1, 0)
    lane = lanes((masked, 128))
    digits = jnp.where(lane == 0, code >> 8, jnp.where(lane == 1, code & 255, 0)).astype(WIDE).astype(LOW)
    pb[z, x, c, y, :, 0:width] = picked
    pb[z, x, c, y, :, width : width + 128] = digits
    mine = pb.at[z, x, c, y]
    flight = [push(mine, mine, peer) for peer in me.others()]

    flat_in = w_in[...].reshape((2 * width, -1))
    classes = flat_in.shape[1]
    w_one, w_two = flat_in[:width], flat_in[width:]
    token_row = rows_of((tok_count, classes))
    ahead = pltpu.roll(dot(head_in, w_two), tok_count - 1, 0)
    logits = dot(head_in, w_one) + jnp.where(token_row == tok_count - 1, 0.0, ahead)
    top = jnp.max(logits, axis=1, keepdims=True)
    exps = jnp.exp(logits - top)
    total = jnp.sum(exps, axis=1, keepdims=True)
    hits = lanes((tok_count, classes)) == col_count
    entropy = top + jnp.log(total) - jnp.sum(jnp.where(hits, logits, 0.0), axis=1, keepdims=True)
    loss_col = col_valid * entropy
    grads = col_valid * (exps * (1.0 / total) - jnp.where(hits, 1.0, 0.0))
    g_insert = grads.astype(LOW)
    before = pltpu.roll(g_insert.astype(WIDE), 1, 0)
    g_before = jnp.where(token_row == 0, 0.0, before).astype(LOW)

    arrive(flight)
    column = pb.at[:, x, c, y]
    flight = [push(column, column, peer) for peer in (me.across_x(), me.across_y(), me.across_both())]

    flat_s = w_s[...].reshape((-1, 128))
    two = dot(head_in, flat_s)
    l_zero, l_one = two[:, 16:17], two[:, 17:18]
    top = jnp.maximum(l_zero, l_one)
    e_zero, e_one = jnp.exp(l_zero - top), jnp.exp(l_one - top)
    total = e_zero + e_one
    is_one = col_label > 0.5
    loss_col = loss_col + col_keep * (top + jnp.log(total) - jnp.where(is_one, l_one, l_zero))
    d_zero = col_keep * (e_zero / total - jnp.where(is_one, 0.0, 1.0))
    d_one = col_keep * (e_one / total - jnp.where(is_one, 1.0, 0.0))
    lane = lanes((tok_count, 128))
    g_delete = jnp.where(lane == 16, d_zero, jnp.where(lane == 17, d_one, 0.0)).astype(LOW)
    gh[...] = dot_nt(g_delete, flat_s) + dot_nt(g_insert, w_one) + dot_nt(g_before, w_two)
    arrive(flight)
    plane = pb.at[:, :, c, :]
    flight = [push(plane, plane, me.across_core())]
    small_cols[...] = dot_tn(head_in, g_delete)
    gw_i[0:width] = dot_tn(head_in, g_insert).astype(LOW)
    gw_i[width : 2 * width] = dot_tn(head_in, g_before).astype(LOW)
    arrive(flight)

    gathered = pb[...].reshape((-1, width + 128))
    rows_all = gathered[:, 0:width]
    numbers = gathered[:, width : width + 128].astype(WIDE).T
    code = numbers[0:1] * 256.0 + numbers[1:2]
    weight = jnp.where(code > 0.5, 1.0, 0.0)
    count = rows_all.shape[0]
    pos = lax.axis_index(BOTH)
    place = rows_of((vocab_local, count)) + pos * vocab_local
    hits = place == (code.astype(jnp.int32) - 1)
    lt[...] = dot_nt(w_vocab[...], rows_all)
    logits = lt[...]
    top = jnp.max(logits, axis=0, keepdims=True)
    total = jnp.sum(jnp.exp(logits - top), axis=0, keepdims=True)
    chosen = jnp.sum(jnp.where(hits, logits, 0.0), axis=0, keepdims=True)
    loss_here = jnp.sum(loss_col, axis=0, keepdims=True)
    stat = jnp.concatenate(
        [top + jnp.log(total), chosen, jnp.broadcast_to(loss_here, (1, count)), jnp.zeros((5, count), WIDE)], axis=0
    )
    st_c[0] = stat
    flight = [push(st_c.at[0], st_c.at[1], me.across_core())]
    arrive(flight)
    st_q[x, y] = merge_all([st_c[0], st_c[1]])
    spot = st_q.at[x, y]
    flight = [push(spot, spot, peer) for peer in (me.across_x(), me.across_y(), me.across_both())]
    arrive(flight)
    st_z[z] = merge_all([st_q[0, 0], st_q[0, 1], st_q[1, 0], st_q[1, 1]])
    flight = [push(st_z.at[z], st_z.at[z], peer) for peer in me.others()]
    arrive(flight)
    stat = merge_all([st_z[k] for k in range(depth)])
    tokens = weight * (stat[0:1] - stat[1:2])
    token_out[...] = jnp.broadcast_to(tokens, (8, count))
    loss = (stat[2:3, 0:128] + jnp.sum(tokens, axis=1, keepdims=True)) * (1.0 / (tok_count * everyone))
    loss_out[...] = jnp.broadcast_to(loss, (8, 128))
    gt[...] = (weight * (jnp.exp(lt[...] - stat[0:1]) - jnp.where(hits, 1.0, 0.0))).astype(LOW)

    rb[...] = dot_tn(gt[...], w_vocab[...]).astype(LOW).reshape(rb.shape)
    flight = [push(rb.at[:, :, 1 - c], got_rc, me.across_core())]
    scale = (tok_count * everyone) ** (-0.5)
    grad_vocab[...] = dot(gt[...], rows_all) * scale
    arrive(flight)
    got_rc[...] = (rb[:, :, c].astype(WIDE) + got_rc[...].astype(WIDE)).astype(LOW)
    flight = [
        push(got_rc.at[:, 1 - x, y], got_rq.at[0], me.across_x()),
        push(got_rc.at[:, x, 1 - y], got_rq.at[1], me.across_y()),
        push(got_rc.at[:, 1 - x, 1 - y], got_rq.at[2], me.across_both()),
    ]
    arrive(flight)
    line = got_rc[:, x, y].astype(WIDE)
    for k in range(3):
        line = line + got_rq[k].astype(WIDE)
    got_rq[3] = line.astype(LOW)
    flight = [
        push(got_rq.at[3, lax.rem(z + k, depth)], got_rz.at[k - 1], me.along(k)) for k in range(1, depth)
    ]
    arrive(flight)
    grad_picked = got_rq[3, z].astype(WIDE)
    for k in range(1, depth):
        grad_picked = grad_picked + got_rz[k - 1].astype(WIDE)
    coarse = grad_picked.astype(LOW)
    fine = (grad_picked - coarse.astype(WIDE)).astype(LOW)
    grad_head = gh[...] + dot_tn(picker, coarse) + dot_tn(picker, fine)

    grad_block, gain_3, bias_3 = norm_back(bs[...], table[3:4], grad_head)
    bs[...] = grad_block
    g_ffn = grad_block.astype(LOW)
    gh[...] = jnp.zeros_like(gh)
    for j in range(blocks):
        at = slice(j * BLOCK, (j + 1) * BLOCK)
        gpre[:, at] = (dot_nt(g_ffn, flat_fo[at]) * slope[:, at]).astype(LOW)
        gh[...] = gh[...] + dot_nt(gpre[:, at], w_fi[j].reshape((-1, BLOCK)))
    back, gain_2, bias_2 = norm_back(ac[...], table[2:3], gh[...])
    grad_state = grad_block + back
    state_out[...] = grad_state
    g_cross = grad_state.astype(LOW)
    g_attn = dot_nt(g_cross, weight_co).astype(LOW)
    g_own[...] = g_attn
    deltas = jnp.zeros((tok_count, 128), WIDE)
    for p in range(width // 128):
        at = slice(p * 128, (p + 1) * 128)
        product = g_attn[:, at].astype(WIDE) * cross_o[:, at]
        first = jnp.sum(jnp.where(low_half, product, 0.0), axis=1, keepdims=True)
        second = jnp.sum(jnp.where(low_half, 0.0, product), axis=1, keepdims=True)
        deltas = jnp.where(lane == 2 * p, first, jnp.where(lane == 2 * p + 1, second, deltas))
    st_own[...] = jnp.concatenate([lse, deltas.T[0:8]], axis=0)
    swap = [push(g_own, g_other, me.across_y()), push(st_own, st_other, me.across_y())]

    for j in range(blocks):
        at = slice(j * BLOCK, (j + 1) * BLOCK)
        gw_f[at] = dot_tn(act[:, at], g_ffn).astype(LOW)
        gw_a[1 + j] = dot_tn(n3[...], gpre[:, at]).astype(LOW)
    gw_a[0] = dot_tn(cross_low[...], g_cross).astype(LOW)
    small_rows[...] = jnp.concatenate([gain_2, gain_3, bias_2, bias_3, jnp.zeros((4, width), WIDE)], axis=0)
    arrive(swap)
    for copy in pending:
        copy.wait_send()


def middle_part(depth, seg, pad, labels, counts, positions, targets, w_vocab, after_self, attended, whole):
    tok_count, width = after_self.shape
    ga, gf, gi, gs = whole
    hidden = gf.shape[0]
    vocab_local = w_vocab.shape[0]
    everyone = depth * 8
    masked = positions.shape[0]
    count = masked * everyone
    sharded = (depth, 2, 2, 2)
    outs = [
        (shape_of((tok_count, width), LOW), VMEM),
        (shape_of((tok_count, width), WIDE), VMEM),
        (shape_of((tok_count, width), LOW), VMEM),
        (shape_of((tok_count, width), LOW), ANY),
        (shape_of((16, tok_count), WIDE), VMEM),
        (shape_of((16, tok_count), WIDE), ANY),
        (shape_of((5, BLOCK, BLOCK), LOW), VMEM),
        (shape_of((hidden, width), LOW), VMEM),
        (shape_of(gi.shape, LOW), VMEM),
        (shape_of((8, width), WIDE), VMEM),
        (shape_of((width, 128), WIDE), VMEM),
        (shape_of((vocab_local, width), WIDE), VMEM),
        (shape_of((8, count), WIDE), VMEM),
        (shape_of((8, 128), WIDE), VMEM),
    ]
    copies = 2 + 2 + 2 * (depth - 1) + 3 + 1 + 1 + 3 + 1 + 3 + (depth - 1)
    return pl.pallas_call(
        partial(middle_kernel, depth, None),
        name="middle_part",
        out_shape=[o for o, _ in outs],
        in_specs=[VMEM] * 12 + [ANY] * 4,
        out_specs=[s for _, s in outs],
        scratch_shapes=[
            pltpu.VMEM((1, BLOCK, BLOCK), LOW),
            pltpu.VMEM((4, BLOCK, BLOCK), LOW),
            pltpu.VMEM(gf.shape, LOW),
            pltpu.VMEM(gi.shape, LOW),
            pltpu.VMEM(gs.shape, LOW),
            pltpu.VMEM((tok_count, width), LOW),
            pltpu.VMEM((8, tok_count), WIDE),
            pltpu.VMEM((tok_count, width), WIDE),
            pltpu.VMEM((tok_count, width), LOW),
            pltpu.VMEM((tok_count, width), WIDE),
            pltpu.VMEM((tok_count, width), WIDE),
            pltpu.VMEM((tok_count, width), LOW),
            pltpu.VMEM((tok_count, hidden), LOW),
            pltpu.VMEM((tok_count, hidden), WIDE),
            pltpu.VMEM((tok_count, hidden), LOW),
            pltpu.VMEM((tok_count, width), LOW),
            pltpu.VMEM((vocab_local, count), WIDE),
            pltpu.VMEM((vocab_local, count), LOW),
            pltpu.VMEM(sharded + (masked, width + 128), LOW),
            pltpu.VMEM(sharded + (masked, width), LOW),
            pltpu.VMEM((depth, 2, 2, masked, width), LOW),
            pltpu.VMEM((4, depth, masked, width), LOW),
            pltpu.VMEM((max(depth - 1, 1), masked, width), LOW),
            pltpu.VMEM((2, 8, count), WIDE),
            pltpu.VMEM((2, 2, 8, count), WIDE),
            pltpu.VMEM((depth, 8, count), WIDE),
            pltpu.VMEM((tok_count, width), WIDE),
            pltpu.SemaphoreType.DMA((5,)),
            pltpu.SemaphoreType.DMA((copies + depth,)),
            pltpu.SemaphoreType.DMA((copies + depth,)),
        ],
        compiler_params=pltpu.CompilerParams(
            collective_id=1, has_side_effects=True, vmem_limit_bytes=LIMIT
        ),
    )(seg, pad, labels, counts, positions, targets, w_vocab, after_self, *attended, *whole)


def self_backward(qkv, out, lse_ref, g_ref, dqkv, dk, dv, row_seg, row_keep, col_seg):
    tok_count, width = out.shape
    blocks = tok_count // 128

    def pair_step(pair, carry):
        base = pl.multiple_of(pair * 128, 128)
        cols = pl.ds(base, 128)
        kcols = pl.ds(pl.multiple_of(base + width, 128), 128)
        vcols = pl.ds(pl.multiple_of(base + 2 * width, 128), 128)
        dk[...] = jnp.zeros_like(dk)
        dv[...] = jnp.zeros_like(dv)

        def one(block, inner):
            at = pl.ds(pl.multiple_of(block * 128, 128), 128)
            low = self_window(block, tok_count)
            keys = pl.ds(low, 384)
            q = both_heads(qkv[at, cols])
            k = qkv[keys, kcols]
            v = qkv[keys, vcols]
            g = both_heads(g_ref[at, cols])
            delta = jnp.sum(g.astype(WIDE) * twice(out[at, cols].astype(WIDE)), axis=1, keepdims=True)
            lane = lanes((128, 128))
            stats = lse_ref[at, :]
            lse_low = jnp.sum(jnp.where(lane == 2 * pair, stats, 0.0), axis=1, keepdims=True)
            lse_high = jnp.sum(jnp.where(lane == 2 * pair + 1, stats, 0.0), axis=1, keepdims=True)
            lse = jnp.concatenate([lse_low, lse_high], axis=0)
            allowed = self_mask(row_seg, row_keep, col_seg, block, low)
            scores = dot_nt(q, k) * SCALE
            probs = jnp.exp(jnp.where(twice(allowed), scores - lse, FILL))
            gscores = (probs * (dot_nt(g, v) - delta)).astype(LOW)
            dqkv[at, cols] = (join_heads(dot(gscores, k)) * SCALE).astype(LOW)
            dk[keys, :] = dk[keys, :] + dot_tn(gscores, q)
            dv[keys, :] = dv[keys, :] + dot_tn(probs.astype(LOW), g)
            return inner

        lax.fori_loop(0, blocks, one, 0)
        dqkv[:, kcols] = (dk[...] * SCALE).astype(LOW)
        dqkv[:, vcols] = dv[...].astype(LOW)
        return carry

    lax.fori_loop(0, width // 128, pair_step, 0)


class Part:
    def __init__(self, src, pieces, span, bufs, put):
        self.src, self.pieces, self.bufs, self.put = src, pieces, bufs, put
        self.first, self.at = pieces[0], pl.ds(span[0], span[1] - span[0])


def reduce_steps(me, chunks, send, recv):
    z, x, c, y = me.z, me.x, me.c, me.y
    depth = me.depth
    count = len(chunks)
    started = [[None] * 4 for _ in chunks]
    used = [0] * count
    every = slice(None)

    def launch(k, stage):
        copies = []

        def push(src, dst, peer):
            slot = used[k]
            used[k] += 1
            copy = remote(src, dst, send.at[k, slot], recv.at[k, slot], peer)
            copy.start()
            copies.append(copy)

        for which, parts in enumerate(chunks[k]):
            for part in parts:
                got_c, got_1, got_2, got_z = part.bufs
                lo, hi = part.pieces
                n = slice(lo, hi)
                s = slice(lo - part.shift, hi - part.shift)
                if stage == 0:
                    push(part.src.at[s, :, :, 1 - c, :, part.at], got_c.at[n, :, :, :, part.at], me.across_core())
                elif stage == 1:
                    if which == 0:
                        push(got_c.at[n, :, :, 1 - y, part.at], got_1.at[n, :, :, part.at], me.across_y())
                    else:
                        push(got_c.at[n, :, 1 - x, :, part.at], got_1.at[n, :, :, part.at], me.across_x())
                elif stage == 2:
                    if which == 0:
                        push(got_c.at[n, :, 1 - x, y, part.at], got_2.at[n, :, part.at], me.across_x())
                    else:
                        push(got_c.at[n, :, x, 1 - y, part.at], got_2.at[n, :, part.at], me.across_y())
                else:
                    for j in range(1, depth):
                        push(
                            got_c.at[n, lax.rem(z + j, depth), x, y, part.at],
                            got_z.at[n, j - 1, part.at],
                            me.along(j),
                        )
        started[k][stage] = copies

    def absorb(k, stage):
        for copy in started[k][stage]:
            copy.wait_recv()
        for which, parts in enumerate(chunks[k]):
            for part in parts:
                got_c, got_1, got_2, got_z = part.bufs

                def each(i, carry, part=part, which=which, got_c=got_c, got_1=got_1, got_2=got_2):
                    piece, zz = part.pieces[0] + i // depth, lax.rem(i, depth)
                    at = part.at
                    if stage == 0:
                        for xx in range(2):
                            for yy in range(2):
                                got_c[piece, zz, xx, yy, at] = (
                                    part.src[piece - part.shift, zz, xx, c, yy, at].astype(WIDE)
                                    + got_c[piece, zz, xx, yy, at].astype(WIDE)
                                ).astype(LOW)
                    elif stage == 1:
                        for q in range(2):
                            where = (piece, zz, q, y, at) if which == 0 else (piece, zz, x, q, at)
                            got_c[where] = (
                                got_c[where].astype(WIDE) + got_1[piece, zz, q, at].astype(WIDE)
                            ).astype(LOW)
                    else:
                        where = (piece, zz, x, y, at)
                        got_c[where] = (got_c[where].astype(WIDE) + got_2[piece, zz, at].astype(WIDE)).astype(LOW)
                    return carry

                lo, hi = part.pieces
                if stage < 3:
                    lax.fori_loop(0, (hi - lo) * depth, each, 0)
                else:
                    for piece in range(lo, hi):
                        total = got_c[piece, z, x, y, part.at].astype(WIDE)
                        for j in range(1, depth):
                            total = total + got_z[piece, j - 1, part.at].astype(WIDE)
                        part.put(piece, total)

    for step in range(count + 4):
        for stage in range(4, -1, -1):
            k = step - stage
            if not 0 <= k < count:
                continue
            if stage > 0:
                absorb(k, stage - 1)
            if stage < 4:
                launch(k, stage)
        yield step
    for stages in started:
        for copies in stages:
            for copy in copies:
                copy.wait_send()


def last_kernel(depth, reduces, *refs):
    (
        pair, seg, pad, dq_own, dq_other, dkv, enc, start, one, qkv, low, lse, after, two, gstate,
        gw_a, gw_f, gw_i, small_rows, small_cols, ga, gs,
    ) = refs[:22]
    refs = refs[22:]
    grad_input, grad_enc = refs[:2]
    refs = refs[2:]
    outs = refs[:9] if reduces else refs[:2]
    refs = refs[9:] if reduces else refs[2:]
    (w_qkv, w_so, w_cq, w_kv, w_s, got_dq, g_attn, dqkv, dk, dv, row_seg, row_keep, col_seg, load_sem, sw_send, sw_recv) = refs[:16]
    refs = refs[16:]
    tok_count, width = dq_own.shape
    src_count = enc.shape[0]
    everyone = depth * 8
    me = Place(depth)
    scale = (tok_count * everyone) ** (-0.5)
    if reduces:
        greet(me.others() + [me.across_x(), me.across_y(), me.across_core()])
    else:
        greet([me.across_y()])
    swap = remote(dq_other, got_dq, sw_send.at[0], sw_recv.at[0], me.across_y())
    swap.start()
    loads = []
    sources = ((ga.at[0:3], w_qkv), (ga.at[3:4], w_so), (ga.at[4:5], w_cq), (ga.at[5:7], w_kv), (gs, w_s))
    for k, (src, dst) in enumerate(sources):
        copy = pltpu.make_async_copy(src, dst, load_sem.at[k])
        copy.start()
        loads.append(copy)

    if reduces:
        (late, late_s, c_a, c_f, c_i, c_s, a_1, f_1, i_1, s_1, a_2, f_2, i_2, s_2, a_z, f_z, i_z, s_z, send, recv) = refs
        (o_qkv, o_so, o_cq, o_kv, o_co, o_fi, o_fo, o_in, o_s) = outs
        homes = [(o_qkv, 0), (o_qkv, 1), (o_qkv, 2), (o_so, 0), (o_cq, 0), (o_kv, 0), (o_kv, 1), (o_co, 0)]
        homes += [(o_fi, k) for k in range(4)]

        def put_a(piece, total):
            ref, k = homes[piece]
            ref[:, k * BLOCK : (k + 1) * BLOCK] = total * scale

        bufs_a, bufs_f, bufs_i, bufs_s = (c_a, a_1, a_2, a_z), (c_f, f_1, f_2, f_z), (c_i, i_1, i_2, i_z), (c_s, s_1, s_2, s_z)
        rows = BLOCK // everyone

        def a_part(lo, hi):
            part = Part(late if lo < 7 else gw_a, (lo, hi), (0, rows), bufs_a, put_a)
            part.shift = 0 if lo < 7 else 7
            return part

        def other(src, bufs, span, out):
            def put(piece, total):
                out[pl.ds(span[0], span[1] - span[0])] = total * scale

            part = Part(src, (0, 1), span, bufs, put)
            part.shift = 0
            return part

        half_f, size_i = o_fo.shape[0] // 2, o_in.shape[0]
        chunks = [
            ([a_part(8, 10)], [a_part(10, 12)]),
            ([other(gw_f, bufs_f, (0, half_f), o_fo)], [other(gw_f, bufs_f, (half_f, 2 * half_f), o_fo)]),
            ([a_part(7, 8)], [other(gw_i, bufs_i, (0, size_i), o_in)]),
            ([a_part(5, 6)], [a_part(6, 7)]),
            ([a_part(3, 4)], [a_part(4, 5)]),
            ([a_part(0, 2)], [a_part(2, 3), other(late_s, bufs_s, (0, rows), o_s)]),
        ]
        steps = reduce_steps(me, chunks, send, recv)

        def keep(piece, value):
            late[piece] = value.astype(LOW).reshape(late.shape[1:])

        def keep_small(value):
            late_s[...] = value.astype(LOW).reshape(late_s.shape)
    else:
        steps = iter(())
        o_late, o_small = outs

        def keep(piece, value):
            o_late[piece] = value.astype(LOW)

        def keep_small(value):
            o_small[...] = value

    def advance():
        return next(steps, None)

    advance()
    segments = seg[...].astype(WIDE)
    row_seg[...] = segments
    row_keep[...] = 1.0 - pad[...].astype(WIDE)
    pair_row = jnp.zeros((1, tok_count), WIDE)
    for k in range(SEGS):
        pair_row = jnp.where(segments == k, pair[0, k].astype(WIDE), pair_row)
    columns = transposed_rows(jnp.concatenate([segments, pair_row, jnp.zeros((6, tok_count), WIDE)], axis=0))
    col_seg[...] = columns
    onehot = (lanes((tok_count, 128)) == (columns[:, 1:2].astype(jnp.int32) + 8)).astype(LOW)
    for copy in loads:
        copy.wait()

    def flat(value):
        return value.reshape((-1, value.shape[-1]))

    table = flat(w_s[...]).astype(WIDE).T
    w_key, w_val = flat(w_kv[0]), flat(w_kv[1])
    advance()
    parts = 4
    span = src_count // parts
    for k in range(parts):
        at = pl.ds(k * span, span)
        grads = dot_nt(dkv[at, 0:width], w_key) + dot_nt(dkv[at, width : 2 * width], w_val)
        grad_enc[at, :] = grads.astype(LOW)
    advance()
    keep(5, dot_tn(enc[...], dkv[:, 0:width]))
    keep(6, dot_tn(enc[...], dkv[:, width : 2 * width]))
    advance()
    swap.wait()
    g_query = (dq_own[...] + got_dq[...].astype(WIDE)).astype(LOW)
    keep(4, dot_tn(two[...], g_query))
    back, gain_1, bias_1 = norm_back(after[...], table[1:2], dot_nt(g_query, flat(w_cq[...])))
    grad_state = gstate[...] + back
    g_self = grad_state.astype(LOW)
    keep(3, dot_tn(low[...], g_self))
    g_attn[...] = dot_nt(g_self, flat(w_so[...])).astype(LOW)
    advance()
    self_backward(qkv, low, lse, g_attn, dqkv, dk, dv, row_seg, row_keep, col_seg)
    for k in range(3):
        keep(k, dot_tn(one[...], dqkv[:, k * width : (k + 1) * width]))
    upstream = dot_nt(dqkv[:, 0:width], flat(w_qkv[0]))
    upstream = upstream + dot_nt(dqkv[:, width : 2 * width], flat(w_qkv[1]))
    upstream = upstream + dot_nt(dqkv[:, 2 * width : 3 * width], flat(w_qkv[2]))
    back, gain_0, bias_0 = norm_back(start[...], table[0:1], upstream)
    grad_start = grad_state + back
    grad_input[...] = grad_start.astype(LOW)
    coarse = grad_start.astype(LOW)
    fine = (grad_start - coarse.astype(WIDE)).astype(LOW)
    g_table = (dot_tn(onehot, coarse) + dot_tn(onehot, fine))[8:16]
    mid = small_rows[...]
    stacked = jnp.concatenate(
        [gain_0, gain_1, mid[0:2], bias_0, bias_1, mid[2:4], g_table], axis=0
    )
    keep_small(transposed_rows(stacked) + small_cols[...])
    for _ in steps:
        pass


def last_part(depth, reduces, pair, seg, pad, dq_own, dq_other, dkv, enc, kept, gstate, grads, whole):
    tok_count, width = dq_own.shape
    src_count = enc.shape[0]
    ga, gf, gi, gs = whole
    gw_a, gw_f, gw_i, small_rows, small_cols = grads
    everyone = depth * 8
    rows = BLOCK // everyone
    sharded = (depth, 2, 2, 2)
    outs = [shape_of((tok_count, width), LOW), shape_of((src_count, width), LOW)]
    scratch = [
        pltpu.VMEM((3, BLOCK, BLOCK), LOW),
        pltpu.VMEM((1, BLOCK, BLOCK), LOW),
        pltpu.VMEM((1, BLOCK, BLOCK), LOW),
        pltpu.VMEM((2, BLOCK, BLOCK), LOW),
        pltpu.VMEM(gs.shape, LOW),
        pltpu.VMEM((tok_count, width), LOW),
        pltpu.VMEM((tok_count, width), LOW),
        pltpu.VMEM((tok_count, 3 * width), LOW),
        pltpu.VMEM((tok_count, 128), WIDE),
        pltpu.VMEM((tok_count, 128), WIDE),
        pltpu.VMEM((1, tok_count), WIDE),
        pltpu.VMEM((1, tok_count), WIDE),
        pltpu.VMEM((tok_count, 128), WIDE),
        pltpu.SemaphoreType.DMA((5,)),
        pltpu.SemaphoreType.DMA((1,)),
        pltpu.SemaphoreType.DMA((1,)),
    ]
    if reduces:
        shapes = [(12, rows, BLOCK), (1, gf.shape[0] // everyone, width), (1, gi.shape[0] // everyone, gi.shape[1]), (1, rows, 128)]
        outs += [
            shape_of((rows, 3 * BLOCK), WIDE),
            shape_of((rows, BLOCK), WIDE),
            shape_of((rows, BLOCK), WIDE),
            shape_of((rows, 2 * BLOCK), WIDE),
            shape_of((rows, BLOCK), WIDE),
            shape_of((rows, 4 * BLOCK), WIDE),
            shape_of(shapes[1][1:], WIDE),
            shape_of(shapes[2][1:], WIDE),
            shape_of((rows, 128), WIDE),
        ]
        gw_a = gw_a.reshape((5,) + sharded + shapes[0][1:])
        gw_f = gw_f.reshape((1,) + sharded + shapes[1][1:])
        gw_i = gw_i.reshape((1,) + sharded + shapes[2][1:])
        scratch += [
            pltpu.VMEM((7,) + sharded + shapes[0][1:], LOW),
            pltpu.VMEM((1,) + sharded + shapes[3][1:], LOW),
        ]
        for lead in ((depth, 2, 2), (depth, 2), (depth,), (depth - 1,)):
            scratch += [pltpu.VMEM((n,) + lead + (r, w), LOW) for n, r, w in shapes]
        slots = 2 * (5 + (depth - 1) * 2)
        scratch += [pltpu.SemaphoreType.DMA((6, slots)), pltpu.SemaphoreType.DMA((6, slots))]
    else:
        outs += [shape_of((7, BLOCK, BLOCK), LOW), shape_of((BLOCK, 128), WIDE)]
    return pl.pallas_call(
        partial(last_kernel, depth, reduces),
        name="last_part",
        out_shape=outs,
        in_specs=[SMEM] + [VMEM] * 19 + [ANY] * 2,
        out_specs=[VMEM] * len(outs),
        scratch_shapes=scratch,
        compiler_params=pltpu.CompilerParams(
            collective_id=2, has_side_effects=True, vmem_limit_bytes=LIMIT
        ),
    )(pair, seg, pad, dq_own, dq_other, dkv, enc, *kept, gstate, gw_a, gw_f, gw_i, small_rows, small_cols, ga, gs)


def gather_by_ops(raw, small):
    qkv, self_out, cross_q, cross_kv, cross_out, ffn_in, ffn_out, insert = raw
    wide = jnp.concatenate([qkv, self_out, cross_q, cross_kv, cross_out, ffn_in], axis=1)
    ga = lax.all_gather(wide, BOTH, axis=0, tiled=True).reshape(BLOCK, 12, BLOCK).swapaxes(0, 1)
    return (
        ga,
        lax.all_gather(ffn_out, BOTH, axis=0, tiled=True),
        lax.all_gather(insert, BOTH, axis=0, tiled=True),
        lax.all_gather(small, BOTH, axis=0, tiled=True),
    )


def reduce_by_ops(late, small, grads, scale):
    gw_a, gw_f, gw_i = grads
    wide = jnp.concatenate([late, gw_a]).swapaxes(0, 1).reshape(BLOCK, 12 * BLOCK)

    def sums(a):
        return lax.psum_scatter(a.astype(WIDE), BOTH, scatter_dimension=0, tiled=True) * scale

    own = sums(wide)
    edges = (0, 3, 4, 5, 7, 8, 12)
    pieces = [own[:, lo * BLOCK : hi * BLOCK] for lo, hi in zip(edges[:-1], edges[1:])]
    return pieces + [sums(gw_f), sums(gw_i), sums(small)]


def body(
    dec_input, enc_output, segment_ids, padding, pair_ids, src_lengths, delete_labels, insert_counts,
    masked_positions, masked_targets, norm_gain, norm_bias, pair_table, self_qkv, self_out, cross_q, cross_kv,
    cross_out, ffn_in, ffn_out, w_delete, w_insert, w_vocab,
):
    everyone = lax.axis_size(BOTH)
    depth = everyone // 8
    tok_count, width = dec_input.shape
    masked = masked_positions.shape[1]
    rows = self_qkv.shape[0]
    aligned = rows % 16 == 0
    src_pos = lax.axis_index("src")
    small = jnp.concatenate([norm_gain, norm_bias, pair_table, w_delete.T], axis=0).T
    small = jnp.pad(small, ((0, 0), (0, 128 - small.shape[1])))
    raw = (self_qkv, self_out, cross_q, cross_kv, cross_out, ffn_in, ffn_out, w_insert)
    whole = None if aligned else gather_by_ops(raw, small)
    whole, firsts = first_part(
        depth, aligned, segment_ids, padding, pair_ids, dec_input, enc_output, small, raw, whole
    )
    start, one, qkv, low, lse, after, two, query, other_query, kv = firsts

    partners = lax.all_gather(segment_ids[0], "src")
    other_seg = lax.dynamic_index_in_dim(partners, 1 - src_pos, 0, keepdims=False)
    seg_s = jnp.stack([src_pos * SEGS + segment_ids[0], (1 - src_pos) * SEGS + other_seg])
    seg_cols = jnp.pad(seg_s.T, ((0, 0), (0, 126)))
    ends_s = jnp.concatenate([jnp.zeros((1,), jnp.int32), jnp.cumsum(src_lengths[0])])
    attended = cross_forward(seg_s, ends_s, seg_cols, query, other_query, kv)

    mids = middle_part(
        depth, segment_ids, padding, delete_labels, insert_counts, masked_positions.reshape(-1, 1),
        masked_targets.reshape(-1, 1), w_vocab, after, attended, whole,
    )
    block_out, gstate, g_own, g_other, st_own, st_other = mids[:6]
    grads, (grad_vocab, tokens, loss) = mids[6:11], mids[11:]
    dq_own, dq_other, dkv = cross_backward(
        seg_s, ends_s, seg_cols, query, other_query, g_own, g_other, st_own, st_other, kv
    )
    res = last_part(
        depth, aligned, pair_ids, segment_ids, padding, dq_own, dq_other, dkv, enc_output,
        (start, one, qkv, low, lse, after, two), gstate, grads, whole,
    )
    grad_input, grad_enc = res[:2]
    if aligned:
        sums = res[2:]
    else:
        scale = (tok_count * everyone) ** (-0.5)
        sums = reduce_by_ops(res[2], res[3], grads[:3], scale)
    small_sum = sums[8].T
    pos = lax.axis_index(BOTH)
    own_tokens = lax.dynamic_slice_in_dim(tokens[0:1], pos * masked, masked, axis=1)
    return (
        block_out, grad_input, grad_enc, small_sum[0:4], small_sum[4:8], small_sum[8:16], *sums[:8][:6],
        sums[6], small_sum[16:18].T, sums[7], grad_vocab, loss[0, 0], own_tokens,
    )


def solution(mesh):
    shared = P(BOTH, None)
    across = P(None, BOTH)
    return jax.shard_map(
        body,
        mesh=mesh,
        in_specs=(shared,) * 5 + (P("batch", None),) + (shared,) * 4 + (across,) * 3 + (shared,) * 10,
        out_specs=(shared,) * 3 + (across,) * 3 + (shared,) * 10 + (P(), shared),
        check_vma=False,
    )
```

time: 2960 us -> 348 us (0.12)
  waiting for transfers between devices: 1460 us -> 0 us
  blocking collectives: 914 us -> 5.45 us
  matrix products: 313 us -> 0 us
  Pallas kernels: 0 us -> 307 us
  other arithmetic: 189 us -> 1.53 us
    reduce_scatter x10 -> x0, waiting for transfers between devices: 887 us -> none  [the longest x1 141 us: body(): lax.psum_scatter(grad_ffn_out_w, ('batch', 'src'), scatter_dimension=0, t...]
    all_gather x15 -> x1, blocking collectives: 827 us -> 5.45 us  [body(): partners = lax.all_gather(segment_ids[0], 'src')]
    unnamed x26 -> x0, waiting for transfers between devices: 526 us -> none
    dot_general x126 -> x0, matrix products: 310 us -> none  [the longest x42 141 us: matmul_nt(): lax.dot_general(left, right, (((1,), (1,)), ((), ())), preferred_element_...]
    pallas_call x0 -> x5, Pallas kernels: none -> 307 us  [the longest x1 92.5 us: last_part(): pl.pallas_call(partial(last_kernel, depth, reduces), name='last_part', ou...]
    convert_element_type x84 -> x0, other arithmetic: 78.4 us -> none  [the longest x11 72.4 us: attention_backward(): (probs_full * (grad_prob - delta[0:block, head_pos:head_pos + 1])).astype...]
    reduce_sum x21 -> x0, other arithmetic: 48.8 us -> none  [the longest x2 28.2 us: attention_stats(): jnp.sum(jnp.where(allowed, jnp.exp(scores - row_top), 0.0), axis=1, keepd...]
    psum x2 -> x0, blocking collectives: 48 us -> none  [the longest x1 40.6 us: body(): mean_loss = lax.psum(local_loss, ('batch', 'src')) / (tok_count * everyone)]
  transfers between devices with their start and end apart: 21 -> 0, of which waited for: 14 -> 0; matrix products, arithmetic and copies ran while one was open for 6% -> 0% of each run, Pallas kernels for 0% -> 0%
where the time goes in v2:
time: 348 us; the launch traced here: 342 us
  Pallas kernels  307 us (88%)
  local copies, waits for them, and re-layouts  25.9 us (7%)
  blocking collectives  5.45 us (2%)
    pallas_call x1, Pallas kernels, last_part(): pl.pallas_call(partial(last_kernel, depth, reduces), name='last_part', ou...  92.5 us
    pallas_call x1, Pallas kernels, first_part(): pl.pallas_call(partial(first_kernel, depth, gathers), name='first_part',...  84.1 us
    pallas_call x1, Pallas kernels, middle_part(): pl.pallas_call(partial(middle_kernel, depth, None), name='middle_part', o...  78.1 us
    pallas_call x1, Pallas kernels, cross_backward(): pl.pallas_call(cross_backward_kernel, name='cross_backward', out_shape=[s...  28.8 us
    pallas_call x1, Pallas kernels, cross_forward(): pl.pallas_call(cross_forward_kernel, name='cross_forward', out_shape=[out...  23.9 us
    unnamed x44, local copies, waits for them, and re-layouts  16 us

profile of v2, /device:TPU:0, one launch (start us, length us, event | category | flops | bytes accessed | tf_op | source)
XLA Modules:
  0.0 341.6 jit_solution(6250168575723081410)
XLA Ops:
  0.7 0.7 broadcast_add_fusion
  1.4 0.8 copy.73
  2.1 0.8 copy.74
  2.9 0.8 copy.75
  3.6 0.7 copy.72
  4.4 0.1 maximum_bitcast_fusion
  4.5 0.6 pad.8.refs_5_
  5.1 5.4 %all-gather = s32[2,1,512]{2,1,0:T(1,128)S(1)} all-gather(s32[1,1,512]{2,1,0:T(1,128)} %bitcast.34), channel_id=1, replica_groups=mesh['batch'=16,'src'=2] {'src'}, dimensions={0}, use_global_device_ids=true | all-gather | bytes 6144 | tf_op jit(solution)/shard_map/all_gather | solution.py:1335
  10.5 0.0 copy-start.6
  10.6 0.7 copy.76
  11.3 0.1 reduce
  11.4 0.6 pad_add_fusion.1.ends_s
  12.0 1.3 copy.78.refs_4_
  13.4 1.3 copy.79.refs_5_
  14.7 0.1 copy.77
  14.8 0.7 pad.9.seg_cols
  15.6 84.1 %first_part.1 = (bf16[12,4,2,2,2,16,512]{6,5,4,3,2,1,0:T(8,128)(2,1)}, bf16[4,2,2,2,64,512]{5,4,3,2,1,0:T(8,128)(2,1)}, bf16[4,2,2,2,32,256]{5,4,3,2,1,0:T(8,128...) custom-call(s32[1,512]{1,0:T(1,128)} %refs_1_.5, ...), custom_call_target="tpu_custom_call" | custom-call | tf_op jit(solution)/shard_map/first_part/pallas_call | solution.py:406
  99.7 0.0 copy-done.6
  99.7 23.9 %cross_forward.1 = (bf16[512,512]{1,0:T(8,128)(2,1)}, bf16[512,512]{1,0:T(8,128)(2,1)}, f32[8,512]{1,0:T(8,128)}, f32[8,512]{1,0:T(8,128)}) custom-call(s32[2,512]{1,0:T(2,128)} %copy-done.6, s32[17]{0:T(128)} %pad_add_fusion.1.ends_s, s32[512,128]{1,0:T(8,128)} %pad.9.seg_cols, bf16[512,512]{1,0:T(8,128)(2,1)} %get-tuple-element.65.q_own, ...), custom_call_target="tpu_custom_call" | custom-call | tf_op jit(solution)/shard_map/cross_forward/pallas_call | solution.py:516
  123.6 78.1 %middle_part.1 = (bf16[512,512]{1,0:T(8,128)(2,1)}, f32[512,512]{1,0:T(8,128)}, bf16[512,512]{1,0:T(8,128)(2,1)}, bf16[512,512]{1,0:T(8,128)(2,1)}, f32[16,512]{...) custom-call(s32[1,512]{1,0:T(1,128)} %refs_1_.5, ...), custom_call_target="tpu_custom_call" | custom-call | tf_op jit(solution)/shard_map/middle_part/pallas_call | solution.py:887
  201.7 1.2 slice.22
  202.9 0.7 slice.23
  203.6 0.6 constant_dynamic-slice_fusion
  204.2 28.8 %cross_backward.1 = (f32[512,512]{1,0:T(8,128)}, bf16[512,512]{1,0:T(8,128)(2,1)}, bf16[2048,1024]{1,0:T(8,128)(2,1)}) custom-call(s32[2,512]{1,0:T(2,128)} %copy-done.6, s32[17]{0:T(128)} %pad_add_fusion.1.ends_s, s32[512,128]{1,0:T(8,128)} %pad.9.seg_cols, bf16[512,512]{1,0:T(8,128)(2,1)} %get-tuple-element.65.q_own, ...), custom_call_target="tpu_custom_call" | custom-call | tf_op jit(solution)/shard_map/cross_backward/pallas_call | solution.py:583
  233.0 92.5 %last_part.1 = (bf16[512,512]{1,0:T(8,128)(2,1)}, bf16[2048,512]{1,0:T(8,128)(2,1)}, f32[16,1536]{1,0:T(8,128)}, f32[16,512]{1,0:T(8,128)}, f32[16,512]{1,0:T(8,...) custom-call(s32[1,8]{1,0:T(1,128)} %refs_0_.5, ...), custom_call_target="tpu_custom_call" | custom-call | tf_op jit(solution)/shard_map/last_part/pallas_call | solution.py:1276
  325.5 0.9 slice.26
  326.5 0.7 copy.82
  327.1 0.8 slice_bitcast_fusion
  327.9 0.6 copy.83
  328.5 0.8 fusion
  329.4 0.7 copy.81
  330.0 0.7 copy.80
  330.7 0.8 copy.96
  331.5 1.9 copy.97
  333.4 0.0 copy-start.7
  333.4 0.0 copy-start.9
  333.4 0.0 copy-start.4
  333.4 0.0 copy-start.3
  333.4 1.3 copy.98
  334.7 0.6 copy.99
  335.4 0.6 copy.100
  336.0 0.6 copy.101
  336.6 0.6 copy.102
  337.3 0.6 copy.103
  337.9 0.7 copy.104
  338.5 0.7 copy.105
  339.2 0.6 copy.106
  339.8 1.3 copy.107
  (21 shorter events, 0.1 us)
Async XLA Ops:
  10.5 89.1 %copy-start.6 = (s32[2,512]{1,0:T(2,128)}, s32[2,512]{1,0:T(2,128)S(1)}, u32[]{:S(2)}) copy-start(s32[2,512]{1,0:T(2,128)S(1)} %pad_add_fusion.seg_s) | copy-start | bytes 12292
  233.0 97.7 %copy-start.2 = (bf16[512,512]{1,0:T(8,128)(2,1)S(1)}, bf16[512,512]{1,0:T(8,128)(2,1)}, u32[]{:S(2)}) copy-start(bf16[512,512]{1,0:T(8,128)(2,1)} %get-tuple-element.184) | copy-start | bytes 1572868
  325.5 7.8 %copy-start.1 = (bf16[2048,512]{1,0:T(8,128)(2,1)S(1)}, bf16[2048,512]{1,0:T(8,128)(2,1)}, u32[]{:S(2)}) copy-start(bf16[2048,512]{1,0:T(8,128)(2,1)} %get-tuple-element.186) | copy-start | bytes 6291460
  333.3 1.4 copy-start.5
  333.3 2.0 copy-start.11
  333.4 2.7 copy-start.10
  333.4 3.3 copy-start.7
  333.4 3.9 %copy-start.9 = (f32[16,512]{1,0:T(8,128)S(1)}, f32[16,512]{1,0:T(8,128)}, u32[]{:S(2)}) copy-start(f32[16,512]{1,0:T(8,128)} %get-tuple-element.194) | copy-start | bytes 98308
  333.4 4.5 %copy-start.4 = (f32[16,2048]{1,0:T(8,128)S(1)}, f32[16,2048]{1,0:T(8,128)}, u32[]{:S(2)}) copy-start(f32[16,2048]{1,0:T(8,128)} %get-tuple-element.195) | copy-start | bytes 393220
  333.4 5.1 %copy-start.3 = (f32[64,512]{1,0:T(8,128)S(1)}, f32[64,512]{1,0:T(8,128)}, u32[]{:S(2)}) copy-start(f32[64,512]{1,0:T(8,128)} %get-tuple-element.196) | copy-start | bytes 393220
  333.4 5.8 %copy-start.8 = (f32[32,256]{1,0:T(8,128)S(1)}, f32[32,256]{1,0:T(8,128)}, u32[]{:S(2)}) copy-start(f32[32,256]{1,0:T(8,128)} %get-tuple-element.198) | copy-start | bytes 98308
  333.4 6.4 %copy-start = (f32[1024,512]{1,0:T(8,128)S(1)}, f32[1024,512]{1,0:T(8,128)}, u32[]{:S(2)}) copy-start(f32[1024,512]{1,0:T(8,128)} %get-tuple-element.199) | copy-start | bytes 6291460

commit v3 on v2

v3 whole, which is shorter than its diff:
```python
from functools import partial

import jax
import jax.numpy as jnp
from jax import lax
from jax.experimental import pallas as pl
from jax.experimental.pallas import tpu as pltpu
from jax.sharding import PartitionSpec as P

HD = 64
PAIRS = 8
SEGS = 8
BLOCK = 512
EPSILON = 1e-05
SCALE = 0.125
FILL = -1e30
GELU = 0.7978845608
CUBIC = 0.044715

MESH = pl.DeviceIdType.MESH
ANY = pl.BlockSpec(memory_space=pl.ANY)
VMEM = pl.BlockSpec(memory_space=pltpu.VMEM)
SMEM = pl.BlockSpec(memory_space=pltpu.SMEM)
BOTH = ("batch", "src")
LOW = jnp.bfloat16
WIDE = jnp.float32
LIMIT = 60 << 20


def shape_of(shape, kind):
    return jax.ShapeDtypeStruct(shape, kind)


def dot(left, right):
    return jnp.dot(left, right, preferred_element_type=WIDE)


def dot_tn(left, right):
    return lax.dot_general(left, right, (((0,), (0,)), ((), ())), preferred_element_type=WIDE)


def dot_nt(left, right):
    return lax.dot_general(left, right, (((1,), (1,)), ((), ())), preferred_element_type=WIDE)


def normalised(v):
    centred = v - jnp.mean(v, axis=-1, keepdims=True)
    r = lax.rsqrt(jnp.mean(centred * centred, axis=-1, keepdims=True) + EPSILON)
    return centred * r, r


def norm_back(v, gain, upstream):
    hat, r = normalised(v)
    scaled = upstream * gain
    first = jnp.mean(scaled, axis=-1, keepdims=True)
    second = jnp.mean(scaled * hat, axis=-1, keepdims=True)
    grad_gain = jnp.sum(upstream * hat, axis=0, keepdims=True)
    grad_bias = jnp.sum(upstream, axis=0, keepdims=True)
    return r * (scaled - first - hat * second), grad_gain, grad_bias


def lanes(shape):
    return lax.broadcasted_iota(jnp.int32, shape, len(shape) - 1)


def rows_of(shape):
    return lax.broadcasted_iota(jnp.int32, shape, len(shape) - 2)


def both_heads(x):
    low = lanes(x.shape) < HD
    zero = jnp.zeros_like(x)
    return jnp.concatenate([jnp.where(low, x, zero), jnp.where(low, zero, x)], axis=0)


def join_heads(x):
    half = x.shape[0] // 2
    return jnp.where(lanes((half, x.shape[1])) < HD, x[:half], x[half:])


def twice(x):
    return jnp.concatenate([x, x], axis=0)


def transposed_rows(rows):
    count, width = rows.shape
    return jnp.concatenate([rows, jnp.zeros((128 - count, width), WIDE)], axis=0).T


def greet(peers):
    barrier = pltpu.get_barrier_semaphore()
    for peer in peers:
        pl.semaphore_signal(barrier, inc=1, device_id=peer, device_id_type=MESH)
    pl.semaphore_wait(barrier, len(peers))


def remote(src, dst, send, recv, peer):
    return pltpu.make_async_remote_copy(
        src_ref=src,
        dst_ref=dst,
        send_sem=send,
        recv_sem=recv,
        device_id=peer,
        device_id_type=MESH,
    )


class Place:
    def __init__(self, depth):
        b = lax.axis_index("batch")
        self.depth = depth
        self.y = lax.axis_index("src")
        self.c = lax.rem(b, 2)
        self.x = lax.rem(b // 2, 2)
        self.z = b // 4

    def at(self, z=None, x=None, c=None, y=None):
        z = self.z if z is None else z
        x = self.x if x is None else x
        c = self.c if c is None else c
        y = self.y if y is None else y
        return ((z * 2 + x) * 2 + c, y)

    def along(self, k):
        return self.at(z=lax.rem(self.z + k, self.depth))

    def others(self):
        return [self.along(k) for k in range(1, self.depth)]

    def across_x(self):
        return self.at(x=1 - self.x)

    def across_y(self):
        return self.at(y=1 - self.y)

    def across_both(self):
        return self.at(x=1 - self.x, y=1 - self.y)

    def across_core(self):
        return self.at(c=1 - self.c)


def gather_steps(me, chunks, send, recv):
    z, x, c, y = me.z, me.x, me.c, me.y
    count = len(chunks)
    started = [[None] * 3 for _ in chunks]
    used = [0] * count
    every = slice(None)

    def launch(k, stage):
        copies = []

        def push(block, peer):
            slot = used[k]
            used[k] += 1
            copy = remote(block, block, send.at[k, slot], recv.at[k, slot], peer)
            copy.start()
            copies.append(copy)

        for view in chunks[k]:
            if stage == 0:
                for peer in me.others():
                    push(view(z, x, c, y), peer)
            elif stage == 1:
                for peer in (me.across_x(), me.across_y(), me.across_both()):
                    push(view(every, x, c, y), peer)
            else:
                push(view(every, every, c, every), me.across_core())
        started[k][stage] = copies

    for step in range(count + 3):
        for stage in range(3, -1, -1):
            k = step - stage
            if not 0 <= k < count:
                continue
            if stage > 0:
                for copy in started[k][stage - 1]:
                    copy.wait_recv()
            if stage < 3:
                launch(k, stage)
        yield step - 3
    for stages in started:
        for copies in stages:
            for copy in copies:
                copy.wait_send()


def self_window(block, tok_count):
    low = jnp.clip(block * 128 - 128, 0, tok_count - 384)
    return pl.multiple_of(low, 128)


def self_mask(row_seg, row_keep, col_seg, block, low):
    at = pl.ds(low, 384)
    keys = row_seg[0:1, at]
    keep = row_keep[0:1, at]
    queries = col_seg[pl.ds(pl.multiple_of(block * 128, 128), 128), 0:1]
    shape = (128, 384)
    own = (rows_of(shape) + block * 128) == (lanes(shape) + low)
    return (queries == keys) & ((keep > 0.5) | own)


def self_forward(blocks, qkv, out, lse_ref, row_seg, row_keep, col_seg):
    tok_count, width = out.shape
    first, last = blocks
    pairs = width // 128

    def one(t, carry):
        block, pair = first + t // pairs, lax.rem(t, pairs)
        at = pl.ds(pl.multiple_of(block * 128, 128), 128)
        low = self_window(block, tok_count)
        keys = pl.ds(low, 384)
        base = pl.multiple_of(pair * 128, 128)
        q = both_heads(qkv[at, pl.ds(base, 128)] * SCALE)
        k = qkv[keys, pl.ds(pl.multiple_of(base + width, 128), 128)]
        v = qkv[keys, pl.ds(pl.multiple_of(base + 2 * width, 128), 128)]
        allowed = self_mask(row_seg, row_keep, col_seg, block, low)
        scores = jnp.where(twice(allowed), dot_nt(q, k), FILL)
        top = jnp.max(scores, axis=1, keepdims=True)
        exps = jnp.exp(scores - top)
        total = jnp.sum(exps, axis=1, keepdims=True)
        probs = (exps * (1.0 / total)).astype(LOW)
        out[at, pl.ds(base, 128)] = join_heads(dot(probs, v)).astype(LOW)
        lse = top + jnp.log(total)
        lane = lanes((128, 128))
        lse_ref[at, :] = jnp.where(
            lane == 2 * pair, lse[:128], jnp.where(lane == 2 * pair + 1, lse[128:], lse_ref[at, :])
        )
        return carry

    lax.fori_loop(0, (last - first) * pairs, one, 0)


def small_matrix(gain, bias, pair_rows, delete):
    def spot(count, first):
        shape = (count, 128)
        return (rows_of(shape) + first == lanes(shape)).astype(LOW)

    total = dot_tn(gain, spot(4, 0)) + dot_tn(bias, spot(4, 4)) + dot_tn(pair_rows, spot(PAIRS, 8))
    return (total + dot_tn(delete, spot(2, 8 + PAIRS))).astype(LOW)


def token_numbers(seg, pad, pair, row_seg, row_keep, col_seg):
    tok_count = seg.shape[1]
    segments = seg[...].astype(WIDE)
    row_seg[...] = segments
    row_keep[...] = 1.0 - pad[...].astype(WIDE)
    pair_row = jnp.zeros((1, tok_count), WIDE)
    for k in range(SEGS):
        pair_row = jnp.where(segments == k, pair[0, k].astype(WIDE), pair_row)
    columns = transposed_rows(jnp.concatenate([segments, pair_row, jnp.zeros((6, tok_count), WIDE)], axis=0))
    col_seg[...] = columns
    return (lanes((tok_count, 128)) == (columns[:, 1:2].astype(jnp.int32) + 8)).astype(LOW)


def cutter(ref):
    every = (slice(None),) * (len(ref.shape) - 2)

    def cut(lo, hi):
        value = ref[every + (slice(lo, hi),)]
        return value.reshape((-1, value.shape[-1]))

    return cut


QKV, SO, CQ, KV, EARLY = 0, 48, 64, 80, 112


def first_kernel(depth, gathers, *refs):
    (seg, pad, pair, dec, enc) = refs[:5]
    refs = refs[5:]
    if gathers:
        (gain, bias, pair_rows, delete, raw_qkv, raw_so, raw_cq, raw_kv, raw_co, raw_fi, raw_fo, raw_in) = refs[:12]
        (ga_out, gs_out, gz) = refs[12:15]
        refs = refs[15:]
    else:
        ga_in, gs_in = refs[:2]
        refs = refs[2:]
    (start_out, one_out, qkv_out, low_out, lse_out, after_out, two_out, query_out, other_out, kv_out, seg_out) = refs[:11]
    (ga, gs, row_seg, row_keep, col_seg, own_sem, send, recv, sw_send, sw_recv) = refs[11:]
    tok_count, width = dec.shape
    src_count = enc.shape[0]
    me = Place(depth)
    z, x, c, y = me.z, me.x, me.c, me.y
    owns = []

    def own(src, dst):
        copy = pltpu.make_async_copy(src, dst, own_sem.at[len(owns)])
        copy.start()
        owns.append(copy)

    if gathers:
        for raw, count, first in ((raw_qkv, 3, QKV), (raw_so, 1, SO), (raw_cq, 1, CQ), (raw_kv, 2, KV)):
            for k in range(count):
                own(raw.at[:, pl.ds(k * BLOCK, BLOCK)], ga.at[z, x, c, y, pl.ds(first + 16 * k, 16)])
        soon = len(owns)
        own(raw_co, gz.at[z, pl.ds(0, 16)])
        for k in range(4):
            own(raw_fi.at[:, pl.ds(k * BLOCK, BLOCK)], gz.at[z, pl.ds(16 + 16 * k, 16)])
        own(raw_fo, gz.at[z, pl.ds(80, 64)])
        for k in range(2):
            half = BLOCK // 2
            own(raw_in.at[pl.ds(16 * k, 16)], gz.at[z, pl.ds(144, 16), pl.ds(half * k, half)])
        gs[z, x, c, y] = small_matrix(gain[...], bias[...], pair_rows[...], delete[...])
        greet(me.others() + [me.across_x(), me.across_y(), me.across_both(), me.across_core()])
        for copy in owns[:soon]:
            copy.wait()

        def rows(lo, hi):
            return lambda *at: ga.at[at + (pl.ds(lo, hi - lo),)]

        chunks = [[lambda *at: gs.at[at], rows(QKV, SO)], [rows(SO, EARLY)]]
        steps = gather_steps(me, chunks, send, recv)
    else:
        own(ga_in, ga)
        own(gs_in, gs)
        greet([me.across_y()])
        for copy in owns:
            copy.wait()
        steps = iter(())

    def advance():
        return next(steps, None)

    def have(chunk):
        while gathers:
            done = advance()
            if done is None or done >= chunk:
                return

    advance()
    onehot = token_numbers(seg, pad, pair, row_seg, row_keep, col_seg)
    lse_out[...] = jnp.zeros_like(lse_out)
    meet = remote(seg, seg_out, sw_send.at[0], sw_recv.at[0], me.across_y())
    meet.start()
    cut = cutter(ga)
    have(0)
    line = []
    if gathers:
        for copy in owns[soon:]:
            copy.wait()
        for k in range(1, depth):
            line.append(remote(gz.at[z], gz.at[z], sw_send.at[3 + k], sw_recv.at[3 + k], me.along(k)))
            line[-1].start()
    table = cutter(gs)(0, gs.shape[-2]).astype(WIDE).T
    start = dec[...].astype(WIDE) + dot(onehot, table.astype(LOW))
    start_out[...] = start
    one = (normalised(start)[0] * table[0:1] + table[4:5]).astype(LOW)
    one_out[...] = one
    for k in range(3):
        qkv_out[:, pl.ds(k * BLOCK, BLOCK)] = dot(one, cut(QKV + 16 * k, QKV + 16 * (k + 1))).astype(LOW)
    advance()
    halves = 2
    span = tok_count // halves
    swaps = []
    for k in range(halves):
        at = pl.ds(k * span, span)
        self_forward((k * span // 128, (k + 1) * span // 128), qkv_out, low_out, lse_out, row_seg, row_keep, col_seg)
        if k == 0:
            have(1)
        after = start_out[at, :] + dot(low_out[at, :], cut(SO, CQ))
        after_out[at, :] = after
        two = (normalised(after)[0] * table[1:2] + table[5:6]).astype(LOW)
        two_out[at, :] = two
        query_out[at, :] = dot(two, cut(CQ, KV)).astype(LOW)
        swap = remote(query_out.at[at], other_out.at[at], sw_send.at[1 + k], sw_recv.at[1 + k], me.across_y())
        swap.start()
        swaps.append(swap)
    if gathers:
        own(ga, ga_out)
        own(gs, gs_out)
    w_key, w_val = cut(KV, KV + 16), cut(KV + 16, EARLY)
    parts = 4
    for k in range(parts):
        span = src_count // parts
        at = pl.ds(k * span, span)
        kv_out[at, 0:width] = dot(enc[at, :], w_key).astype(LOW)
        kv_out[at, width : 2 * width] = dot(enc[at, :], w_val).astype(LOW)
    for _ in steps:
        pass
    for copy in swaps + [meet] + line:
        copy.wait()
    if gathers:
        for copy in owns[-2:]:
            copy.wait()


def first_part(depth, gathers, seg, pad, pair, dec, enc, tiny, raw, late, whole):
    tok_count, width = dec.shape
    src_count = enc.shape[0]
    lead = (depth, 2, 2, 2) if gathers else (BLOCK // 16,)
    outs = [
        (shape_of((tok_count, width), WIDE), VMEM),
        (shape_of((tok_count, width), LOW), VMEM),
        (shape_of((tok_count, 3 * width), LOW), VMEM),
        (shape_of((tok_count, width), LOW), VMEM),
        (shape_of((tok_count, 128), WIDE), VMEM),
        (shape_of((tok_count, width), WIDE), VMEM),
        (shape_of((tok_count, width), LOW), VMEM),
        (shape_of((tok_count, width), LOW), VMEM),
        (shape_of((tok_count, width), LOW), ANY),
        (shape_of((src_count, 2 * width), LOW), VMEM),
        (shape_of((1, tok_count), jnp.int32), ANY),
    ]
    if gathers:
        outs = [
            (shape_of(lead + (EARLY, BLOCK), LOW), ANY),
            (shape_of(lead + (16, 128), LOW), ANY),
            (shape_of((depth, 160, BLOCK), LOW), ANY),
        ] + outs
    extra = (*tiny, *raw, *late) if gathers else whole
    res = pl.pallas_call(
        partial(first_kernel, depth, gathers),
        name="first_part",
        out_shape=[o for o, _ in outs],
        in_specs=[VMEM, VMEM, SMEM, VMEM, VMEM] + ([VMEM] * 4 + [ANY] * 8 if gathers else [ANY] * 2),
        out_specs=[s for _, s in outs],
        scratch_shapes=[
            pltpu.VMEM(lead + (EARLY, BLOCK), LOW),
            pltpu.VMEM(lead + (16, 128), LOW),
            pltpu.VMEM((1, tok_count), WIDE),
            pltpu.VMEM((1, tok_count), WIDE),
            pltpu.VMEM((tok_count, 128), WIDE),
            pltpu.SemaphoreType.DMA((18,)),
            pltpu.SemaphoreType.DMA((2, 2 * (depth + 3))),
            pltpu.SemaphoreType.DMA((2, 2 * (depth + 3))),
            pltpu.SemaphoreType.DMA((depth + 3,)),
            pltpu.SemaphoreType.DMA((depth + 3,)),
        ],
        compiler_params=pltpu.CompilerParams(
            collective_id=0, has_side_effects=True, vmem_limit_bytes=LIMIT
        ),
    )(seg, pad, pair, dec, enc, *extra)
    if gathers:
        whole, line, res = res[:2], res[2], res[3:]
        return whole, line, res
    return whole, None, res


def segment_ends(lengths, ends):
    total = jnp.int32(0)
    ends[0] = total
    for s in range(2 * SEGS):
        total = total + lengths[0, s]
        ends[s + 1] = total


def block_ranges(seg_s, first_seg, ends, off, src_count, block):
    at = pl.multiple_of(block * 128, 128)
    low = jnp.clip(ends[first_seg + seg_s[0, at]] - off, 0, src_count)
    high = jnp.clip(ends[first_seg + seg_s[0, at + 127] + 1] - off, 0, src_count)
    first = low // TILE
    return first, jnp.where(high > low, (high + TILE - 1) // TILE, first)


def key_bounds(segs, firsts, ends, off):
    rows = []
    for seg, first_seg in zip(segs, firsts):
        low = jnp.zeros(seg.shape, jnp.int32)
        high = jnp.zeros(seg.shape, jnp.int32)
        for s in range(SEGS):
            low = jnp.where(seg == s, ends[first_seg + s] - off, low)
            high = jnp.where(seg == s, ends[first_seg + s + 1] - off, high)
        rows += [low.astype(WIDE), high.astype(WIDE)]
    rows = jnp.concatenate(rows + [jnp.zeros((4, rows[0].shape[1]), WIDE)], axis=0)
    return transposed_rows(rows).astype(jnp.int32)


TILE = 256


def cross_forward_kernel(
    lengths, seg_so, seg_sp, seg_vo, seg_vp, q_own, q_other, kv, o_own, o_other, lse_own, lse_other,
    ends, cols_ref, top_ref, total_ref, acc_ref,
):
    tok_count, width = q_own.shape
    src_count = kv.shape[0]
    pairs = width // 128
    pos = lax.axis_index("src")
    off = pos * src_count
    firsts = (pos * SEGS, (1 - pos) * SEGS)
    segment_ends(lengths, ends)
    cols_ref[...] = key_bounds((seg_vo[...], seg_vp[...]), firsts, ends, off)
    for side, (q, o, lse_ref) in enumerate(((q_own, o_own, lse_own), (q_other, o_other, lse_other))):

        @pl.loop(0, tok_count // 128)
        def _(block):
            at = pl.ds(pl.multiple_of(block * 128, 128), 128)
            first, last = block_ranges((seg_so, seg_sp)[side], firsts[side], ends, off, src_count, block)
            low, high = cols_ref[at, 2 * side : 2 * side + 1], cols_ref[at, 2 * side + 1 : 2 * side + 2]
            top_ref[...] = jnp.full_like(top_ref, FILL)
            total_ref[...] = jnp.zeros_like(total_ref)
            acc_ref[...] = jnp.zeros_like(acc_ref)

            def one(t, carry):
                base = pl.multiple_of(t * TILE, TILE)
                keys = pl.ds(base, TILE)
                index = lanes((128, TILE)) + base
                allowed = twice((index >= low) & (index < high))
                for p in range(pairs):
                    cols = pl.ds(p * 128, 128)
                    k = kv[keys, cols]
                    v = kv[keys, pl.ds(width + p * 128, 128)]
                    scores = dot_nt(both_heads(q[at, cols]), k) * SCALE
                    scores = jnp.where(allowed, scores, FILL)
                    old = top_ref[p]
                    top = jnp.maximum(old, jnp.max(scores, axis=1, keepdims=True))
                    exps = jnp.where(allowed, jnp.exp(scores - top[:, 0:1]), 0.0)
                    fade = jnp.exp(old - top)
                    top_ref[p] = top
                    total_ref[p] = total_ref[p] * fade + jnp.sum(exps, axis=1, keepdims=True)
                    acc_ref[p] = acc_ref[p] * fade + dot(exps.astype(LOW), v)
                return carry

            lax.fori_loop(first, last, one, 0)
            lane = lanes((128, 128))
            stats = jnp.zeros((128, 128), WIDE)
            for p in range(pairs):
                total = total_ref[p]
                safe = jnp.where(total > 0.0, total, 1.0)
                o[at, pl.ds(p * 128, 128)] = join_heads(acc_ref[p] / safe).astype(LOW)
                lse = jnp.where(total > 0.0, top_ref[p] + jnp.log(safe), FILL)
                stats = jnp.where(lane == 2 * p, lse[:128], jnp.where(lane == 2 * p + 1, lse[128:], stats))
            lse_ref[:, at] = stats.T[0:8]


def cross_forward(lengths, seg_own, seg_other, q_own, q_other, kv):
    tok_count, width = q_own.shape
    heads = width // HD
    out = shape_of((tok_count, width), LOW)
    lse = shape_of((heads, tok_count), WIDE)
    return pl.pallas_call(
        cross_forward_kernel,
        name="cross_forward",
        out_shape=[out, out, lse, lse],
        in_specs=[SMEM] * 3 + [VMEM] * 5,
        out_specs=[VMEM] * 4,
        scratch_shapes=[pltpu.SMEM((32,), jnp.int32), pltpu.VMEM((tok_count, 128), jnp.int32)]
        + [pltpu.VMEM((width // 128, 256, 128), WIDE)] * 3,
        compiler_params=pltpu.CompilerParams(vmem_limit_bytes=LIMIT),
    )(lengths, seg_own, seg_other, seg_own, seg_other, q_own, q_other, kv)


def cross_backward_kernel(
    lengths, seg_so, seg_sp, seg_vo, seg_vp, q_own, q_other, g_own, g_other, st_own, st_other, kv,
    dq_own, dq_other, dkv, ends, cols_ref, acc, col_ref, dq_acc,
):
    tok_count, width = q_own.shape
    src_count = kv.shape[0]
    pairs = width // 128
    pos = lax.axis_index("src")
    off = pos * src_count
    firsts = (pos * SEGS, (1 - pos) * SEGS)
    segment_ends(lengths, ends)
    cols_ref[...] = key_bounds((seg_vo[...], seg_vp[...]), firsts, ends, off)
    acc[...] = jnp.zeros_like(acc)
    sides = ((q_own, g_own, st_own, dq_own), (q_other, g_other, st_other, dq_other))
    for side, (q, g, st, dq) in enumerate(sides):

        @pl.loop(0, tok_count // 128)
        def _(block):
            at = pl.ds(pl.multiple_of(block * 128, 128), 128)
            first, last = block_ranges((seg_so, seg_sp)[side], firsts[side], ends, off, src_count, block)
            low, high = cols_ref[at, 2 * side : 2 * side + 1], cols_ref[at, 2 * side + 1 : 2 * side + 2]
            dq_acc[...] = jnp.zeros_like(dq_acc)
            col_ref[...] = jnp.concatenate([st[:, at], jnp.zeros((112, 128), WIDE)], axis=0).T

            def one(t, carry):
                base = pl.multiple_of(t * TILE, TILE)
                keys = pl.ds(base, TILE)
                index = lanes((128, TILE)) + base
                allowed = twice((index >= low) & (index < high))
                for p in range(pairs):
                    cols = pl.ds(p * 128, 128)
                    vals = pl.ds(width + p * 128, 128)
                    k = kv[keys, cols]
                    v = kv[keys, vals]
                    qs = both_heads(q[at, cols])
                    gs = both_heads(g[at, cols])
                    lse = jnp.concatenate([col_ref[:, 2 * p : 2 * p + 1], col_ref[:, 2 * p + 1 : 2 * p + 2]], axis=0)
                    delta = jnp.concatenate(
                        [col_ref[:, 8 + 2 * p : 9 + 2 * p], col_ref[:, 9 + 2 * p : 10 + 2 * p]], axis=0
                    )
                    scores = dot_nt(qs, k) * SCALE
                    probs = jnp.exp(jnp.where(allowed, scores - lse, FILL))
                    gscores = (probs * (dot_nt(gs, v) - delta)).astype(LOW)
                    dq_acc[:, cols] = dq_acc[:, cols] + join_heads(dot(gscores, k))
                    acc[keys, cols] = acc[keys, cols] + dot_tn(gscores, qs)
                    acc[keys, vals] = acc[keys, vals] + dot_tn(probs.astype(LOW), gs)
                return carry

            lax.fori_loop(first, last, one, 0)
            dq[at, :] = (dq_acc[...] * SCALE).astype(dq.dtype)

    @pl.loop(0, src_count // 256)
    def _(t):
        at = pl.ds(pl.multiple_of(t * 256, 256), 256)
        dkv[at, 0:width] = (acc[at, 0:width] * SCALE).astype(LOW)
        dkv[at, width : 2 * width] = acc[at, width : 2 * width].astype(LOW)


def cross_backward(lengths, seg_own, seg_other, q_own, q_other, g_own, g_other, st_own, st_other, kv):
    tok_count, width = q_own.shape
    src_count = kv.shape[0]
    return pl.pallas_call(
        cross_backward_kernel,
        name="cross_backward",
        out_shape=[
            shape_of((tok_count, width), WIDE),
            shape_of((tok_count, width), LOW),
            shape_of((src_count, 2 * width), LOW),
        ],
        in_specs=[SMEM] * 3 + [VMEM] * 9,
        out_specs=[VMEM] * 3,
        scratch_shapes=[
            pltpu.SMEM((32,), jnp.int32),
            pltpu.VMEM((tok_count, 128), jnp.int32),
            pltpu.VMEM((src_count, 2 * width), WIDE),
            pltpu.VMEM((128, 128), WIDE),
            pltpu.VMEM((128, width), WIDE),
        ],
        compiler_params=pltpu.CompilerParams(vmem_limit_bytes=LIMIT),
    )(lengths, seg_own, seg_other, seg_own, seg_other, q_own, q_other, g_own, g_other, st_own, st_other, kv)


def merge_all(parts):
    top = parts[0][0:1]
    for part in parts[1:]:
        top = jnp.maximum(top, part[0:1])
    total = sum(jnp.exp(part[0:1] - top) for part in parts)
    rest = sum(part for part in parts)
    return jnp.where(rows_of(rest.shape) == 0, top + jnp.log(total), rest)


def middle_kernel(depth, split, *refs):
    (
        seg, pad, labels, counts, positions, targets, w_vocab, after_self, o_own, o_other, lse_own, lse_other,
        gs,
    ) = refs[:13]
    parts = refs[13 : 13 + (4 if split else 1)]
    refs = refs[13 + len(parts) :]
    sums = refs[:len(parts)]
    refs = refs[len(parts) :]
    (
        block_out, state_out, g_own, g_other, st_own, st_other, small_rows, small_cols, grad_vocab, token_out, loss_out,
    ) = refs[:11]
    (
        wm, eb, eb_got, w_s, got_o, got_lse, cross_o, cross_low, ac, bs, n3, act, slope, gpre, head,
        lt, gt, pb, rb, got_rc, got_rq, got_rz, st_c, st_q, st_z, gh, load_sem, send, recv,
    ) = refs[11:]
    tok_count, width = after_self.shape
    hidden = act.shape[1]
    masked = positions.shape[1]
    vocab_local = w_vocab.shape[0]
    everyone = depth * 8
    me = Place(depth)
    z, x, c, y = me.z, me.x, me.c, me.y
    greet(me.others() + [me.across_x(), me.across_y(), me.across_both(), me.across_core()])
    used = [0]

    def push(src, dst, peer):
        k = used[0]
        used[0] += 1
        copy = remote(src, dst, send.at[k], recv.at[k], peer)
        copy.start()
        return copy

    pending = []

    def arrive(copies):
        for copy in copies:
            copy.wait_recv()
        pending.extend(copies)

    swap = [push(o_other, got_o, me.across_y()), push(lse_other, got_lse, me.across_y())]
    loads = []

    def load(src, dst):
        copy = pltpu.make_async_copy(src, dst, load_sem.at[len(loads)])
        copy.start()
        loads.append(copy)

    load(gs, w_s)
    shared = []
    if split:
        spots = ((x, y), (1 - x, y), (x, 1 - y), (1 - x, 1 - y))
        for part, (px, py) in zip(parts, spots):
            load(part, wm.at[:, px, c, py])
            shared.append(push(part, wm.at[:, px, c, py], me.across_core()))
    else:
        load(parts[0], wm)

    def cut(lo, hi):
        value = wm[:, :, :, :, lo:hi] if split else wm[:, lo:hi]
        return value.reshape((-1, BLOCK))

    def put(lo, value, first=0, last=None, cols=slice(0, BLOCK)):
        groups, rows, wide = value.shape
        last = depth if last is None else last
        if split:
            eb[first:last, :, :, :, lo : lo + rows, cols] = value.reshape((last - first, 2, 2, 2, rows, wide))
        else:
            step = eb.shape[0] // depth
            eb[first * step : last * step, lo : lo + rows, cols] = value

    segments = seg[...].astype(WIDE)
    keep = 1.0 - pad[...].astype(WIDE)
    lane_row = lanes((1, tok_count))
    inside = lane_row < tok_count - 1

    def following(row):
        return pltpu.roll(jnp.concatenate([row, jnp.zeros((7, tok_count), WIDE)], axis=0), tok_count - 1, 1)[0:1]

    follows = inside & (following(segments) == segments) & (keep > 0.5) & (following(keep) > 0.5)
    valid = jnp.where(follows, 1.0, 0.0)
    rows = [keep, valid, labels[...].astype(WIDE), counts[...].astype(WIDE)]
    columns = transposed_rows(jnp.concatenate(rows + [jnp.zeros((4, tok_count), WIDE)], axis=0))
    col_keep, col_valid = columns[:, 0:1], columns[:, 1:2]
    col_label, col_count = columns[:, 2:3], columns[:, 3:4].astype(jnp.int32)

    for copy in loads:
        copy.wait()
    arrive(shared)
    table = w_s[...].reshape((-1, 128)).astype(WIDE).T

    arrive(swap)
    top = jnp.maximum(lse_own[...], got_lse[...])
    lse = top + jnp.log(jnp.exp(lse_own[...] - top) + jnp.exp(got_lse[...] - top))
    shares = jnp.concatenate([jnp.exp(lse_own[...] - lse), jnp.exp(got_lse[...] - lse)], axis=0)
    shares = transposed_rows(shares)
    low_half = lanes((tok_count, 128)) < HD
    for p in range(width // 128):
        at = slice(p * 128, (p + 1) * 128)
        share_own = jnp.where(low_half, shares[:, 2 * p : 2 * p + 1], shares[:, 2 * p + 1 : 2 * p + 2])
        share_got = jnp.where(low_half, shares[:, 8 + 2 * p : 9 + 2 * p], shares[:, 9 + 2 * p : 10 + 2 * p])
        mixed = o_own[:, at].astype(WIDE) * share_own + got_o[:, at].astype(WIDE) * share_got
        cross_o[:, at] = mixed
        cross_low[:, at] = mixed.astype(LOW)
    weight_co = cut(0, 16)
    after_cross = after_self[...] + dot(cross_low[...], weight_co)
    ac[...] = after_cross
    n3[...] = (normalised(after_cross)[0] * table[2:3] + table[6:7]).astype(LOW)
    bs[...] = after_cross
    blocks = hidden // BLOCK
    flat_fo = cut(80, 144)
    for j in range(blocks):
        at = slice(j * BLOCK, (j + 1) * BLOCK)
        pre = dot(n3[...], cut(16 + 16 * j, 32 + 16 * j))
        square = pre * pre
        bent = jnp.tanh(GELU * pre * (1.0 + CUBIC * square))
        half = 0.5 * (1.0 + bent)
        act[:, at] = (pre * half).astype(LOW)
        slope[:, at] = half + 0.5 * pre * (1.0 - bent * bent) * (GELU * (1.0 + 3.0 * CUBIC * square))
        bs[...] = bs[...] + dot(act[:, at], flat_fo[at])
    state = bs[...]
    block_out[...] = state.astype(LOW)
    head_in = (normalised(state)[0] * table[3:4] + table[7:8]).astype(LOW)
    head[...] = head_in

    picker = (positions[...] == rows_of((tok_count, masked))).astype(LOW)
    picked = dot_tn(picker, head_in).astype(LOW)
    kept = dot(jnp.concatenate([keep, jnp.zeros((7, tok_count), WIDE)], axis=0).astype(LOW), picker)
    code = jnp.where(kept[0:1] > 0.5, targets[...] + 1, 0)
    digits = jnp.concatenate([code >> 8, code & 255, jnp.zeros((6, masked), jnp.int32)], axis=0)
    digits = dot_tn(digits.astype(WIDE).astype(LOW), (rows_of((8, 128)) == lanes((8, 128))).astype(LOW)).astype(LOW)
    pb[z, x, c, y, :, 0:width] = picked
    pb[z, x, c, y, :, width : width + 128] = digits
    mine = pb.at[z, x, c, y]
    flight = [push(mine, mine, peer) for peer in me.others()]

    classes = BLOCK // 2
    flat_in = cut(144, 160).reshape((-1, 16, BLOCK))
    flat_in = jnp.concatenate([flat_in[:, :, :classes], flat_in[:, :, classes:]], axis=1).reshape((-1, classes))
    w_one, w_two = flat_in[:width], flat_in[width:]
    token_row = rows_of((tok_count, classes))
    ahead = pltpu.roll(dot(head_in, w_two), tok_count - 1, 0)
    logits = dot(head_in, w_one) + jnp.where(token_row == tok_count - 1, 0.0, ahead)
    top = jnp.max(logits, axis=1, keepdims=True)
    exps = jnp.exp(logits - top)
    total = jnp.sum(exps, axis=1, keepdims=True)
    hits = lanes((tok_count, classes)) == col_count
    entropy = top + jnp.log(total) - jnp.sum(jnp.where(hits, logits, 0.0), axis=1, keepdims=True)
    loss_col = col_valid * entropy
    grads = col_valid * (exps * (1.0 / total) - jnp.where(hits, 1.0, 0.0))
    g_insert = grads.astype(LOW)
    before = pltpu.roll(g_insert.astype(WIDE), 1, 0)
    g_before = jnp.where(token_row == 0, 0.0, before).astype(LOW)

    arrive(flight)
    column = pb.at[:, x, c, y]
    flight = [push(column, column, peer) for peer in (me.across_x(), me.across_y(), me.across_both())]

    flat_s = w_s[...].reshape((-1, 128))
    two = dot(head_in, flat_s)
    l_zero, l_one = two[:, 16:17], two[:, 17:18]
    top = jnp.maximum(l_zero, l_one)
    e_zero, e_one = jnp.exp(l_zero - top), jnp.exp(l_one - top)
    total = e_zero + e_one
    is_one = col_label > 0.5
    loss_col = loss_col + col_keep * (top + jnp.log(total) - jnp.where(is_one, l_one, l_zero))
    d_zero = col_keep * (e_zero / total - jnp.where(is_one, 0.0, 1.0))
    d_one = col_keep * (e_one / total - jnp.where(is_one, 1.0, 0.0))
    lane = lanes((tok_count, 128))
    g_delete = jnp.where(lane == 16, d_zero, jnp.where(lane == 17, d_one, 0.0)).astype(LOW)
    gh[...] = dot_nt(g_delete, flat_s) + dot_nt(g_insert, w_one) + dot_nt(g_before, w_two)
    arrive(flight)
    plane = pb.at[:, :, c, :]
    flight = [push(plane, plane, me.across_core())]
    small_cols[...] = dot_tn(head_in, g_delete)
    for k, grad in enumerate((g_insert, g_before)):
        pairs = dot_tn(head_in, grad).astype(LOW).reshape((-1, 2, 16, classes))
        for side in range(2):
            cols = slice(side * classes, (side + 1) * classes)
            put(144, pairs[:, side], k * (depth // 2), (k + 1) * (depth // 2), cols)
    arrive(flight)

    gathered = pb[...].reshape((-1, width + 128))
    rows_all = gathered[:, 0:width]
    numbers = gathered[:, width : width + 128].astype(WIDE).T
    code = numbers[0:1] * 256.0 + numbers[1:2]
    weight = jnp.where(code > 0.5, 1.0, 0.0)
    count = rows_all.shape[0]
    pos = lax.axis_index(BOTH)
    place = rows_of((vocab_local, count)) + pos * vocab_local
    hits = place == (code.astype(jnp.int32) - 1)
    lt[...] = dot_nt(w_vocab[...], rows_all)
    logits = lt[...]
    top = jnp.max(logits, axis=0, keepdims=True)
    total = jnp.sum(jnp.exp(logits - top), axis=0, keepdims=True)
    chosen = jnp.sum(jnp.where(hits, logits, 0.0), axis=0, keepdims=True)
    loss_here = jnp.sum(loss_col, axis=0, keepdims=True)
    stat = jnp.concatenate(
        [top + jnp.log(total), chosen, jnp.broadcast_to(loss_here, (1, count)), jnp.zeros((5, count), WIDE)], axis=0
    )
    st_c[0] = stat
    flight = [push(st_c.at[0], st_c.at[1], me.across_core())]
    arrive(flight)
    st_q[x, y] = merge_all([st_c[0], st_c[1]])
    spot = st_q.at[x, y]
    flight = [push(spot, spot, peer) for peer in (me.across_x(), me.across_y(), me.across_both())]
    arrive(flight)
    st_z[z] = merge_all([st_q[0, 0], st_q[0, 1], st_q[1, 0], st_q[1, 1]])
    flight = [push(st_z.at[z], st_z.at[z], peer) for peer in me.others()]
    arrive(flight)
    stat = merge_all([st_z[k] for k in range(depth)])
    tokens = weight * (stat[0:1] - stat[1:2])
    mine = rows_of((masked, count)) + pos * masked == lanes((masked, count))
    own = jnp.sum(jnp.where(mine, tokens, 0.0), axis=1, keepdims=True)
    token_out[...] = jnp.sum(
        jnp.where(rows_of((masked, masked)) == lanes((masked, masked)), own, 0.0), axis=0, keepdims=True
    )
    loss = (stat[2:3, 0:128] + jnp.sum(tokens, axis=1, keepdims=True)) * (1.0 / (tok_count * everyone))
    loss_out[...] = loss[:, 0:1]
    gt[...] = (weight * (jnp.exp(lt[...] - stat[0:1]) - jnp.where(hits, 1.0, 0.0))).astype(LOW)

    rb[...] = dot_tn(gt[...], w_vocab[...]).astype(LOW).reshape(rb.shape)
    flight = [push(rb.at[:, :, 1 - c], got_rc, me.across_core())]
    scale = (tok_count * everyone) ** (-0.5)
    grad_vocab[...] = dot(gt[...], rows_all) * scale
    arrive(flight)
    got_rc[...] = (rb[:, :, c].astype(WIDE) + got_rc[...].astype(WIDE)).astype(LOW)
    flight = [
        push(got_rc.at[:, 1 - x, y], got_rq.at[0], me.across_x()),
        push(got_rc.at[:, x, 1 - y], got_rq.at[1], me.across_y()),
        push(got_rc.at[:, 1 - x, 1 - y], got_rq.at[2], me.across_both()),
    ]
    arrive(flight)
    line = got_rc[:, x, y].astype(WIDE)
    for k in range(3):
        line = line + got_rq[k].astype(WIDE)
    got_rq[3] = line.astype(LOW)
    flight = [
        push(got_rq.at[3, lax.rem(z + k, depth)], got_rz.at[k - 1], me.along(k)) for k in range(1, depth)
    ]
    arrive(flight)
    grad_picked = got_rq[3, z].astype(WIDE)
    for k in range(1, depth):
        grad_picked = grad_picked + got_rz[k - 1].astype(WIDE)
    coarse = grad_picked.astype(LOW)
    fine = (grad_picked - coarse.astype(WIDE)).astype(LOW)
    grad_head = gh[...] + dot(picker, coarse) + dot(picker, fine)

    grad_block, gain_3, bias_3 = norm_back(bs[...], table[3:4], grad_head)
    bs[...] = grad_block
    g_ffn = grad_block.astype(LOW)
    gh[...] = jnp.zeros_like(gh)
    for j in range(blocks):
        at = slice(j * BLOCK, (j + 1) * BLOCK)
        gpre[:, at] = (dot_nt(g_ffn, flat_fo[at]) * slope[:, at]).astype(LOW)
        gh[...] = gh[...] + dot_nt(gpre[:, at], cut(16 + 16 * j, 32 + 16 * j))
    back, gain_2, bias_2 = norm_back(ac[...], table[2:3], gh[...])
    grad_state = grad_block + back
    state_out[...] = grad_state
    g_cross = grad_state.astype(LOW)
    g_attn = dot_nt(g_cross, weight_co).astype(LOW)
    g_own[...] = g_attn
    deltas = jnp.zeros((tok_count, 128), WIDE)
    for p in range(width // 128):
        at = slice(p * 128, (p + 1) * 128)
        product = g_attn[:, at].astype(WIDE) * cross_o[:, at]
        first = jnp.sum(jnp.where(low_half, product, 0.0), axis=1, keepdims=True)
        second = jnp.sum(jnp.where(low_half, 0.0, product), axis=1, keepdims=True)
        deltas = jnp.where(lane == 2 * p, first, jnp.where(lane == 2 * p + 1, second, deltas))
    st_own[...] = jnp.concatenate([lse, deltas.T[0:8]], axis=0)
    swap = [push(g_own, g_other, me.across_y()), push(st_own, st_other, me.across_y())]

    for j in range(blocks):
        at = slice(j * BLOCK, (j + 1) * BLOCK)
        grad = dot_tn(act[:, at], g_ffn).astype(LOW)
        put(80, grad.reshape((-1, 64, BLOCK)), j * depth // blocks, (j + 1) * depth // blocks)
        grad = dot_tn(n3[...], gpre[:, at]).astype(LOW)
        put(16 + 16 * j, grad.reshape((-1, 16, BLOCK)))
    put(0, dot_tn(cross_low[...], g_cross).astype(LOW).reshape((-1, 16, BLOCK)))
    if split:
        halves = [push(eb.at[:, :, 1 - c], eb_got, me.across_core())]
    small_rows[...] = jnp.concatenate([gain_2, gain_3, bias_2, bias_3, jnp.zeros((4, width), WIDE)], axis=0)
    if split:
        arrive(halves)
        for out, (px, py) in zip(sums, spots):

            @pl.loop(0, depth)
            def _(zz):
                total = eb[zz, px, c, py].astype(WIDE) + eb_got[zz, px, py].astype(WIDE)
                out[zz] = total.astype(LOW)

    else:
        sums[0][...] = eb[...]
    arrive(swap)
    for copy in pending:
        copy.wait_send()


def middle_part(depth, split, seg, pad, labels, counts, positions, targets, w_vocab, after_self, attended, gs, parts):
    tok_count, width = after_self.shape
    hidden = 4 * BLOCK
    vocab_local = w_vocab.shape[0]
    everyone = depth * 8
    masked = positions.shape[1]
    count = masked * everyone
    sharded = (depth, 2, 2, 2)
    lead = sharded if split else (BLOCK // 16,)
    own = lead[:1] if split else lead
    sharded = (depth, 2, 2, 2)
    outs = [(shape_of(own + (160, BLOCK), LOW), VMEM)] * len(parts)
    outs += [
        (shape_of((tok_count, width), LOW), VMEM),
        (shape_of((tok_count, width), WIDE), VMEM),
        (shape_of((tok_count, width), LOW), VMEM),
        (shape_of((tok_count, width), LOW), ANY),
        (shape_of((16, tok_count), WIDE), VMEM),
        (shape_of((16, tok_count), WIDE), ANY),
        (shape_of((8, width), WIDE), VMEM),
        (shape_of((width, 128), WIDE), VMEM),
        (shape_of((vocab_local, width), WIDE), VMEM),
        (shape_of((1, masked), WIDE), VMEM),
        (shape_of((1, 1), WIDE), VMEM),
    ]
    copies = 9 + 2 * (depth - 1) + 3 + 1 + 1 + 3 + 1 + 3 + (depth - 1)
    return pl.pallas_call(
        partial(middle_kernel, depth, split),
        name="middle_part",
        out_shape=[o for o, _ in outs],
        in_specs=[VMEM] * 12 + [ANY] * (1 + len(parts)),
        out_specs=[s for _, s in outs],
        scratch_shapes=[
            pltpu.VMEM(lead + (160, BLOCK), LOW),
            pltpu.VMEM(lead + (160, BLOCK), LOW),
            pltpu.VMEM(((depth, 2, 2) if split else (1,)) + (160, BLOCK), LOW),
            pltpu.VMEM(gs.shape, LOW),
            pltpu.VMEM((tok_count, width), LOW),
            pltpu.VMEM((8, tok_count), WIDE),
            pltpu.VMEM((tok_count, width), WIDE),
            pltpu.VMEM((tok_count, width), LOW),
            pltpu.VMEM((tok_count, width), WIDE),
            pltpu.VMEM((tok_count, width), WIDE),
            pltpu.VMEM((tok_count, width), LOW),
            pltpu.VMEM((tok_count, hidden), LOW),
            pltpu.VMEM((tok_count, hidden), WIDE),
            pltpu.VMEM((tok_count, hidden), LOW),
            pltpu.VMEM((tok_count, width), LOW),
            pltpu.VMEM((vocab_local, count), WIDE),
            pltpu.VMEM((vocab_local, count), LOW),
            pltpu.VMEM(sharded + (masked, width + 128), LOW),
            pltpu.VMEM(sharded + (masked, width), LOW),
            pltpu.VMEM((depth, 2, 2, masked, width), LOW),
            pltpu.VMEM((4, depth, masked, width), LOW),
            pltpu.VMEM((max(depth - 1, 1), masked, width), LOW),
            pltpu.VMEM((2, 8, count), WIDE),
            pltpu.VMEM((2, 2, 8, count), WIDE),
            pltpu.VMEM((depth, 8, count), WIDE),
            pltpu.VMEM((tok_count, width), WIDE),
            pltpu.SemaphoreType.DMA((9,)),
            pltpu.SemaphoreType.DMA((copies + depth,)),
            pltpu.SemaphoreType.DMA((copies + depth,)),
        ],
        compiler_params=pltpu.CompilerParams(
            collective_id=1, has_side_effects=True, vmem_limit_bytes=LIMIT
        ),
    )(seg, pad, labels, counts, positions, targets, w_vocab, after_self, *attended, gs, *parts)


def self_backward_start(dk, dv):
    dk[...] = jnp.zeros_like(dk)
    dv[...] = jnp.zeros_like(dv)


def self_backward(blocks, qkv, out, lse_ref, g_ref, dqkv, dk, dv, row_seg, row_keep, col_seg):
    tok_count, width = out.shape
    first, last = blocks
    pairs = width // 128

    def one(t, carry):
        block, pair = first + t // pairs, lax.rem(t, pairs)
        base = pl.multiple_of(pair * 128, 128)
        cols = pl.ds(base, 128)
        at = pl.ds(pl.multiple_of(block * 128, 128), 128)
        low = self_window(block, tok_count)
        keys = pl.ds(low, 384)
        q = both_heads(qkv[at, cols] * SCALE)
        k = qkv[keys, pl.ds(pl.multiple_of(base + width, 128), 128)]
        v = qkv[keys, pl.ds(pl.multiple_of(base + 2 * width, 128), 128)]
        g = both_heads(g_ref[at, cols])
        delta = jnp.sum(g.astype(WIDE) * twice(out[at, cols].astype(WIDE)), axis=1, keepdims=True)
        lane = lanes((128, 128))
        stats = lse_ref[at, :]
        lse_low = jnp.sum(jnp.where(lane == 2 * pair, stats, 0.0), axis=1, keepdims=True)
        lse_high = jnp.sum(jnp.where(lane == 2 * pair + 1, stats, 0.0), axis=1, keepdims=True)
        lse = jnp.concatenate([lse_low, lse_high], axis=0)
        allowed = self_mask(row_seg, row_keep, col_seg, block, low)
        scores = dot_nt(q, k)
        probs = jnp.exp(jnp.where(twice(allowed), scores - lse, FILL))
        gscores = (probs * (dot_nt(g, v) - delta)).astype(LOW)
        dqkv[at, cols] = (join_heads(dot(gscores, k)) * SCALE).astype(LOW)
        dk[keys, cols] = dk[keys, cols] + dot_tn(gscores, q)
        dv[keys, cols] = dv[keys, cols] + dot_tn(probs.astype(LOW), g)
        return carry

    lax.fori_loop(0, (last - first) * pairs, one, 0)


def self_backward_end(dqkv, dk, dv):
    width = dk.shape[1]
    dqkv[:, width : 2 * width] = dk[...].astype(LOW)
    dqkv[:, 2 * width : 3 * width] = dv[...].astype(LOW)


def reduce_steps(me, chunks, send, recv):
    z, x, c, y = me.z, me.x, me.c, me.y
    depth = me.depth
    count = len(chunks)
    started = [[None] * 3 for _ in chunks]
    used = [0] * count

    def launch(k, stage):
        copies = []

        def push(src, dst, peer):
            slot = used[k]
            used[k] += 1
            copy = remote(src, dst, send.at[k, slot], recv.at[k, slot], peer)
            copy.start()
            copies.append(copy)

        for src, got_c, got_q, got_z, at, put in chunks[k]:
            if stage == 0:
                push(src.at[:, :, 1 - c, :, at], got_c.at[:, :, :, at], me.across_core())
            elif stage == 1:
                push(got_c.at[:, 1 - x, y, at], got_q.at[0, :, at], me.across_x())
                push(got_c.at[:, x, 1 - y, at], got_q.at[1, :, at], me.across_y())
                push(got_c.at[:, 1 - x, 1 - y, at], got_q.at[2, :, at], me.across_both())
            else:
                for j in range(1, depth):
                    push(got_c.at[lax.rem(z + j, depth), x, y, at], got_z.at[j - 1, at], me.along(j))
        started[k][stage] = copies

    def absorb(k, stage):
        for copy in started[k][stage]:
            copy.wait_recv()
        for src, got_c, got_q, got_z, at, put in chunks[k]:
            if stage == 0:

                @pl.loop(0, depth)
                def _(zz):
                    for xx in range(2):
                        for yy in range(2):
                            total = src[zz, xx, c, yy, at].astype(WIDE) + got_c[zz, xx, yy, at].astype(WIDE)
                            got_c[zz, xx, yy, at] = total.astype(LOW)

            elif stage == 1:

                @pl.loop(0, depth)
                def _(zz):
                    total = got_c[zz, x, y, at].astype(WIDE)
                    for k in range(3):
                        total = total + got_q[k, zz, at].astype(WIDE)
                    got_c[zz, x, y, at] = total.astype(LOW)

            else:
                total = got_c[z, x, y, at].astype(WIDE)
                for j in range(1, depth):
                    total = total + got_z[j - 1, at].astype(WIDE)
                put(total)

    for step in range(count + 3):
        for stage in range(3, -1, -1):
            k = step - stage
            if not 0 <= k < count:
                continue
            if stage > 0:
                absorb(k, stage - 1)
            if stage < 3:
                launch(k, stage)
        yield step
    for stages in started:
        for copies in stages:
            for copy in copies:
                copy.wait_send()


def last_kernel(depth, reduces, *refs):
    (pair, seg, pad, dkv, enc, dq_own, dq_other) = refs[:7]
    held = refs[7:15]
    (small_rows, small_cols, ga_in, gs_in) = refs[15:19]
    refs = refs[19:]
    if reduces:
        parts, refs = refs[:4], refs[4:]
    grad_input, grad_enc = refs[:2]
    refs = refs[2:]
    outs = refs[:9] if reduces else refs[:2]
    refs = refs[9:] if reduces else refs[2:]
    (start, one, qkv, low, lse, after, two, gstate) = refs[:8]
    (ga, gs, got_dq, g_attn, dqkv, dk, dv, row_seg, row_keep, col_seg, load_sem, sw_send, sw_recv) = refs[8:21]
    refs = refs[21:]
    tok_count, width = dq_own.shape
    src_count = enc.shape[0]
    everyone = depth * 8
    me = Place(depth)
    scale = (tok_count * everyone) ** (-0.5)
    loads = []
    for src, dst in [(gs_in, gs), (ga_in, ga)] + list(zip(held, (start, one, qkv, low, lse, after, two, gstate))):
        copy = pltpu.make_async_copy(src, dst, load_sem.at[len(loads)])
        copy.start()
        loads.append(copy)
    if reduces:
        greet(me.others() + [me.across_x(), me.across_y(), me.across_both(), me.across_core()])
    else:
        greet([me.across_y()])
    halves = 2
    span = tok_count // halves
    swaps = []
    for k in range(halves):
        at = pl.ds(k * span, span)
        swaps.append(remote(dq_other.at[at], got_dq.at[at], sw_send.at[k], sw_recv.at[k], me.across_y()))
        swaps[-1].start()

    if reduces:
        (late, late_s, ez, ez_got, c_a, c_s, q_a, q_s, z_a, z_s, ez_send, ez_recv, send, recv) = refs
        (o_qkv, o_so, o_cq, o_kv, o_co, o_fi, o_fo, o_in, o_s) = outs

        def put_kv(total):
            o_kv[:, 0:BLOCK] = total[0:16] * scale
            o_kv[:, BLOCK : 2 * BLOCK] = total[16:32] * scale

        def put_mid(total):
            o_so[...] = total[0:16] * scale
            o_cq[...] = total[16:32] * scale

        def put_qkv(total):
            for k in range(3):
                o_qkv[:, k * BLOCK : (k + 1) * BLOCK] = total[16 * k : 16 * (k + 1)] * scale

        def put_s(total):
            o_s[...] = total * scale

        def rows(lo, hi, put):
            return (late, c_a, q_a, z_a, pl.ds(lo, hi - lo), put)

        chunks = [
            [rows(KV, EARLY, put_kv)],
            [],
            [rows(SO, KV, put_mid)],
            [rows(QKV, SO, put_qkv), (late_s, c_s, q_s, z_s, pl.ds(0, 16), put_s)],
        ]

        @pl.loop(0, depth)
        def _(zz):
            total = parts[0][zz].astype(WIDE)
            for part in parts[1:]:
                total = total + part[zz].astype(WIDE)
            ez[zz] = total.astype(LOW)

        along = []
        for k in range(1, depth):
            to = lax.rem(me.z + k, depth)
            along.append(remote(ez.at[to], ez_got.at[k - 1], ez_send.at[k - 1], ez_recv.at[k - 1], me.along(k)))
            along[-1].start()

        def settle():
            for copy in along:
                copy.wait()
            total = ez[me.z].astype(WIDE)
            for k in range(depth - 1):
                total = total + ez_got[k].astype(WIDE)
            total = total * scale
            o_co[...] = total[0:16]
            for k in range(4):
                o_fi[:, k * BLOCK : (k + 1) * BLOCK] = total[16 + 16 * k : 32 + 16 * k]
            o_fo[...] = total[80:144]
            half = BLOCK // 2
            for k in range(2):
                o_in[16 * k : 16 * (k + 1)] = total[144:160, half * k : half * (k + 1)]

        steps = reduce_steps(me, chunks, send, recv)

        def keep(lo, value):
            late[:, :, :, :, lo : lo + 16] = value.astype(LOW).reshape(late.shape[:4] + (16, BLOCK))

        def keep_small(value):
            late_s[...] = value.astype(LOW).reshape(late_s.shape)
    else:
        steps = iter(())
        o_late, o_small = outs

        def keep(lo, value):
            o_late[:, lo : lo + 16] = value.astype(LOW).reshape((-1, 16, BLOCK))

        def keep_small(value):
            o_small[...] = value

    def advance():
        return next(steps, None)

    onehot = token_numbers(seg, pad, pair, row_seg, row_keep, col_seg)
    cut = cutter(ga)
    keep(KV, dot_tn(enc[...], dkv[:, 0:width]))
    keep(KV + 16, dot_tn(enc[...], dkv[:, width : 2 * width]))
    advance()
    for copy in loads:
        copy.wait()
    table = cutter(gs)(0, gs.shape[-2]).astype(WIDE).T
    gains = biases = 0.0
    blocks = span // 128
    self_backward_start(dk, dv)
    for k in range(halves):
        at = pl.ds(k * span, span)
        swaps[k].wait()
        g_query = (dq_own[at, :] + got_dq[at, :].astype(WIDE)).astype(LOW)
        got_dq[at, :] = g_query
        back, gain_1, bias_1 = norm_back(after[at, :], table[1:2], dot_nt(g_query, cut(CQ, KV)))
        gains, biases = gains + gain_1, biases + bias_1
        state = gstate[at, :] + back
        gstate[at, :] = state
        g_attn[at, :] = dot_nt(state.astype(LOW), cut(SO, CQ)).astype(LOW)
        if k == halves - 1:
            advance()
        self_backward((k * blocks, (k + 1) * blocks), qkv, low, lse, g_attn, dqkv, dk, dv, row_seg, row_keep, col_seg)
    self_backward_end(dqkv, dk, dv)
    keep(CQ, dot_tn(two[...], got_dq[...]))
    keep(SO, dot_tn(low[...], gstate[...].astype(LOW)))
    advance()
    for k in range(3):
        keep(QKV + 16 * k, dot_tn(one[...], dqkv[:, k * width : (k + 1) * width]))
    upstream = dot_nt(dqkv[:, 0:width], cut(QKV, QKV + 16))
    upstream = upstream + dot_nt(dqkv[:, width : 2 * width], cut(QKV + 16, QKV + 32))
    upstream = upstream + dot_nt(dqkv[:, 2 * width : 3 * width], cut(QKV + 32, SO))
    back, gain_0, bias_0 = norm_back(start[...], table[0:1], upstream)
    grad_start = gstate[...] + back
    grad_input[...] = grad_start.astype(LOW)
    coarse = grad_start.astype(LOW)
    fine = (grad_start - coarse.astype(WIDE)).astype(LOW)
    g_table = (dot_tn(onehot, coarse) + dot_tn(onehot, fine))[8:16]
    mid = small_rows[...]
    stacked = jnp.concatenate([gain_0, gains, mid[0:2], bias_0, biases, mid[2:4], g_table], axis=0)
    keep_small(transposed_rows(stacked) + small_cols[...])
    advance()
    w_key, w_val = cut(KV, KV + 16), cut(KV + 16, EARLY)
    span = src_count // 4
    for k in range(4):
        at = pl.ds(k * span, span)
        grads = dot_nt(dkv[at, 0:width], w_key) + dot_nt(dkv[at, width : 2 * width], w_val)
        grad_enc[at, :] = grads.astype(LOW)
        if k == 0:
            advance()
    advance()
    if reduces:
        settle()
    for _ in steps:
        pass


def last_part(depth, reduces, pair, seg, pad, dq_own, dq_other, dkv, enc, kept, gstate, grads, whole):
    tok_count, width = dq_own.shape
    src_count = enc.shape[0]
    ga, gs = whole
    parts, small_rows, small_cols = grads
    everyone = depth * 8
    rows = BLOCK // everyone
    sharded = (depth, 2, 2, 2)
    held = (*kept, gstate)
    outs = [shape_of((tok_count, width), LOW), shape_of((src_count, width), LOW)]
    scratch = [pltpu.VMEM(a.shape, a.dtype) for a in held]
    scratch += [
        pltpu.VMEM(ga.shape, LOW),
        pltpu.VMEM(gs.shape, LOW),
        pltpu.VMEM((tok_count, width), LOW),
        pltpu.VMEM((tok_count, width), LOW),
        pltpu.VMEM((tok_count, 3 * width), LOW),
        pltpu.VMEM((tok_count, width), WIDE),
        pltpu.VMEM((tok_count, width), WIDE),
        pltpu.VMEM((1, tok_count), WIDE),
        pltpu.VMEM((1, tok_count), WIDE),
        pltpu.VMEM((tok_count, 128), WIDE),
        pltpu.SemaphoreType.DMA((10,)),
        pltpu.SemaphoreType.DMA((2,)),
        pltpu.SemaphoreType.DMA((2,)),
    ]
    if reduces:
        shapes = [(EARLY, BLOCK), (16, 128)]
        outs += [
            shape_of((rows, 3 * BLOCK), WIDE),
            shape_of((rows, BLOCK), WIDE),
            shape_of((rows, BLOCK), WIDE),
            shape_of((rows, 2 * BLOCK), WIDE),
            shape_of((rows, BLOCK), WIDE),
            shape_of((rows, 4 * BLOCK), WIDE),
            shape_of((4 * rows, BLOCK), WIDE),
            shape_of((2 * rows, BLOCK // 2), WIDE),
            shape_of((rows, 128), WIDE),
        ]
        scratch += [pltpu.VMEM(sharded + s, LOW) for s in shapes]
        scratch += [pltpu.VMEM((depth, 160, BLOCK), LOW), pltpu.VMEM((depth - 1, 160, BLOCK), LOW)]
        for lead in ((depth, 2, 2), (3, depth), (depth - 1,)):
            scratch += [pltpu.VMEM(lead + s, LOW) for s in shapes]
        scratch += [pltpu.SemaphoreType.DMA((depth,))] * 2
        slots = 2 * (depth + 3)
        scratch += [pltpu.SemaphoreType.DMA((4, slots)), pltpu.SemaphoreType.DMA((4, slots))]
    else:
        outs += [shape_of((BLOCK // 16, EARLY, BLOCK), LOW), shape_of((BLOCK, 128), WIDE)]
    return pl.pallas_call(
        partial(last_kernel, depth, reduces),
        name="last_part",
        out_shape=outs,
        in_specs=[SMEM] + [VMEM] * 5 + [ANY] * 9 + [VMEM] * 2 + [ANY] * 2 + [VMEM] * len(parts),
        out_specs=[VMEM] * len(outs),
        scratch_shapes=scratch,
        compiler_params=pltpu.CompilerParams(
            collective_id=2, has_side_effects=True, vmem_limit_bytes=LIMIT
        ),
    )(pair, seg, pad, dkv, enc, dq_own, dq_other, *held, small_rows, small_cols, ga, gs, *parts)


def finish_kernel(count, *refs):
    ins, small, loss = refs[:count], refs[count], refs[count + 1]
    refs = refs[count + 2 :]
    outs, (gain, bias, table, delete, loss_out) = refs[:count], refs[count : count + 5]
    held, sems = refs[count + 5 : 2 * count + 5], refs[2 * count + 5]
    first = [pltpu.make_async_copy(ins[k], held[k], sems.at[0, k]) for k in range(count)]
    copies = [pltpu.make_async_copy(held[k], outs[k], sems.at[1, k]) for k in range(count)]
    for copy in first:
        copy.start()
    values = small[...]
    shape = (values.shape[0], values.shape[0])
    turned = jnp.concatenate([values, jnp.zeros((128 - values.shape[0], 128), WIDE)], axis=0).T
    gain[...] = turned[0:4, 0 : shape[0]]
    bias[...] = turned[4:8, 0 : shape[0]]
    table[...] = turned[8:16, 0 : shape[0]]
    delete[...] = values[:, 16:18]
    loss_out[...] = loss[...]
    for before, copy in zip(first, copies):
        before.wait()
        copy.start()
    for copy in copies:
        copy.wait()


def finish(results, small, loss):
    count = len(results)
    rows = small.shape[0]
    outs = [shape_of(a.shape, a.dtype) for a in results]
    outs += [shape_of(s, WIDE) for s in ((4, rows), (4, rows), (PAIRS, rows), (rows, 2), (1, 1))]
    res = pl.pallas_call(
        partial(finish_kernel, count),
        name="finish",
        out_shape=outs,
        in_specs=[ANY] * count + [VMEM] * 2,
        out_specs=[ANY] * count + [VMEM] * 5,
        scratch_shapes=[pltpu.VMEM(a.shape, a.dtype) for a in results] + [pltpu.SemaphoreType.DMA((2, count))],
        compiler_params=pltpu.CompilerParams(vmem_limit_bytes=LIMIT),
    )(*results, small, loss)
    block_out, grad_input, grad_enc, qkv, so, cq, kv, co, fi, fo, insert, vocab, tokens = res[:count]
    gain, bias, table, delete, loss = res[count:]
    return (
        block_out, grad_input, grad_enc, gain, bias, table, qkv, so, cq, kv, co, fi, fo, delete, insert, vocab,
        loss[0, 0], tokens,
    )


def late_blocks(cross_out, ffn_in, ffn_out, insert):
    groups = cross_out.shape[0] // 16
    return jnp.concatenate(
        [
            cross_out.reshape(groups, 16, BLOCK),
            ffn_in.reshape(groups, 16, 4, BLOCK).swapaxes(1, 2).reshape(groups, 64, BLOCK),
            ffn_out.reshape(groups, 64, BLOCK),
            insert.reshape(groups, 2, 16, BLOCK // 2).swapaxes(1, 2).reshape(groups, 16, BLOCK),
        ],
        axis=1,
    )


def gather_by_ops(qkv, self_out, cross_q, cross_kv, small):
    wide = jnp.concatenate([qkv, self_out, cross_q, cross_kv], axis=1)
    ga = lax.all_gather(wide, BOTH, axis=0, tiled=True).reshape(-1, 16, 7, BLOCK).swapaxes(1, 2)
    gs = lax.all_gather(small, BOTH, axis=0, tiled=True)
    return ga.reshape(-1, EARLY, BLOCK), gs.reshape(-1, 16, 128)


def across(depth, arrays):
    res = []
    for array, (dx, dy) in zip(arrays, ((1, 0), (0, 1), (1, 1))):
        pairs = []
        for z in range(depth):
            for x in range(2):
                for c in range(2):
                    for y in range(2):
                        here = ((z * 2 + x) * 2 + c) * 2 + y
                        there = ((z * 2 + (x ^ dx)) * 2 + c) * 2 + (y ^ dy)
                        pairs.append((here, there))
        res.append(lax.ppermute(array, BOTH, pairs))
    return res


def reduce_by_ops(early, small, late, scale):
    groups = late.shape[0]
    gw_f = late[:, 80:144].reshape(groups * 64, BLOCK)
    gw_i = late[:, 144:160].reshape(groups, 16, 2, BLOCK // 2).swapaxes(1, 2).reshape(groups * 32, BLOCK // 2)
    late = late[:, 0:80].reshape(groups, 5, 16, BLOCK).swapaxes(0, 1).reshape(5, BLOCK, BLOCK)
    early = early.reshape(groups, 7, 16, BLOCK).swapaxes(0, 1).reshape(7, BLOCK, BLOCK)
    wide = jnp.concatenate([early, late]).swapaxes(0, 1).reshape(BLOCK, 12 * BLOCK)

    def sums(a):
        return lax.psum_scatter(a.astype(WIDE), BOTH, scatter_dimension=0, tiled=True) * scale

    own = sums(wide)
    edges = (0, 3, 4, 5, 7, 8, 12)
    pieces = [own[:, lo * BLOCK : hi * BLOCK] for lo, hi in zip(edges[:-1], edges[1:])]
    return pieces + [sums(gw_f), sums(gw_i), sums(small)]


def body(
    dec_input, enc_output, segment_ids, padding, pair_ids, src_lengths, delete_labels, insert_counts,
    masked_positions, masked_targets, norm_gain, norm_bias, pair_table, self_qkv, self_out, cross_q, cross_kv,
    cross_out, ffn_in, ffn_out, w_delete, w_insert, w_vocab,
):
    everyone = lax.axis_size(BOTH)
    depth = everyone // 8
    tok_count = dec_input.shape[0]
    aligned = self_qkv.shape[0] == 16
    late = (cross_out, ffn_in, ffn_out, w_insert)
    tiny = (norm_gain, norm_bias, pair_table, w_delete.T)
    raw = (self_qkv, self_out, cross_q, cross_kv)
    whole = None
    if not aligned:
        gathered = late_blocks(*[lax.all_gather(a, BOTH, axis=0, tiled=True) for a in late])
        small = jnp.concatenate([norm_gain, norm_bias, pair_table, w_delete.T], axis=0).T
        small = jnp.pad(small, ((0, 0), (0, 128 - small.shape[1])))
        whole = gather_by_ops(*raw, small)
    whole, line, firsts = first_part(
        depth, aligned, segment_ids, padding, pair_ids, dec_input, enc_output, tiny, raw, late, whole
    )
    start, one, qkv, low, lse, after, two, query, other_query, kv, other_seg = firsts
    parts = (line, *across(depth, (line,) * 3)) if aligned else (gathered,)
    attended = cross_forward(src_lengths, segment_ids, other_seg, query, other_query, kv)
    mids = middle_part(
        depth, aligned, segment_ids, padding, delete_labels, insert_counts, masked_positions, masked_targets,
        w_vocab, after, attended, whole[1], parts,
    )
    parts, mids = mids[: len(parts)], mids[len(parts) :]
    block_out, gstate, g_own, g_other, st_own, st_other, small_rows, small_cols, grad_vocab, tokens, loss = mids
    sums = (parts[0], *across(depth, parts[1:])) if aligned else ()
    dq_own, dq_other, dkv = cross_backward(
        src_lengths, segment_ids, other_seg, query, other_query, g_own, g_other, st_own, st_other, kv
    )
    res = last_part(
        depth, aligned, pair_ids, segment_ids, padding, dq_own, dq_other, dkv, enc_output,
        (start, one, qkv, low, lse, after, two), gstate, (sums, small_rows, small_cols), whole,
    )
    if aligned:
        sums = res[2:]
    else:
        scale = (tok_count * everyone) ** (-0.5)
        sums = reduce_by_ops(res[2], res[3], parts[0], scale)
    return finish((block_out, res[0], res[1], *sums[:8], grad_vocab, tokens), sums[8], loss)


def solution(mesh):
    shared = P(BOTH, None)
    across = P(None, BOTH)
    return jax.shard_map(
        body,
        mesh=mesh,
        in_specs=(shared,) * 5 + (P("batch", None),) + (shared,) * 4 + (across,) * 3 + (shared,) * 10,
        out_specs=(shared,) * 3 + (across,) * 3 + (shared,) * 10 + (P(), shared),
        check_vma=False,
    )
```

time: 348 us -> 285 us (0.82)
  Pallas kernels: 307 us -> 269 us
  local copies, waits for them, and re-layouts: 25.9 us -> 3.78 us
  starting transfers between devices: 0 us -> 7.11 us
  blocking collectives: 5.45 us -> 0 us
    pallas_call x1, Pallas kernels: 92.5 us -> 61.9 us  [last_part(): pl.pallas_call(partial(last_kernel, depth, reduces), name='last_part', ou...]
    pallas_call x1, Pallas kernels: 84.1 us -> 60 us  [first_part(): pl.pallas_call(partial(first_kernel, depth, gathers), name='first_part',...]
    unnamed x44 -> x13, local copies, waits for them, and re-layouts: 16 us -> 3.78 us
    ppermute x0 -> x6, starting transfers between devices: none -> 7.11 us  [across(): res.append(lax.ppermute(array, BOTH, pairs))]
    pallas_call x1 -> x2, Pallas kernels: 78.1 us -> 84.2 us  [the longest x1 77.2 us: middle_part(): pl.pallas_call(partial(middle_kernel, depth, split), name='middle_part',...]
    pallas_call x1, Pallas kernels: 28.8 us -> 34.7 us  [cross_backward(): pl.pallas_call(cross_backward_kernel, name='cross_backward', out_shape=[s...]
    all_gather x1 -> x0, blocking collectives: 5.45 us -> none  [body(): partners = lax.all_gather(segment_ids[0], 'src')]
    pallas_call x1, Pallas kernels: 23.9 us -> 28.5 us  [cross_forward(): pl.pallas_call(cross_forward_kernel, name='cross_forward', out_shape=[out...]
  transfers between devices with their start and end apart: 0 -> 6, of which waited for: 0 -> 0; matrix products, arithmetic and copies ran while one was open for 0% -> 0% of each run, Pallas kernels for 0% -> 22%
where the time goes in v3:
time: 285 us; the launch traced here: 281 us
  Pallas kernels  269 us (94%)
  starting transfers between devices  7.11 us (2%)
  local copies, waits for them, and re-layouts  3.78 us (1%)
    pallas_call x1, Pallas kernels, middle_part(): pl.pallas_call(partial(middle_kernel, depth, split), name='middle_part',...  77.2 us
    pallas_call x1, Pallas kernels, last_part(): pl.pallas_call(partial(last_kernel, depth, reduces), name='last_part', ou...  61.9 us
    pallas_call x1, Pallas kernels, first_part(): pl.pallas_call(partial(first_kernel, depth, gathers), name='first_part',...  60 us
    pallas_call x1, Pallas kernels, cross_backward(): pl.pallas_call(cross_backward_kernel, name='cross_backward', out_shape=[s...  34.7 us
    pallas_call x1, Pallas kernels, cross_forward(): pl.pallas_call(cross_forward_kernel, name='cross_forward', out_shape=[out...  28.5 us
    ppermute x6, starting transfers between devices, across(): res.append(lax.ppermute(array, BOTH, pairs))  7.11 us
    pallas_call x1, Pallas kernels, finish(): pl.pallas_call(partial(finish_kernel, count), name='finish', out_shape=ou...  7 us
  transfers between devices with their start and end apart: 6, of which 0 were waited for; matrix products, arithmetic and copies ran while one was open for 0% of the time, Pallas kernels for 22%

profile of v3, /device:TPU:0, one launch (start us, length us, event | category | flops | bytes accessed | tf_op | source)
XLA Modules:
  0.0 281.5 jit_solution(10440284771137190287)
XLA Ops:
  0.7 60.0 %first_part.1 = (bf16[4,2,2,2,112,512]{5,4,3,2,1,0:T(8,128)(2,1)}, bf16[4,2,2,2,16,128]{5,4,3,2,1,0:T(8,128)(2,1)}, bf16[4,160,512]{2,1,0:T(8,128)(2,1)}, f32[51...) custom-call(s32[1,512]{1,0:T(1,128)} %refs_1_.5, ...), custom_call_target="tpu_custom_call" | custom-call | tf_op jit(solution)/shard_map/first_part/pallas_call | solution.py:412
  60.7 0.7 collective-permute-start.2
  61.4 2.3 collective-permute-start.1
  63.7 0.5 collective-permute-start
  64.2 28.5 %cross_forward.1 = (bf16[512,512]{1,0:T(8,128)(2,1)}, bf16[512,512]{1,0:T(8,128)(2,1)}, f32[8,512]{1,0:T(8,128)}, f32[8,512]{1,0:T(8,128)}) custom-call(s32[1,16]{1,0:T(1,128)} %lengths.3, s32[1,512]{1,0:T(1,128)} %refs_1_.5, s32[1,512]{1,0:T(1,128)} %get-tuple-element.84.seg_sp.seg_vp, s32[1,512]{1,0:T(1,128)} %refs_1_.5, ...), custom_call_target="tpu_custom_call" | custom-call | tf_op jit(solution)/shard_map/cross_forward/pallas_call | solution.py:532
  92.7 0.0 collective-permute-done.2.refs_16_
  92.7 0.0 copy-start.3
  92.7 0.0 collective-permute-done.1.refs_15_
  92.8 0.0 copy-start.4
  92.8 0.0 collective-permute-done.refs_14_
  92.8 0.0 copy-start.5
  92.8 0.8 copy-done.3
  93.6 0.2 copy-done.4
  93.8 0.2 copy-done.5
  94.0 77.2 %middle_part.1 = (bf16[4,160,512]{2,1,0:T(8,128)(2,1)}, bf16[4,160,512]{2,1,0:T(8,128)(2,1)}, bf16[4,160,512]{2,1,0:T(8,128)(2,1)}, bf16[4,160,512]{2,1,0:T(8,12...) custom-call(s32[1,512]{1,0:T(1,128)} %refs_1_.5, ...), custom_call_target="tpu_custom_call" | custom-call | tf_op jit(solution)/shard_map/middle_part/pallas_call | solution.py:959
  171.3 1.5 collective-permute-start.3
  172.8 0.7 collective-permute-start.4
  173.5 1.4 collective-permute-start.5
  174.8 34.7 %cross_backward.1 = (f32[512,512]{1,0:T(8,128)}, bf16[512,512]{1,0:T(8,128)(2,1)}, bf16[2048,1024]{1,0:T(8,128)(2,1)}) custom-call(s32[1,16]{1,0:T(1,128)} %lengths.3, s32[1,512]{1,0:T(1,128)} %refs_1_.5, s32[1,512]{1,0:T(1,128)} %get-tuple-element.84.seg_sp.seg_vp, s32[1,512]{1,0:T(1,128)} %refs_1_.5, s32[1,512]{1,0:T(1,128)} %get-tuple-element.84.seg_sp.seg_vp, ...), custom_call_target="tpu_custom_call" | custom-call | tf_op jit(solution)/shard_map/cross_backward/pallas_call | solution.py:605
  209.5 0.0 collective-permute-done.3.refs_20_
  209.5 0.0 copy-start
  209.5 0.0 collective-permute-done.4.refs_21_
  209.5 0.0 copy-start.1
  209.5 0.0 collective-permute-done.5.refs_22_
  209.6 0.0 copy-start.2
  209.6 0.8 copy-done
  210.4 0.2 copy-done.1
  210.6 0.2 copy-done.2
  210.8 61.9 %last_part.1 = (bf16[512,512]{1,0:T(8,128)(2,1)}, bf16[2048,512]{1,0:T(8,128)(2,1)}, f32[16,1536]{1,0:T(8,128)}, f32[16,512]{1,0:T(8,128)}, f32[16,512]{1,0:T(8,...) custom-call(s32[1,8]{1,0:T(1,128)} %refs_0_.5, ...), custom_call_target="tpu_custom_call" | custom-call | tf_op jit(solution)/shard_map/last_part/pallas_call | solution.py:1339
  272.7 7.0 %finish.1 = (bf16[512,512]{1,0:T(8,128)(2,1)}, bf16[512,512]{1,0:T(8,128)(2,1)}, bf16[2048,512]{1,0:T(8,128)(2,1)}, f32[16,1536]{1,0:T(8,128)}, f32[16,512]{1,0:...) custom-call(bf16[512,512]{1,0:T(8,128)(2,1)} %get-tuple-element.94.r, ...), custom_call_target="tpu_custom_call" | custom-call | tf_op jit(solution)/shard_map/finish/pallas_call | solution.py:1381
  279.7 1.3 copy.41
Async XLA Ops:
  60.7 32.1 %collective-permute-start.2 = (bf16[4,160,512]{2,1,0:T(8,128)(2,1)}, bf16[4,160,512]{2,1,0:T(8,128)(2,1)S(1)}, u32[]{:S(2)}, u32[]{:S(2)}) collective-permute-start(bf16[4,160,512]{2,1,0:T(8,128)(2,1)} %get-tuple-element.93.refs_13_), channel_id=1, source_target_pairs={{0,5},{1,4},{2,7},{3,6},{4,1},{5,0},{6,3},{7,2},{8,13},{9,12},{10,... | collective-permute-start | bytes 1966088 | tf_op jit(solution)/shard_map/ppermute | solution.py:1429
  61.4 31.4 %collective-permute-start.1 = (bf16[4,160,512]{2,1,0:T(8,128)(2,1)}, bf16[4,160,512]{2,1,0:T(8,128)(2,1)S(1)}, u32[]{:S(2)}, u32[]{:S(2)}) collective-permute-start(bf16[4,160,512]{2,1,0:T(8,128)(2,1)} %get-tuple-element.93.refs_13_), channel_id=1, source_target_pairs={{0,1},{1,0},{2,3},{3,2},{4,5},{5,4},{6,7},{7,6},{8,9},{9,8},{10,11... | collective-permute-start | bytes 1966088 | tf_op jit(solution)/shard_map/ppermute | solution.py:1429
  63.7 29.1 %collective-permute-start = (bf16[4,160,512]{2,1,0:T(8,128)(2,1)}, bf16[4,160,512]{2,1,0:T(8,128)(2,1)S(1)}, u32[]{:S(2)}, u32[]{:S(2)}) collective-permute-start(bf16[4,160,512]{2,1,0:T(8,128)(2,1)} %get-tuple-element.93.refs_13_), channel_id=1, source_target_pairs={{0,4},{1,5},{2,6},{3,7},{4,0},{5,1},{6,2},{7,3},{8,12},{9,13},{10,... | collective-permute-start | bytes 1966088 | tf_op jit(solution)/shard_map/ppermute | solution.py:1429
  92.7 0.9 copy-start.3
  92.8 1.0 copy-start.4
  92.8 1.2 copy-start.5
  171.3 38.2 %collective-permute-start.3 = (bf16[4,160,512]{2,1,0:T(8,128)(2,1)}, bf16[4,160,512]{2,1,0:T(8,128)(2,1)S(1)}, u32[]{:S(2)}, u32[]{:S(2)}) collective-permute-start(bf16[4,160,512]{2,1,0:T(8,128)(2,1)} %get-tuple-element.113), channel_id=1, source_target_pairs={{0,4},{1,5},{2,6},{3,7},{4,0},{5,1},{6,2},{7,3},{8,12},{9,13},{10,... | collective-permute-start | bytes 1966088 | tf_op jit(solution)/shard_map/ppermute | solution.py:1429
  172.8 36.7 %collective-permute-start.4 = (bf16[4,160,512]{2,1,0:T(8,128)(2,1)}, bf16[4,160,512]{2,1,0:T(8,128)(2,1)S(1)}, u32[]{:S(2)}, u32[]{:S(2)}) collective-permute-start(bf16[4,160,512]{2,1,0:T(8,128)(2,1)} %get-tuple-element.114), channel_id=1, source_target_pairs={{0,1},{1,0},{2,3},{3,2},{4,5},{5,4},{6,7},{7,6},{8,9},{9,8},{10,11... | collective-permute-start | bytes 1966088 | tf_op jit(solution)/shard_map/ppermute | solution.py:1429
  173.5 36.1 %collective-permute-start.5 = (bf16[4,160,512]{2,1,0:T(8,128)(2,1)}, bf16[4,160,512]{2,1,0:T(8,128)(2,1)S(1)}, u32[]{:S(2)}, u32[]{:S(2)}) collective-permute-start(bf16[4,160,512]{2,1,0:T(8,128)(2,1)} %get-tuple-element.115), channel_id=1, source_target_pairs={{0,5},{1,4},{2,7},{3,6},{4,1},{5,0},{6,3},{7,2},{8,13},{9,12},{10,... | collective-permute-start | bytes 1966088 | tf_op jit(solution)/shard_map/ppermute | solution.py:1429
  209.5 0.8 copy-start
  209.5 1.0 copy-start.1
  209.6 1.2 copy-start.2
